TPU v7x, 256 devices: a whole 4x4x8 slice. The times are simulated.
256 devices in a mesh: spin: 2 (over x_lo), band: 128 (over y, x_hi, z, core).
Axes of the slice: x: 4 (x_hi: 2, x_lo: 2; x = x_hi * 2 + x_lo), y: 4, z: 8, core: 2. Of those that a mesh axis runs over, the one named last changes fastest.
Arguments:
- orbitals: bfloat16 [256, 262144], P(('spin', 'band')), parts along dimension 0, may hold values from -6 to 6
- trial: bfloat16 [256, 262144], P(('spin', 'band')), parts along dimension 0, may hold values from -6 to 6
- occupations: int32 [256], P(('spin', 'band')), parts along dimension 0, may hold values 0 or 1
Outputs:
- exchange: bfloat16 [256, 262144], P(('spin', 'band')), parts along dimension 0
- projected: bfloat16 [256, 262144], P('spin', 'band'), parts along dimension 0
There are 2 independent parts, one for each index of `spin`. A program takes and returns all parts, laid end to end along the dimension named above; each array names one. Nothing has to cross between parts.
All inputs are finite; a program needn't handle non-finite values. No bound on the sum of `occupations` on one device may be relied on, other than what follows from the above.
Results may differ from a plain program's by a relative error of at most 0.018.
Values may be sent and summed in bfloat16 or wider, within the bound.
No kernel may reach another device: no remote copies, remote signals or barrier semaphores. Data moves between devices by JAX's collectives and lax.ppermute only.
A program may use at most 64 MiB of HBM per device.

v0:
```python
import functools
import math

import jax
import jax.numpy as jnp
import ml_dtypes
import numpy as np
from jax import lax
from jax.experimental import pallas as pl
from jax.experimental.pallas import tpu as pltpu
from jax.sharding import Mesh
from jax.sharding import PartitionSpec as P

NG = 64
G = NG**3
ROWS = G // 128
FRACTION = 0.25
OMEGA = 1.0
BAND = ("y", "x", "z", "core")
SPIN_BAND = ("spin",) + BAND
ORDER = np.concatenate([np.arange(0, NG, 2), np.arange(1, NG, 2)])
STEP = 4


def cas_table():
    indices = np.arange(NG)
    phases = (indices[:, None] * indices[None, :] % NG) * (2.0 * math.pi / NG)
    return (np.cos(phases) + np.sin(phases)).astype(np.float32).astype(ml_dtypes.bfloat16)


def screened_kernel():
    modes = np.arange(NG)
    modes = np.where(2 * modes < NG, modes, modes - NG)
    squares = (modes * (2.0 * math.pi / NG)) ** 2
    norm_sq = squares[:, None, None] + squares[None, :, None] + squares[None, None, :]
    bounded = np.where(norm_sq > 0, norm_sq, 1.0)
    screened = np.where(
        norm_sq > 0,
        4.0 * math.pi / bounded * (1.0 - np.exp(-bounded / (4.0 * OMEGA * OMEGA))),
        math.pi / (OMEGA * OMEGA),
    )
    return (screened / NG**3).astype(np.float32)


def constants():
    table = cas_table()
    mixed = table[ORDER][:, ORDER]
    blocks = np.kron(np.eye(4, dtype=np.float32), table.astype(np.float32)).astype(table.dtype)
    kernel = screened_kernel().transpose(1, 0, 2)[ORDER]
    return table, mixed, blocks, np.concatenate([kernel, kernel], axis=2)


def dot(left, right):
    return lax.dot_general(
        left, right, (((1,), (0,)), ((), ())), preferred_element_type=jnp.float32
    )


def exchange_body(
    own_ref, prev_ref, next_ref, fill_ref, table_ref, mixed_ref, blocks_ref, kernel_ref,
    out_ref, sides, middle, visitors, owner,
):
    lane = lax.broadcasted_iota(jnp.int32, (NG // 2, 128), 1)
    low = lane < 64
    low_wide = lax.broadcasted_iota(jnp.int32, (NG, 128), 1) < 64
    f32, bf16 = jnp.float32, jnp.bfloat16

    def forward(step, carry):
        for part in range(STEP):
            plane = step * STEP + part
            rows = pl.ds(pl.multiple_of(plane * 32, 32), 32)
            own, before, after = (
                ref[rows, :].astype(f32) for ref in (own_ref, prev_ref, next_ref)
            )
            own_turned, before_turned, after_turned = (
                pltpu.roll(value, 64, 1) for value in (own, before, after)
            )
            pairs = jnp.concatenate(
                [jnp.where(low, before, after_turned), jnp.where(low, before_turned, after)], axis=0
            )
            mine = jnp.concatenate(
                [jnp.where(low, own, own_turned), jnp.where(low, own_turned, own)], axis=0
            )
            wide = pl.ds(pl.multiple_of(plane * 64, 64), 64)
            visitors[wide, :] = pairs.astype(bf16)
            owner[wide, :] = mine.astype(bf16)
            density = jnp.concatenate([mine * pairs, mine * mine], axis=1).astype(bf16)
            values = dot(density, blocks_ref[...]).astype(bf16)
            values = dot(mixed_ref[...], values)
            sides[wide, :] = values[:, :128]
            middle[wide, :] = values[:, 128:]
        return carry

    lax.fori_loop(0, NG // STEP, forward, 0)

    def across(step, carry):
        for part in range(STEP):
            line = step * STEP + part
            rows = pl.ds(line, NG, stride=NG)
            values = jnp.concatenate([sides[rows, :], middle[rows, :]], axis=1).astype(bf16)
            values = dot(table_ref[...], values)
            kernel = kernel_ref[line]
            values = (values * jnp.concatenate([kernel, kernel], axis=1)).astype(bf16)
            values = dot(table_ref[...], values)
            sides[rows, :] = values[:, :128]
            middle[rows, :] = values[:, 128:]
        return carry

    lax.fori_loop(0, NG // STEP, across, 0)

    side_fill = jnp.where(low_wide, fill_ref[0], fill_ref[2])
    own_fill = jnp.where(low_wide, fill_ref[1], 0.0)

    def backward(step, carry):
        for part in range(STEP):
            plane = step * STEP + part
            wide = pl.ds(pl.multiple_of(plane * 64, 64), 64)
            values = jnp.concatenate([sides[wide, :], middle[wide, :]], axis=1).astype(bf16)
            values = dot(mixed_ref[...], values).astype(bf16)
            values = dot(values, blocks_ref[...])
            total = values[:, :128] * (visitors[wide, :].astype(f32) * side_fill)
            total = total + values[:, 128:] * (owner[wide, :].astype(f32) * own_fill)
            total = total + pltpu.roll(total, 64, 1)
            rows = pl.ds(pl.multiple_of(plane * 32, 32), 32)
            out_ref[rows, :] = jnp.where(low, total[:32], total[32:]).astype(bf16)
        return carry

    lax.fori_loop(0, NG // STEP, backward, 0)


def exchange_of(own, before, after, fills):
    table, mixed, blocks, kernel = (jnp.asarray(value) for value in constants())
    vmem = pl.BlockSpec(memory_space=pltpu.VMEM)
    return pl.pallas_call(
        exchange_body,
        out_shape=jax.ShapeDtypeStruct((ROWS, 128), jnp.bfloat16),
        in_specs=[vmem] * 3 + [pl.BlockSpec(memory_space=pltpu.SMEM)] + [vmem] * 4,
        out_specs=vmem,
        scratch_shapes=[
            pltpu.VMEM((NG * NG, 128), jnp.float32),
            pltpu.VMEM((NG * NG, 128), jnp.float32),
            pltpu.VMEM((NG * NG, 128), jnp.bfloat16),
            pltpu.VMEM((NG * NG, 128), jnp.bfloat16),
        ],
        compiler_params=pltpu.CompilerParams(vmem_limit_bytes=32 * 1024 * 1024),
        cost_estimate=pl.CostEstimate(
            flops=4 * 6 * 2 * G * NG, bytes_accessed=4 * 1024 * 1024, transcendentals=0
        ),
        name="exchange",
    )(own, before, after, fills, table, mixed, blocks, kernel)


def by_line_body(count, tiles_ref, out_ref, wide):
    wide[...] = tiles_ref[...].astype(jnp.float32)
    for line in range(16):
        rows = wide[pl.ds(line, count, stride=16), :]
        out_ref[pl.ds(line * count, count), :] = rows.astype(jnp.bfloat16)


def by_line(tiles):
    count = tiles.shape[0]
    vmem = pl.BlockSpec(memory_space=pltpu.VMEM)
    return pl.pallas_call(
        functools.partial(by_line_body, count),
        out_shape=jax.ShapeDtypeStruct((16 * count, 128), jnp.bfloat16),
        in_specs=[vmem],
        out_specs=vmem,
        scratch_shapes=[pltpu.VMEM((16 * count, 128), jnp.float32)],
        compiler_params=pltpu.CompilerParams(vmem_limit_bytes=16 * 1024 * 1024),
        cost_estimate=pl.CostEstimate(flops=0, bytes_accessed=2 * 1024 * 1024, transcendentals=0),
        name="by_line",
    )(tiles.reshape(16 * count, 128))


def intersection_body(tiles_ref, trial_ref, core_ref, lines_ref, mine_ref, other_ref, wide):
    by_line_body(128, tiles_ref, lines_ref, wide)
    total = jnp.zeros((128, 128), jnp.float32)
    for line in range(16):
        rows = pl.ds(line * 128, 128)
        total = total + lax.dot_general(
            trial_ref[rows, :], lines_ref[rows, :], (((1,), (1,)), ((), ())),
            preferred_element_type=jnp.float32,
        )
    total = total * (1.0 / math.sqrt(G))
    first = core_ref[0] == 0
    mine_ref[...] = jnp.where(first, total[:64], total[64:])
    other_ref[...] = jnp.where(first, total[64:], total[:64])


def intersection_of(tiles, trial_lines, core):
    vmem = pl.BlockSpec(memory_space=pltpu.VMEM)
    half = jax.ShapeDtypeStruct((64, 128), jnp.float32)
    return pl.pallas_call(
        intersection_body,
        out_shape=(jax.ShapeDtypeStruct((ROWS, 128), jnp.bfloat16), half, half),
        in_specs=[vmem, vmem, pl.BlockSpec(memory_space=pltpu.SMEM)],
        out_specs=(vmem, vmem, vmem),
        scratch_shapes=[pltpu.VMEM((ROWS, 128), jnp.float32)],
        compiler_params=pltpu.CompilerParams(vmem_limit_bytes=16 * 1024 * 1024),
        name="intersection",
    )(tiles.reshape(ROWS, 128), trial_lines, core)


def projected_body(lines_ref, mine_ref, other_ref, core_ref, out_ref):
    first = core_ref[0] == 0
    mine, other = mine_ref[...].astype(jnp.float32), other_ref[...].astype(jnp.float32)
    table = jnp.concatenate(
        [jnp.where(first, mine, other), jnp.where(first, other, mine)], axis=0
    ).astype(jnp.bfloat16)
    for line in range(16):
        rows = pl.ds(line * 128, 128)
        value = dot(table, lines_ref[rows, :]) * (-1.0 / math.sqrt(128))
        out_ref[:, rows] = value.astype(jnp.bfloat16)


def projected_of(lines, mine, other, core):
    vmem = pl.BlockSpec(memory_space=pltpu.VMEM)
    return pl.pallas_call(
        projected_body,
        out_shape=jax.ShapeDtypeStruct((128, ROWS), jnp.bfloat16),
        in_specs=[vmem, vmem, vmem, pl.BlockSpec(memory_space=pltpu.SMEM)],
        out_specs=vmem,
        compiler_params=pltpu.CompilerParams(vmem_limit_bytes=16 * 1024 * 1024),
        name="projected",
    )(lines, mine, other, core)


def passed_along(value, steps):
    count = lax.axis_size(BAND)
    return lax.ppermute(value, BAND, [(i, (i + steps) % count) for i in range(count)])


def swapped(value):
    return lax.ppermute(value, "core", [(0, 1), (1, 0)])


def summed_over(value, axes):
    peers = lax.axis_size(axes)
    copies = jnp.broadcast_to(value[None], (peers,) + value.shape)
    tiles = lax.all_to_all(copies, axes, 0, 0, tiled=True)
    return jnp.sum(tiles.astype(jnp.float32), axis=0).astype(jnp.bfloat16)


def to_slabs(rows):
    return lax.all_to_all(rows.reshape(128, 16, 128), BAND, 0, 0, tiled=True)


def local(orbitals, trial, occupations):
    own = orbitals.reshape(ROWS, 128)
    before, after = passed_along(own, 1), passed_along(own, -1)
    filled = occupations.astype(jnp.float32)
    fills = jnp.concatenate([passed_along(filled, 1), filled, passed_along(filled, -1)])
    trial_lines = by_line(to_slabs(trial.reshape(ROWS, 128)))
    exchange = exchange_of(own, before, after, -FRACTION * fills)
    core = lax.axis_index("core").astype(jnp.int32).reshape(1)
    lines, mine, other = intersection_of(to_slabs(exchange), trial_lines, core)
    half = (mine + swapped(other)).astype(jnp.bfloat16)
    half = summed_over(half, ("y", "x"))
    half = summed_over(half, "z")
    projected = projected_of(lines, half, swapped(half), core)
    return exchange.reshape(1, G), projected


def solution(mesh):
    finer = Mesh(mesh.devices.reshape(mesh.shape["spin"], 4, 2, 8, 2), SPIN_BAND)
    return jax.shard_map(
        local,
        mesh=finer,
        in_specs=(P(SPIN_BAND, None), P(SPIN_BAND, None), P(SPIN_BAND)),
        out_specs=(P(SPIN_BAND, None), P("spin", BAND)),
        check_vma=False,
    )
```

profile of v0, /device:TPU:1, one launch (start us, length us, event | category | flops | bytes accessed | tf_op | source)
XLA Modules:
  0.0 153.0 jit_solution(11553528856434671413)
XLA Ops:
  0.6 0.0 copy-start
  0.6 0.0 copy-start.1
  0.7 0.0 copy-start.2
  0.7 0.0 copy-start.3
  0.7 12.8 %reduce.3 = bf16[262144]{0:T(1024)(128)(2,1)} reduce(bf16[1,262144]{1,0:T(2,128)(2,1)} %param.8, bf16[]{:T(256)} %constant.25), dimensions={0}, to_apply=%param.8.reduce_sub_computation | reduce | bytes 1048578 | tf_op args[1]
  13.5 16.4 %all-to-all-start.1 = ((bf16[128,16,128]{2,1,0:T(8,128)(2,1)}), bf16[128,16,128]{2,1,0:T(8,128)(2,1)S(1)}, u32[]{:S(2)}, u32[]{:S(2)}) async-start(bf16[128,16,128]{2,1,0:T(8,128)(2,1)} %bitcast.5), calls=%async_computation.1 | async-start | bytes 1048576 | tf_op jit(solution)/shard_map/all_to_all | solution.py:245
  29.9 11.9 %reduce.2 = bf16[262144]{0:T(1024)(128)(2,1)S(1)} reduce(bf16[1,262144]{1,0:T(2,128)(2,1)} %param.7, bf16[]{:T(256)} %constant.25), dimensions={0}, to_apply=%param.7.reduce_sub_computation | reduce | bytes 1048578 | tf_op args[0]
  41.8 1.9 %collective-permute-start = (bf16[2048,128]{1,0:T(8,128)(2,1)S(1)}, bf16[2048,128]{1,0:T(8,128)(2,1)S(1)}, u32[]{:S(2)}, u32[]{:S(2)}) collective-permute-start(bf16[2048,128]{1,0:T(8,128)(2,1)S(1)} %bitcast.11), channel_id=1, source_target_pairs={{0,1},{1,2},{2,3},{3,4},{4,5},{5,6},{6,7},{7,8},{8,9},{9,10},{10,1... | collective-permute-start | bytes 1572872 | tf_op jit(solution)/shard_map/ppermute | solution.py:230
  43.7 0.0 collective-permute-start.1
  44.4 5.5 %collective-permute-start.2 = (f32[1]{0:T(128)}, f32[1]{0:T(128)}, u32[]{:S(2)}, u32[]{:S(2)}) collective-permute-start(f32[1]{0:T(128)} %convert_element_type.4), channel_id=1, source_target_pairs={{0,1},{1,2},{2,3},{3,4},{4,5},{5,6},{6,7},{7,8},{8,9},{9,10},{10,1... | collective-permute-start | bytes 20 | tf_op jit(solution)/shard_map/ppermute | solution.py:230
  49.9 3.1 %collective-permute-start.3 = (f32[1]{0:T(128)}, f32[1]{0:T(128)}, u32[]{:S(2)}, u32[]{:S(2)}) collective-permute-start(f32[1]{0:T(128)} %convert_element_type.4), channel_id=1, source_target_pairs={{0,127},{1,0},{2,1},{3,2},{4,3},{5,4},{6,5},{7,6},{8,7},{9,8},{10,... | collective-permute-start | bytes 20 | tf_op jit(solution)/shard_map/ppermute | solution.py:230
  53.0 0.0 collective-permute-done.2
  53.0 0.2 collective-permute-done.3
  53.2 1.3 maximum_multiply_fusion.fill_ref
  54.5 0.0 collective-permute-done.prev_ref
  54.5 0.0 collective-permute-done.1.next_ref
  54.5 0.0 copy-done
  54.5 0.0 copy-done.1
  54.5 0.0 copy-done.2
  54.5 0.0 copy-done.3
  54.5 30.9 %exchange.1 = bf16[2048,128]{1,0:T(8,128)(2,1)} custom-call(bf16[2048,128]{1,0:T(8,128)(2,1)S(1)} %bitcast.13, bf16[2048,128]{1,0:T(8,128)(2,1)S(1)} %collective-permute-done.prev_ref, bf16[2048,128]{1,0:T(8,128)(2,1)S(1)} %collective-permute-done.1.next_ref, f32[3]{0:T(128)S(1)} %maximum_multiply_fusion.fill_ref, bf16[64,64]{1,0:T(8,128)(2,1)S(1)} %copy-done.2, ...), custom_call_target="tpu_custom_call" | custom-call | flops 805306368 | bytes 4194304 | tf_op jit(solution)/shard_map/exchange/pallas_call | solution.py:134
  85.4 0.0 all-to-all-done.1
  85.4 17.6 %all-to-all-start = ((bf16[128,16,128]{2,1,0:T(8,128)(2,1)}), bf16[128,16,128]{2,1,0:T(8,128)(2,1)S(1)}, u32[]{:S(2)}, u32[]{:S(2)}) async-start(bf16[128,16,128]{2,1,0:T(8,128)(2,1)} %bitcast), calls=%async_computation | async-start | bytes 1048576 | tf_op jit(solution)/shard_map/all_to_all | solution.py:245
  103.1 0.4 by_line.1.trial_ref
  103.5 21.1 %all-to-all-done = bf16[128,16,128]{2,1,0:T(8,128)(2,1)S(1)} async-done(((bf16[128,16,128]{2,1,0:T(8,128)(2,1)}), bf16[128,16,128]{2,1,0:T(8,128)(2,1)S(1)}, u32[]{:S(2)}, u32[]{:S(2)}) %all-to-all-start) | async-done | bytes 524320 | tf_op jit(solution)/shard_map/all_to_all | solution.py:245
  124.5 0.6 intersection.1
  125.2 0.1 collective-permute-start.4
  125.3 1.2 collective-permute-done.4
  126.5 9.4 %all_to_all.20 = bf16[8,64,128]{2,1,0:T(8,128)(2,1)S(1)} all-to-all(bf16[8,64,128]{2,1,0:T(8,128)(2,1)S(1)} %broadcast_in_dim.4), channel_id=1, replica_groups=mesh['spin'=2,'y'=4,'x'=2,'z'=8,'core'=2] {'y','x'}, dimensions={0} | all-to-all | bytes 262144 | tf_op jit(solution)/shard_map/all_to_all | solution.py:240
  136.0 10.3 %all_to_all.21 = bf16[8,64,128]{2,1,0:T(8,128)(2,1)S(1)} all-to-all(bf16[8,64,128]{2,1,0:T(8,128)(2,1)S(1)} %broadcast_in_dim.5), channel_id=1, replica_groups=mesh['spin'=2,'y'=4,'x'=2,'z'=8,'core'=2] {'z'}, dimensions={0} | all-to-all | bytes 262144 | tf_op jit(solution)/shard_map/all_to_all | solution.py:240
  146.4 3.0 %collective-permute-start.5 = (bf16[64,128]{1,0:T(8,128)(2,1)S(1)}, bf16[64,128]{1,0:T(8,128)(2,1)S(1)}, u32[]{:S(2)}, u32[]{:S(2)}) collective-permute-start(bf16[64,128]{1,0:T(8,128)(2,1)S(1)} %reduce_sum.25.mine_ref), channel_id=1, source_target_pairs={{0,1},{1,0},{2,3},{3,2},{4,5},{5,4},{6,7},{7,6},{8,9},{9,8},{10,11... | collective-permute-start | bytes 49160 | tf_op jit(solution)/shard_map/ppermute | solution.py:234
  149.3 2.6 %copy.11 = bf16[1,1,2048,128]{3,1,2,0:T(2,128)(2,1)} copy(bf16[1,1,2048,128]{3,2,1,0:T(8,128)(2,1)} %bitcast.7) | data formatting | bytes 1048576
  151.9 0.0 collective-permute-done.5.other_ref
  151.9 1.1 projected.1
  (5 shorter events, 0.1 us)
Async XLA Ops:
  0.6 53.8 %copy-start = (f32[64,64,128]{2,1,0:T(8,128)S(1)}, f32[64,64,128]{2,1,0:T(8,128)}, u32[]{:S(2)}) copy-start(f32[64,64,128]{2,1,0:T(8,128)} %constant.21.clone.kernel_ref) | copy-start | bytes 6291460
  0.6 53.8 %copy-start.1 = (bf16[256,256]{1,0:T(8,128)(2,1)S(1)}, bf16[256,256]{1,0:T(8,128)(2,1)}, u32[]{:S(2)}) copy-start(bf16[256,256]{1,0:T(8,128)(2,1)} %constant.20.clone.blocks_ref) | copy-start | bytes 393220
  0.7 53.8 %copy-start.2 = (bf16[64,64]{1,0:T(8,128)(2,1)S(1)}, bf16[64,64]{1,0:T(8,128)(2,1)}, u32[]{:S(2)}) copy-start(bf16[64,64]{1,0:T(8,128)(2,1)} %constant.18.clone.table_ref) | copy-start | bytes 24580
  0.7 53.8 %copy-start.3 = (bf16[64,64]{1,0:T(8,128)(2,1)S(1)}, bf16[64,64]{1,0:T(8,128)(2,1)}, u32[]{:S(2)}) copy-start(bf16[64,64]{1,0:T(8,128)(2,1)} %constant.19.clone.mixed_ref) | copy-start | bytes 24580
  13.5 71.9 %all-to-all-start.1 = ((bf16[128,16,128]{2,1,0:T(8,128)(2,1)}), bf16[128,16,128]{2,1,0:T(8,128)(2,1)S(1)}, u32[]{:S(2)}, u32[]{:S(2)}) async-start(bf16[128,16,128]{2,1,0:T(8,128)(2,1)} %bitcast.5), calls=%async_computation.1 | async-start | bytes 1048576 | tf_op jit(solution)/shard_map/all_to_all | solution.py:245
  41.8 12.6 %collective-permute-start = (bf16[2048,128]{1,0:T(8,128)(2,1)S(1)}, bf16[2048,128]{1,0:T(8,128)(2,1)S(1)}, u32[]{:S(2)}, u32[]{:S(2)}) collective-permute-start(bf16[2048,128]{1,0:T(8,128)(2,1)S(1)} %bitcast.11), channel_id=1, source_target_pairs={{0,1},{1,2},{2,3},{3,4},{4,5},{5,6},{6,7},{7,8},{8,9},{9,10},{10,1... | collective-permute-start | bytes 1572872 | tf_op jit(solution)/shard_map/ppermute | solution.py:230
  43.7 10.7 %collective-permute-start.1 = (bf16[2048,128]{1,0:T(8,128)(2,1)S(1)}, bf16[2048,128]{1,0:T(8,128)(2,1)S(1)}, u32[]{:S(2)}, u32[]{:S(2)}) collective-permute-start(bf16[2048,128]{1,0:T(8,128)(2,1)S(1)} %bitcast.12), channel_id=1, source_target_pairs={{0,127},{1,0},{2,1},{3,2},{4,3},{5,4},{6,5},{7,6},{8,7},{9,8},{10,... | collective-permute-start | bytes 1572872 | tf_op jit(solution)/shard_map/ppermute | solution.py:230
  44.4 8.6 %collective-permute-start.2 = (f32[1]{0:T(128)}, f32[1]{0:T(128)}, u32[]{:S(2)}, u32[]{:S(2)}) collective-permute-start(f32[1]{0:T(128)} %convert_element_type.4), channel_id=1, source_target_pairs={{0,1},{1,2},{2,3},{3,4},{4,5},{5,6},{6,7},{7,8},{8,9},{9,10},{10,1... | collective-permute-start | bytes 20 | tf_op jit(solution)/shard_map/ppermute | solution.py:230
  49.9 3.3 %collective-permute-start.3 = (f32[1]{0:T(128)}, f32[1]{0:T(128)}, u32[]{:S(2)}, u32[]{:S(2)}) collective-permute-start(f32[1]{0:T(128)} %convert_element_type.4), channel_id=1, source_target_pairs={{0,127},{1,0},{2,1},{3,2},{4,3},{5,4},{6,5},{7,6},{8,7},{9,8},{10,... | collective-permute-start | bytes 20 | tf_op jit(solution)/shard_map/ppermute | solution.py:230
  85.4 39.1 %all-to-all-start = ((bf16[128,16,128]{2,1,0:T(8,128)(2,1)}), bf16[128,16,128]{2,1,0:T(8,128)(2,1)S(1)}, u32[]{:S(2)}, u32[]{:S(2)}) async-start(bf16[128,16,128]{2,1,0:T(8,128)(2,1)} %bitcast), calls=%async_computation | async-start | bytes 1048576 | tf_op jit(solution)/shard_map/all_to_all | solution.py:245
  125.2 1.3 collective-permute-start.4
  146.4 5.5 %collective-permute-start.5 = (bf16[64,128]{1,0:T(8,128)(2,1)S(1)}, bf16[64,128]{1,0:T(8,128)(2,1)S(1)}, u32[]{:S(2)}, u32[]{:S(2)}) collective-permute-start(bf16[64,128]{1,0:T(8,128)(2,1)S(1)} %reduce_sum.25.mine_ref), channel_id=1, source_target_pairs={{0,1},{1,0},{2,3},{3,2},{4,5},{5,4},{6,7},{7,6},{8,9},{9,8},{10,11... | collective-permute-start | bytes 49160 | tf_op jit(solution)/shard_map/ppermute | solution.py:234
where the time goes:
time: 153 us
  starting transfers between devices  47.6 us (31%)
  Pallas kernels  33 us (22%)
  other arithmetic  26.1 us (17%)
  waiting for transfers between devices  22.5 us (15%)
  blocking collectives  19.8 us (13%)
  local copies, waits for them, and re-layouts  2.63 us (2%)
    all_to_all x2, starting transfers between devices, to_slabs(): return lax.all_to_all(rows.reshape(128, 16, 128), BAND, 0, 0, tiled=True)  34 us
    pallas_call x1, Pallas kernels, exchange_of(): pl.pallas_call(exchange_body, out_shape=jax.ShapeDtypeStruct((ROWS, 128),...  30.9 us
    unnamed x2, other arithmetic  24.8 us
    all_to_all x2, waiting for transfers between devices, to_slabs(): return lax.all_to_all(rows.reshape(128, 16, 128), BAND, 0, 0, tiled=True)  21.1 us
    all_to_all x2, blocking collectives, summed_over(): tiles = lax.all_to_all(copies, axes, 0, 0, tiled=True)  19.8 us
    ppermute x4, starting transfers between devices, passed_along(): lax.ppermute(value, BAND, [(i, (i + steps) % count) for i in range(count)])  10.5 us
  transfers between devices with their start and end apart: 8, of which 3 were waited for; matrix products, arithmetic and copies ran while one was open for 10% of the time, Pallas kernels for 20%

commit v1 on v0

v1 whole, which is shorter than its diff:
```python
import math

import jax
import jax.numpy as jnp
import ml_dtypes
import numpy as np
from jax import lax
from jax.experimental import pallas as pl
from jax.experimental.pallas import tpu as pltpu
from jax.sharding import Mesh
from jax.sharding import PartitionSpec as P

NG = 64
G = NG**3
ROWS = G // 128
FRACTION = 0.25
OMEGA = 1.0
BAND = ("y", "x", "z", "core")
SPIN_BAND = ("spin",) + BAND
ORDER = np.concatenate([np.arange(0, NG, 2), np.arange(1, NG, 2)])
STEP = 4
UNROLL = 8
PITCH = 72
EXCHANGE_FLOPS = 10**11
VMEM = pl.BlockSpec(memory_space=pltpu.VMEM)
SMEM = pl.BlockSpec(memory_space=pltpu.SMEM)


def cas_table():
    indices = np.arange(NG)
    phases = (indices[:, None] * indices[None, :] % NG) * (2.0 * math.pi / NG)
    return (np.cos(phases) + np.sin(phases)).astype(np.float32).astype(ml_dtypes.bfloat16)


def screened_kernel():
    modes = np.arange(NG)
    modes = np.where(2 * modes < NG, modes, modes - NG)
    squares = (modes * (2.0 * math.pi / NG)) ** 2
    norm_sq = squares[:, None, None] + squares[None, :, None] + squares[None, None, :]
    bounded = np.where(norm_sq > 0, norm_sq, 1.0)
    screened = np.where(
        norm_sq > 0,
        4.0 * math.pi / bounded * (1.0 - np.exp(-bounded / (4.0 * OMEGA * OMEGA))),
        math.pi / (OMEGA * OMEGA),
    )
    return (screened / NG**3).astype(np.float32)


def repeated(table):
    return np.kron(np.eye(STEP, dtype=np.float32), table.astype(np.float32)).astype(table.dtype)


def constants():
    table = cas_table()
    mixed = table[ORDER][:, ORDER]
    kernel = screened_kernel().transpose(1, 0, 2)[ORDER]
    return repeated(table), repeated(mixed), np.concatenate([kernel, kernel], axis=2)


def dot(left, right):
    return lax.dot_general(
        left, right, (((1,), (0,)), ((), ())), preferred_element_type=jnp.float32
    )


def pack_body(flat_ref, tiles_ref):
    def part(step, carry):
        columns = pl.ds(pl.multiple_of(step * 16384, 16384), 16384)
        rows = pl.ds(pl.multiple_of(step * 128, 128), 128)
        tiles_ref[rows, :] = flat_ref[0:1, columns].reshape(128, 128)
        return carry

    lax.fori_loop(0, 16, part, 0)


def unpack_body(tiles_ref, flat_ref):
    def part(step, carry):
        columns = pl.ds(pl.multiple_of(step * 16384, 16384), 16384)
        rows = pl.ds(pl.multiple_of(step * 128, 128), 128)
        value = tiles_ref[rows, :].astype(jnp.float32).reshape(1, 16384)
        flat_ref[0:1, columns] = value.astype(jnp.bfloat16)
        return carry

    lax.fori_loop(0, 16, part, 0)


def pack_flagged_body(flat_ref, flag_ref, tiles_ref):
    pack_body(flat_ref, tiles_ref)
    flag = jnp.full((16, 128), flag_ref[0], jnp.int32)
    tiles_ref[pl.ds(ROWS, 16), :] = flag.astype(jnp.float32).astype(jnp.bfloat16)


def pack_after_body(flat_ref, earlier_ref, tiles_ref):
    pack_body(flat_ref, tiles_ref)


def packed_after(flat, earlier):
    return pl.pallas_call(
        pack_after_body,
        out_shape=jax.ShapeDtypeStruct((ROWS, 128), jnp.bfloat16),
        in_specs=[VMEM, pl.BlockSpec(memory_space=pl.ANY)],
        out_specs=VMEM,
        compiler_params=pltpu.CompilerParams(vmem_limit_bytes=16 * 1024 * 1024),
        name="pack",
    )(flat, earlier)


def packed_with_flag(flat, flag):
    return pl.pallas_call(
        pack_flagged_body,
        out_shape=jax.ShapeDtypeStruct((ROWS + 16, 128), jnp.bfloat16),
        in_specs=[VMEM, SMEM],
        out_specs=VMEM,
        compiler_params=pltpu.CompilerParams(vmem_limit_bytes=16 * 1024 * 1024),
        name="pack_flagged",
    )(flat, flag)


def exchange_body(
    own_ref, prev_ref, next_ref, table_ref, mixed_ref, kernel_ref,
    out_ref, sides, middle, visitors, owner,
):
    f32, bf16 = jnp.float32, jnp.bfloat16
    low = lax.broadcasted_iota(jnp.int32, (NG // 2, 128), 1) < 64
    low_wide = lax.broadcasted_iota(jnp.int32, (NG, 128), 1) < 64

    def across_rows(plane):
        return pl.ds(pl.multiple_of(plane * PITCH, 8), NG)

    def forward(step, carry):
        densities = []
        for part in range(STEP):
            plane = step * STEP + part
            rows = pl.ds(pl.multiple_of(plane * 32, 32), 32)
            own, before, after = (
                ref[rows, :].astype(f32) for ref in (own_ref, prev_ref, next_ref)
            )
            own_turned, before_turned, after_turned = (
                pltpu.roll(value, 64, 1) for value in (own, before, after)
            )
            pairs = jnp.concatenate(
                [jnp.where(low, before, after_turned), jnp.where(low, before_turned, after)], axis=0
            )
            mine = jnp.concatenate(
                [jnp.where(low, own, own_turned), jnp.where(low, own_turned, own)], axis=0
            )
            wide = pl.ds(pl.multiple_of(plane * 64, 64), 64)
            visitors[wide, :] = pairs.astype(bf16)
            owner[wide, :] = mine.astype(bf16)
            densities.append(jnp.concatenate([mine * pairs, mine * mine], axis=1).astype(bf16))
        values = dot(jnp.concatenate(densities, axis=0), table_ref[...]).astype(bf16)
        values = dot(mixed_ref[...], values)
        for part in range(STEP):
            rows = across_rows(step * STEP + part)
            sides[rows, :] = values[part * 64 : part * 64 + 64, :128]
            middle[rows, :] = values[part * 64 : part * 64 + 64, 128:]
        return carry

    lax.fori_loop(0, NG // STEP, forward, 0, unroll=UNROLL)

    def across(step, carry):
        lines = [pl.ds(step * STEP + part, NG, stride=PITCH) for part in range(STEP)]
        values = jnp.concatenate(
            [jnp.concatenate([sides[rows, :], middle[rows, :]], axis=1) for rows in lines], axis=0
        ).astype(bf16)
        values = dot(table_ref[...], values)
        kernel = jnp.concatenate([kernel_ref[step * STEP + part] for part in range(STEP)], axis=0)
        values = (values * jnp.concatenate([kernel, kernel], axis=1)).astype(bf16)
        values = dot(table_ref[...], values)
        for part, rows in enumerate(lines):
            sides[rows, :] = values[part * 64 : part * 64 + 64, :128]
            middle[rows, :] = values[part * 64 : part * 64 + 64, 128:]
        return carry

    lax.fori_loop(0, NG // STEP, across, 0, unroll=UNROLL)

    own_fill, prev_fill, next_fill = (
        ref[pl.ds(ROWS, 16), :].astype(f32)[:1] * -FRACTION
        for ref in (own_ref, prev_ref, next_ref)
    )
    side_fill = jnp.where(low_wide, prev_fill, next_fill)
    own_fill = jnp.where(low_wide, own_fill, 0.0)

    def backward(step, carry):
        planes = [step * STEP + part for part in range(STEP)]
        values = jnp.concatenate(
            [
                jnp.concatenate(
                    [sides[across_rows(plane), :], middle[across_rows(plane), :]], axis=1
                )
                for plane in planes
            ],
            axis=0,
        ).astype(bf16)
        values = dot(mixed_ref[...], values).astype(bf16)
        values = dot(values, table_ref[...])
        for part, plane in enumerate(planes):
            wide = pl.ds(pl.multiple_of(plane * 64, 64), 64)
            potential = values[part * 64 : part * 64 + 64]
            total = potential[:, :128] * (visitors[wide, :].astype(f32) * side_fill)
            total = total + potential[:, 128:] * (owner[wide, :].astype(f32) * own_fill)
            total = total + pltpu.roll(total, 64, 1)
            rows = pl.ds(pl.multiple_of(plane * 32, 32), 32)
            out_ref[rows, :] = jnp.where(low, total[:32], total[32:]).astype(bf16)
        return carry

    lax.fori_loop(0, NG // STEP, backward, 0, unroll=UNROLL)


def exchange_of(own, before, after):
    table, mixed, kernel = (jnp.asarray(value) for value in constants())
    return pl.pallas_call(
        exchange_body,
        out_shape=jax.ShapeDtypeStruct((ROWS, 128), jnp.bfloat16),
        in_specs=[VMEM] * 6,
        out_specs=VMEM,
        scratch_shapes=[
            pltpu.VMEM((NG * PITCH, 128), jnp.float32),
            pltpu.VMEM((NG * PITCH, 128), jnp.float32),
            pltpu.VMEM((NG * NG, 128), jnp.bfloat16),
            pltpu.VMEM((NG * NG, 128), jnp.bfloat16),
        ],
        compiler_params=pltpu.CompilerParams(vmem_limit_bytes=32 * 1024 * 1024),
        cost_estimate=pl.CostEstimate(
            flops=EXCHANGE_FLOPS, bytes_accessed=4 * 1024 * 1024, transcendentals=0
        ),
        name="exchange",
    )(own, before, after, table, mixed, kernel)


def by_line_body(tiles_ref, out_ref, wide):
    wide[...] = tiles_ref[...].astype(jnp.float32)
    for line in range(16):
        rows = wide[pl.ds(line, 128, stride=16), :]
        out_ref[pl.ds(line * 128, 128), :] = rows.astype(jnp.bfloat16)


def aside_body(tiles_ref, exchange_ref, lines_ref, flat_ref, wide):
    by_line_body(tiles_ref, lines_ref, wide)
    unpack_body(exchange_ref, flat_ref)


def beside_slabs(tiles, exchange):
    return pl.pallas_call(
        aside_body,
        out_shape=(
            jax.ShapeDtypeStruct((ROWS, 128), jnp.bfloat16),
            jax.ShapeDtypeStruct((1, G), jnp.bfloat16),
        ),
        in_specs=[VMEM, VMEM],
        out_specs=(VMEM, VMEM),
        scratch_shapes=[pltpu.VMEM((ROWS, 128), jnp.float32)],
        compiler_params=pltpu.CompilerParams(vmem_limit_bytes=16 * 1024 * 1024),
        name="beside_slabs",
    )(tiles.reshape(ROWS, 128), exchange)


def intersection_body(tiles_ref, trial_ref, core_ref, lines_ref, mine_ref, other_ref, wide):
    by_line_body(tiles_ref, lines_ref, wide)
    total = jnp.zeros((128, 128), jnp.float32)
    for line in range(16):
        rows = pl.ds(line * 128, 128)
        total = total + lax.dot_general(
            trial_ref[rows, :], lines_ref[rows, :], (((1,), (1,)), ((), ())),
            preferred_element_type=jnp.float32,
        )
    total = total * (1.0 / math.sqrt(G))
    first = core_ref[0] == 0
    mine_ref[...] = jnp.where(first, total[:64], total[64:])
    other_ref[...] = jnp.where(first, total[64:], total[:64])


def intersection_of(tiles, trial_lines, core):
    half = jax.ShapeDtypeStruct((64, 128), jnp.float32)
    return pl.pallas_call(
        intersection_body,
        out_shape=(jax.ShapeDtypeStruct((ROWS, 128), jnp.bfloat16), half, half),
        in_specs=[VMEM, VMEM, SMEM],
        out_specs=(VMEM, VMEM, VMEM),
        scratch_shapes=[pltpu.VMEM((ROWS, 128), jnp.float32)],
        compiler_params=pltpu.CompilerParams(vmem_limit_bytes=16 * 1024 * 1024),
        name="intersection",
    )(tiles.reshape(ROWS, 128), trial_lines, core)


def projected_body(lines_ref, mine_ref, other_ref, core_ref, out_ref):
    first = core_ref[0] == 0
    mine, other = mine_ref[...].astype(jnp.float32), other_ref[...].astype(jnp.float32)
    table = jnp.concatenate(
        [jnp.where(first, mine, other), jnp.where(first, other, mine)], axis=0
    ).astype(jnp.bfloat16)
    for line in range(16):
        rows = pl.ds(line * 128, 128)
        value = dot(table, lines_ref[rows, :]) * (-1.0 / math.sqrt(128))
        out_ref[:, rows] = value.astype(jnp.bfloat16)


def projected_of(lines, mine, other, core):
    return pl.pallas_call(
        projected_body,
        out_shape=jax.ShapeDtypeStruct((128, ROWS), jnp.bfloat16),
        in_specs=[VMEM, VMEM, VMEM, SMEM],
        out_specs=VMEM,
        compiler_params=pltpu.CompilerParams(vmem_limit_bytes=16 * 1024 * 1024),
        name="projected",
    )(lines, mine, other, core)


def passed_along(value, steps):
    count = lax.axis_size(BAND)
    return lax.ppermute(value, BAND, [(i, (i + steps) % count) for i in range(count)])


def swapped(value):
    return lax.ppermute(value, "core", [(0, 1), (1, 0)])


def summed_over(value, axes):
    peers = lax.axis_size(axes)
    copies = jnp.broadcast_to(value[None], (peers,) + value.shape)
    tiles = lax.all_to_all(copies, axes, 0, 0, tiled=True)
    return jnp.sum(tiles.astype(jnp.float32), axis=0).astype(jnp.bfloat16)


def to_slabs(rows):
    return lax.all_to_all(rows.reshape(128, 16, 128), BAND, 0, 0, tiled=True)


def local(orbitals, trial, occupations):
    own = packed_with_flag(orbitals, occupations)
    before, after = passed_along(own, 1), passed_along(own, -1)
    trial_tiles = to_slabs(packed_after(trial, own))
    exchange = exchange_of(own, before, after)
    exchange_tiles = to_slabs(exchange)
    trial_lines, flat = beside_slabs(trial_tiles, exchange)
    core = lax.axis_index("core").astype(jnp.int32).reshape(1)
    lines, mine, other = intersection_of(exchange_tiles, trial_lines, core)
    half = (mine + swapped(other)).astype(jnp.bfloat16)
    half = summed_over(half, ("y", "x"))
    half = summed_over(half, "z")
    projected = projected_of(lines, half, swapped(half), core)
    return flat, projected


def solution(mesh):
    finer = Mesh(mesh.devices.reshape(mesh.shape["spin"], 4, 2, 8, 2), SPIN_BAND)
    return jax.shard_map(
        local,
        mesh=finer,
        in_specs=(P(SPIN_BAND, None), P(SPIN_BAND, None), P(SPIN_BAND)),
        out_specs=(P(SPIN_BAND, None), P("spin", BAND)),
        check_vma=False,
    )
```

time: 153 us -> 98.3 us (0.64)
  other arithmetic: 26.1 us -> 0.06 us
  Pallas kernels: 33 us -> 12.7 us
  starting transfers between devices: 47.6 us -> 27.8 us
  waiting for transfers between devices: 22.5 us -> 33.4 us
    unnamed x2 -> x0, other arithmetic: 24.8 us -> none
    pallas_call x1, Pallas kernels: 30.9 us -> 6.52 us  [exchange_of(): pl.pallas_call(exchange_body, out_shape=jax.ShapeDtypeStruct((ROWS, 128),...]
    all_to_all x2, starting transfers between devices: 34 us -> 21.3 us  [to_slabs(): return lax.all_to_all(rows.reshape(128, 16, 128), BAND, 0, 0, tiled=True)]
    all_to_all x2, waiting for transfers between devices: 21.1 us -> 31.3 us  [to_slabs(): return lax.all_to_all(rows.reshape(128, 16, 128), BAND, 0, 0, tiled=True)]
    ppermute x4 -> x2, starting transfers between devices: 10.5 us -> 3.41 us  [passed_along(): lax.ppermute(value, BAND, [(i, (i + steps) % count) for i in range(count)])]
    pallas_call x1 -> x3, Pallas kernels: 0.38 us -> 4.41 us  [the longest x1 3.34 us: beside_slabs(): pl.pallas_call(aside_body, out_shape=(jax.ShapeDtypeStruct((ROWS, 128), j...]
  transfers between devices with their start and end apart: 8 -> 6, of which waited for: 3 -> 4; matrix products, arithmetic and copies ran while one was open for 10% -> 0% of each run, Pallas kernels for 20% -> 11%
where the time goes in v1:
time: 98.3 us; the launch traced here: 97.9 us
  waiting for transfers between devices  33.4 us (34%)
  starting transfers between devices  27.8 us (28%)
  blocking collectives  19.8 us (20%)
  Pallas kernels  12.7 us (13%)
  local copies, waits for them, and re-layouts  2.86 us (3%)
  between operations  1.38 us (1%)
    all_to_all x2, waiting for transfers between devices, to_slabs(): return lax.all_to_all(rows.reshape(128, 16, 128), BAND, 0, 0, tiled=True)  31.3 us
    all_to_all x2, starting transfers between devices, to_slabs(): return lax.all_to_all(rows.reshape(128, 16, 128), BAND, 0, 0, tiled=True)  21.3 us
    all_to_all x2, blocking collectives, summed_over(): tiles = lax.all_to_all(copies, axes, 0, 0, tiled=True)  19.8 us
    pallas_call x1, Pallas kernels, exchange_of(): pl.pallas_call(exchange_body, out_shape=jax.ShapeDtypeStruct((ROWS, 128),...  6.52 us
    ppermute x2, starting transfers between devices, passed_along(): lax.ppermute(value, BAND, [(i, (i + steps) % count) for i in range(count)])  3.41 us
    pallas_call x1, Pallas kernels, beside_slabs(): pl.pallas_call(aside_body, out_shape=(jax.ShapeDtypeStruct((ROWS, 128), j...  3.34 us
    ppermute x2, starting transfers between devices, swapped(): return lax.ppermute(value, 'core', [(0, 1), (1, 0)])  3.06 us
    unnamed x10, local copies, waits for them, and re-layouts  2.82 us
  transfers between devices with their start and end apart: 6, of which 4 were waited for; matrix products, arithmetic and copies ran while one was open for 0% of the time, Pallas kernels for 11%

profile of v1, /device:TPU:1, one launch (start us, length us, event | category | flops | bytes accessed | tf_op | source)
XLA Modules:
  0.0 97.9 jit_solution(15163190309112765729)
XLA Ops:
  1.3 0.0 copy-start
  1.3 1.2 %copy-done = bf16[1,262144]{1,0:T(2,128)(2,1)S(1)} copy-done((bf16[1,262144]{1,0:T(2,128)(2,1)S(1)}, bf16[1,262144]{1,0:T(2,128)(2,1)}, u32[]{:S(2)}) %copy-start) | copy-done | bytes 524312
  2.5 0.0 copy-start.1
  2.5 0.0 copy-start.3
  2.5 0.0 copy-start.4
  2.5 0.1 pack_flagged.1.earlier_ref.own_ref
  2.7 3.1 %collective-permute-start = (bf16[2064,128]{1,0:T(8,128)(2,1)S(1)}, bf16[2064,128]{1,0:T(8,128)(2,1)S(1)}, u32[]{:S(2)}, u32[]{:S(2)}) collective-permute-start(bf16[2064,128]{1,0:T(8,128)(2,1)S(1)} %pack_flagged.1.earlier_ref.own_ref), channel_id=1, source_target_pairs={{0,1},{1,2},{2,3},{3,4},{4,5},{5,6},{6,7},{7,8},{8,9},{9,10},{10,1... | collective-permute-start | bytes 1585160 | tf_op jit(solution)/shard_map/ppermute | solution.py:311
  5.8 0.3 collective-permute-start.1
  6.1 0.0 copy-done.1
  6.1 0.9 pack.1
  7.0 16.0 %all-to-all-start = ((bf16[128,16,128]{2,1,0:T(8,128)(2,1)}), bf16[128,16,128]{2,1,0:T(8,128)(2,1)S(1)}, u32[]{:S(2)}, u32[]{:S(2)}) async-start(bf16[128,16,128]{2,1,0:T(8,128)(2,1)} %bitcast), calls=%async_computation | async-start | bytes 1048576 | tf_op jit(solution)/shard_map/all_to_all | solution.py:326
  23.0 0.0 collective-permute-done.prev_ref
  23.0 0.0 collective-permute-done.1.next_ref
  23.0 0.0 copy-done.3
  23.1 0.0 copy-done.4
  23.1 0.0 copy-start.2
  23.1 1.6 %copy-done.2 = f32[64,64,128]{2,1,0:T(8,128)S(1)} copy-done((f32[64,64,128]{2,1,0:T(8,128)S(1)}, f32[64,64,128]{2,1,0:T(8,128)}, u32[]{:S(2)}) %copy-start.2) | copy-done | bytes 2097176
  24.7 6.5 %exchange.1.exchange_ref = bf16[2048,128]{1,0:T(8,128)(2,1)} custom-call(bf16[2064,128]{1,0:T(8,128)(2,1)S(1)} %pack_flagged.1.earlier_ref.own_ref, bf16[2064,128]{1,0:T(8,128)(2,1)S(1)} %collective-permute-done.prev_ref, bf16[2064,128]{1,0:T(8,128)(2,1)S(1)} %collective-permute-done.1.next_ref, bf16[256,256]{1,0:T(8,128)(2,1)S(1)} %copy-done.3, ...), custom_call_target="tpu_custom_call" | custom-call | flops 99999997952 | bytes 4194304 | tf_op jit(solution)/shard_map/exchange/pallas_call | solution.py:212
  31.2 13.3 %all-to-all-done = bf16[128,16,128]{2,1,0:T(8,128)(2,1)S(1)} async-done(((bf16[128,16,128]{2,1,0:T(8,128)(2,1)}), bf16[128,16,128]{2,1,0:T(8,128)(2,1)S(1)}, u32[]{:S(2)}, u32[]{:S(2)}) %all-to-all-start) | async-done | bytes 524320 | tf_op jit(solution)/shard_map/all_to_all | solution.py:326
  44.5 5.3 %all-to-all-start.1 = ((bf16[128,16,128]{2,1,0:T(8,128)(2,1)}), bf16[128,16,128]{2,1,0:T(8,128)(2,1)S(1)}, u32[]{:S(2)}, u32[]{:S(2)}) async-start(bf16[128,16,128]{2,1,0:T(8,128)(2,1)} %bitcast.2), calls=%async_computation.1 | async-start | bytes 1048576 | tf_op jit(solution)/shard_map/all_to_all | solution.py:326
  49.8 3.3 %beside_slabs.1 = (bf16[2048,128]{1,0:T(8,128)(2,1)S(1)}, bf16[1,262144]{1,0:T(2,128)(2,1)}) custom-call(bf16[2048,128]{1,0:T(8,128)(2,1)S(1)} %bitcast.5, bf16[2048,128]{1,0:T(8,128)(2,1)} %exchange.1.exchange_ref), custom_call_target="tpu_custom_call" | custom-call | tf_op jit(solution)/shard_map/beside_slabs/pallas_call | solution.py:244
  53.2 18.0 %all-to-all-done.1 = bf16[128,16,128]{2,1,0:T(8,128)(2,1)S(1)} async-done(((bf16[128,16,128]{2,1,0:T(8,128)(2,1)}), bf16[128,16,128]{2,1,0:T(8,128)(2,1)S(1)}, u32[]{:S(2)}, u32[]{:S(2)}) %all-to-all-start.1) | async-done | bytes 524320 | tf_op jit(solution)/shard_map/all_to_all | solution.py:326
  71.2 0.7 intersection.1
  71.9 0.1 collective-permute-start.2
  72.0 1.2 %collective-permute-done.2 = f32[64,128]{1,0:T(8,128)S(1)} collective-permute-done((f32[64,128]{1,0:T(8,128)S(1)}, f32[64,128]{1,0:T(8,128)S(1)}, u32[]{:S(2)}, u32[]{:S(2)}) %collective-permute-start.2) | collective-permute-done | bytes 32800 | tf_op jit(solution)/shard_map/ppermute | solution.py:315
  73.2 9.4 %all_to_all.20 = bf16[8,64,128]{2,1,0:T(8,128)(2,1)S(1)} all-to-all(bf16[8,64,128]{2,1,0:T(8,128)(2,1)S(1)} %broadcast_in_dim.4), channel_id=1, replica_groups=mesh['spin'=2,'y'=4,'x'=2,'z'=8,'core'=2] {'y','x'}, dimensions={0} | all-to-all | bytes 262144 | tf_op jit(solution)/shard_map/all_to_all | solution.py:321
  82.7 10.3 %all_to_all.21 = bf16[8,64,128]{2,1,0:T(8,128)(2,1)S(1)} all-to-all(bf16[8,64,128]{2,1,0:T(8,128)(2,1)S(1)} %broadcast_in_dim.5), channel_id=1, replica_groups=mesh['spin'=2,'y'=4,'x'=2,'z'=8,'core'=2] {'z'}, dimensions={0} | all-to-all | bytes 262144 | tf_op jit(solution)/shard_map/all_to_all | solution.py:321
  93.0 3.0 %collective-permute-start.3 = (bf16[64,128]{1,0:T(8,128)(2,1)S(1)}, bf16[64,128]{1,0:T(8,128)(2,1)S(1)}, u32[]{:S(2)}, u32[]{:S(2)}) collective-permute-start(bf16[64,128]{1,0:T(8,128)(2,1)S(1)} %reduce_sum.25.mine_ref), channel_id=1, source_target_pairs={{0,1},{1,0},{2,3},{3,2},{4,5},{5,4},{6,7},{7,6},{8,9},{9,8},{10,11... | collective-permute-start | bytes 49160 | tf_op jit(solution)/shard_map/ppermute | solution.py:315
  96.0 0.8 collective-permute-done.3.other_ref
  96.8 1.1 %projected.1 = bf16[128,2048]{1,0:T(8,128)(2,1)} custom-call(bf16[2048,128]{1,0:T(8,128)(2,1)S(1)} %get-tuple-element.9.lines_ref, bf16[64,128]{1,0:T(8,128)(2,1)S(1)} %reduce_sum.25.mine_ref, bf16[64,128]{1,0:T(8,128)(2,1)S(1)} %collective-permute-done.3.other_ref, s32[1]{0:T(128)} %bitcast.4.core_ref), custom_call_target="tpu_custom_call" | custom-call | tf_op jit(solution)/shard_map/projected/pallas_call | solution.py:299
  (5 shorter events, 0.1 us)
Async XLA Ops:
  1.3 1.2 %copy-start = (bf16[1,262144]{1,0:T(2,128)(2,1)S(1)}, bf16[1,262144]{1,0:T(2,128)(2,1)}, u32[]{:S(2)}) copy-start(bf16[1,262144]{1,0:T(2,128)(2,1)} %flat_ref.2) | copy-start | bytes 1572868
  2.5 3.6 %copy-start.1 = (bf16[1,262144]{1,0:T(2,128)(2,1)S(1)}, bf16[1,262144]{1,0:T(2,128)(2,1)}, u32[]{:S(2)}) copy-start(bf16[1,262144]{1,0:T(2,128)(2,1)} %flat_ref.3) | copy-start | bytes 1572868
  2.5 20.5 %copy-start.3 = (bf16[256,256]{1,0:T(8,128)(2,1)S(1)}, bf16[256,256]{1,0:T(8,128)(2,1)}, u32[]{:S(2)}) copy-start(bf16[256,256]{1,0:T(8,128)(2,1)} %constant.14.clone.table_ref) | copy-start | bytes 393220
  2.5 20.6 %copy-start.4 = (bf16[256,256]{1,0:T(8,128)(2,1)S(1)}, bf16[256,256]{1,0:T(8,128)(2,1)}, u32[]{:S(2)}) copy-start(bf16[256,256]{1,0:T(8,128)(2,1)} %constant.15.clone.mixed_ref) | copy-start | bytes 393220
  2.7 20.4 %collective-permute-start = (bf16[2064,128]{1,0:T(8,128)(2,1)S(1)}, bf16[2064,128]{1,0:T(8,128)(2,1)S(1)}, u32[]{:S(2)}, u32[]{:S(2)}) collective-permute-start(bf16[2064,128]{1,0:T(8,128)(2,1)S(1)} %pack_flagged.1.earlier_ref.own_ref), channel_id=1, source_target_pairs={{0,1},{1,2},{2,3},{3,4},{4,5},{5,6},{6,7},{7,8},{8,9},{9,10},{10,1... | collective-permute-start | bytes 1585160 | tf_op jit(solution)/shard_map/ppermute | solution.py:311
  5.8 17.3 %collective-permute-start.1 = (bf16[2064,128]{1,0:T(8,128)(2,1)S(1)}, bf16[2064,128]{1,0:T(8,128)(2,1)S(1)}, u32[]{:S(2)}, u32[]{:S(2)}) collective-permute-start(bf16[2064,128]{1,0:T(8,128)(2,1)S(1)} %pack_flagged.1.earlier_ref.own_ref), channel_id=1, source_target_pairs={{0,127},{1,0},{2,1},{3,2},{4,3},{5,4},{6,5},{7,6},{8,7},{9,8},{10,... | collective-permute-start | bytes 1585160 | tf_op jit(solution)/shard_map/ppermute | solution.py:311
  7.0 37.5 %all-to-all-start = ((bf16[128,16,128]{2,1,0:T(8,128)(2,1)}), bf16[128,16,128]{2,1,0:T(8,128)(2,1)S(1)}, u32[]{:S(2)}, u32[]{:S(2)}) async-start(bf16[128,16,128]{2,1,0:T(8,128)(2,1)} %bitcast), calls=%async_computation | async-start | bytes 1048576 | tf_op jit(solution)/shard_map/all_to_all | solution.py:326
  23.1 1.6 %copy-start.2 = (f32[64,64,128]{2,1,0:T(8,128)S(1)}, f32[64,64,128]{2,1,0:T(8,128)}, u32[]{:S(2)}) copy-start(f32[64,64,128]{2,1,0:T(8,128)} %constant.16.clone.kernel_ref) | copy-start | bytes 6291460
  44.5 26.7 %all-to-all-start.1 = ((bf16[128,16,128]{2,1,0:T(8,128)(2,1)}), bf16[128,16,128]{2,1,0:T(8,128)(2,1)S(1)}, u32[]{:S(2)}, u32[]{:S(2)}) async-start(bf16[128,16,128]{2,1,0:T(8,128)(2,1)} %bitcast.2), calls=%async_computation.1 | async-start | bytes 1048576 | tf_op jit(solution)/shard_map/all_to_all | solution.py:326
  71.9 1.3 %collective-permute-start.2 = (f32[64,128]{1,0:T(8,128)S(1)}, f32[64,128]{1,0:T(8,128)S(1)}, u32[]{:S(2)}, u32[]{:S(2)}) collective-permute-start(f32[64,128]{1,0:T(8,128)S(1)} %get-tuple-element.11), channel_id=1, source_target_pairs={{0,1},{1,0},{2,3},{3,2},{4,5},{5,4},{6,7},{7,6},{8,9},{9,8},{10,11... | collective-permute-start | bytes 98312 | tf_op jit(solution)/shard_map/ppermute | solution.py:315
  93.0 3.8 %collective-permute-start.3 = (bf16[64,128]{1,0:T(8,128)(2,1)S(1)}, bf16[64,128]{1,0:T(8,128)(2,1)S(1)}, u32[]{:S(2)}, u32[]{:S(2)}) collective-permute-start(bf16[64,128]{1,0:T(8,128)(2,1)S(1)} %reduce_sum.25.mine_ref), channel_id=1, source_target_pairs={{0,1},{1,0},{2,3},{3,2},{4,5},{5,4},{6,7},{7,6},{8,9},{9,8},{10,11... | collective-permute-start | bytes 49160 | tf_op jit(solution)/shard_map/ppermute | solution.py:315

commit v2 on v0

v2 whole, which is shorter than its diff:
```python
import math

import jax
import jax.numpy as jnp
import ml_dtypes
import numpy as np
from jax import lax
from jax.experimental import pallas as pl
from jax.experimental.pallas import tpu as pltpu
from jax.sharding import Mesh
from jax.sharding import PartitionSpec as P

NG = 64
G = NG**3
ROWS = G // 128
FRACTION = 0.25
OMEGA = 1.0
BAND = ("y", "x", "z", "core")
SPIN_BAND = ("spin",) + BAND
ORDER = np.concatenate([np.arange(0, NG, 2), np.arange(1, NG, 2)])
STEP = 4
SPAN = 2 * STEP
PITCH = 72
OWN_FLOPS = 10**10
VMEM = pl.BlockSpec(memory_space=pltpu.VMEM)
SMEM = pl.BlockSpec(memory_space=pltpu.SMEM)


def cas_table():
    indices = np.arange(NG)
    phases = (indices[:, None] * indices[None, :] % NG) * (2.0 * math.pi / NG)
    return (np.cos(phases) + np.sin(phases)).astype(np.float32).astype(ml_dtypes.bfloat16)


def screened_kernel():
    modes = np.arange(NG)
    modes = np.where(2 * modes < NG, modes, modes - NG)
    squares = (modes * (2.0 * math.pi / NG)) ** 2
    norm_sq = squares[:, None, None] + squares[None, :, None] + squares[None, None, :]
    bounded = np.where(norm_sq > 0, norm_sq, 1.0)
    screened = np.where(
        norm_sq > 0,
        4.0 * math.pi / bounded * (1.0 - np.exp(-bounded / (4.0 * OMEGA * OMEGA))),
        math.pi / (OMEGA * OMEGA),
    )
    return (screened / NG**3).astype(np.float32)


def repeated(table):
    return np.kron(np.eye(STEP, dtype=np.float32), table.astype(np.float32)).astype(table.dtype)


def constants():
    table = cas_table()
    mixed = table[ORDER][:, ORDER]
    kernel = screened_kernel().transpose(1, 0, 2)[ORDER]
    return repeated(table), repeated(mixed), np.concatenate([kernel, kernel], axis=2)


def dot(left, right):
    return lax.dot_general(
        left, right, (((1,), (0,)), ((), ())), preferred_element_type=jnp.float32
    )


def pack_body(flat_ref, tiles_ref):
    def part(step, carry):
        columns = pl.ds(pl.multiple_of(step * 16384, 16384), 16384)
        rows = pl.ds(pl.multiple_of(step * 128, 128), 128)
        tiles_ref[rows, :] = flat_ref[0:1, columns].reshape(128, 128)
        return carry

    lax.fori_loop(0, 16, part, 0)


def pack_flagged_body(flat_ref, flag_ref, tiles_ref):
    pack_body(flat_ref, tiles_ref)
    flag = jnp.full((16, 128), flag_ref[0], jnp.int32)
    tiles_ref[pl.ds(ROWS, 16), :] = flag.astype(jnp.float32).astype(jnp.bfloat16)


def pack_after_body(flat_ref, earlier_ref, tiles_ref):
    pack_body(flat_ref, tiles_ref)


def packed_after(flat, earlier):
    return pl.pallas_call(
        pack_after_body,
        out_shape=jax.ShapeDtypeStruct((ROWS, 128), jnp.bfloat16),
        in_specs=[VMEM, pl.BlockSpec(memory_space=pl.ANY)],
        out_specs=VMEM,
        compiler_params=pltpu.CompilerParams(vmem_limit_bytes=16 * 1024 * 1024),
        name="pack",
    )(flat, earlier)


def packed_with_flag(flat, flag):
    return pl.pallas_call(
        pack_flagged_body,
        out_shape=jax.ShapeDtypeStruct((ROWS + 16, 128), jnp.bfloat16),
        in_specs=[VMEM, SMEM],
        out_specs=VMEM,
        compiler_params=pltpu.CompilerParams(vmem_limit_bytes=16 * 1024 * 1024),
        name="pack_flagged",
    )(flat, flag)


def plane_rows(plane, height):
    return pl.ds(pl.multiple_of(plane * height, height), height)


def passes_there(density_of, table_ref, mixed_ref, kernel_ref, grid):
    bf16 = jnp.bfloat16

    def pitched(plane):
        return pl.ds(pl.multiple_of(plane * PITCH, 8), NG)

    def beside(parts):
        return jnp.concatenate(
            [jnp.concatenate(parts[:STEP], axis=0), jnp.concatenate(parts[STEP:], axis=0)], axis=1
        )

    def part_of(values, part):
        rows = slice(part % STEP * NG, part % STEP * NG + NG)
        return values[rows, :128] if part < STEP else values[rows, 128:]

    def forward(step, carry):
        planes = [step * SPAN + part for part in range(SPAN)]
        values = beside([density_of(plane) for plane in planes])
        values = dot(values, table_ref[...]).astype(bf16)
        values = dot(mixed_ref[...], values)
        for part, plane in enumerate(planes):
            grid[pitched(plane), :] = part_of(values, part)
        return carry

    lax.fori_loop(0, NG // SPAN, forward, 0, unroll=True)

    def across(step, carry):
        lines = [step * SPAN + part for part in range(SPAN)]
        rows = [pl.ds(line, NG, stride=PITCH) for line in lines]
        values = beside([grid[row, :].astype(bf16) for row in rows])
        values = dot(table_ref[...], values)
        values = (values * beside([kernel_ref[line] for line in lines])).astype(bf16)
        values = dot(table_ref[...], values)
        for part, row in enumerate(rows):
            grid[row, :] = part_of(values, part)
        return carry

    lax.fori_loop(0, NG // SPAN, across, 0, unroll=True)

    def potentials(step):
        planes = [step * SPAN + part for part in range(SPAN)]
        values = beside([grid[pitched(plane), :].astype(bf16) for plane in planes])
        values = dot(mixed_ref[...], values).astype(bf16)
        values = dot(values, table_ref[...])
        return [(plane, part_of(values, part)) for part, plane in enumerate(planes)]

    return potentials


def fill_of(ref):
    return ref[pl.ds(ROWS, 16), :].astype(jnp.float32)[:1] * -FRACTION


def both_halves(value, low):
    turned = pltpu.roll(value, 64, 1)
    return jnp.concatenate([jnp.where(low, value, turned), jnp.where(low, turned, value)], axis=0)


def low_lanes(height):
    return lax.broadcasted_iota(jnp.int32, (height, 128), 1) < 64


def own_body(own_ref, table_ref, mixed_ref, kernel_ref, owner_ref, term_ref, grid):
    f32, bf16 = jnp.float32, jnp.bfloat16
    low = low_lanes(NG // 2)

    def density_of(plane):
        mine = both_halves(own_ref[plane_rows(plane, 32), :].astype(f32), low)
        owner_ref[plane_rows(plane, 64), :] = mine.astype(bf16)
        return (mine * mine).astype(bf16)

    potentials = passes_there(density_of, table_ref, mixed_ref, kernel_ref, grid)
    fill = fill_of(own_ref)

    def backward(step, carry):
        for plane, potential in potentials(step):
            total = potential * (owner_ref[plane_rows(plane, 64), :].astype(f32) * fill)
            term_ref[plane_rows(plane, 32), :] = jnp.where(low, total[:32], total[32:])
        return carry

    lax.fori_loop(0, NG // SPAN, backward, 0, unroll=True)


def own_term(own, table, mixed, kernel):
    return pl.pallas_call(
        own_body,
        out_shape=(
            jax.ShapeDtypeStruct((NG * NG, 128), jnp.bfloat16),
            jax.ShapeDtypeStruct((ROWS, 128), jnp.float32),
        ),
        in_specs=[VMEM] * 4,
        out_specs=(VMEM, VMEM),
        scratch_shapes=[pltpu.VMEM((NG * PITCH, 128), jnp.float32)],
        compiler_params=pltpu.CompilerParams(vmem_limit_bytes=24 * 1024 * 1024),
        cost_estimate=pl.CostEstimate(
            flops=OWN_FLOPS, bytes_accessed=4 * 1024 * 1024, transcendentals=0
        ),
        name="own_term",
    )(own, table, mixed, kernel)


def exchange_body(
    prev_ref, next_ref, owner_ref, term_ref, trial_ref, table_ref, mixed_ref, kernel_ref,
    out_ref, visitors, grid,
):
    f32, bf16 = jnp.float32, jnp.bfloat16
    low = low_lanes(NG // 2)

    def density_of(plane):
        before, after = (ref[plane_rows(plane, 32), :].astype(f32) for ref in (prev_ref, next_ref))
        before_turned, after_turned = (pltpu.roll(value, 64, 1) for value in (before, after))
        pairs = jnp.concatenate(
            [jnp.where(low, before, after_turned), jnp.where(low, before_turned, after)], axis=0
        )
        wide = plane_rows(plane, 64)
        visitors[wide, :] = pairs.astype(bf16)
        return (pairs * owner_ref[wide, :].astype(f32)).astype(bf16)

    potentials = passes_there(density_of, table_ref, mixed_ref, kernel_ref, grid)
    fill = jnp.where(low_lanes(NG), fill_of(prev_ref), fill_of(next_ref))

    def backward(step, carry):
        for plane, potential in potentials(step):
            total = potential * (visitors[plane_rows(plane, 64), :].astype(f32) * fill)
            total = total + pltpu.roll(total, 64, 1)
            rows = plane_rows(plane, 32)
            value = (jnp.where(low, total[:32], total[32:]) + term_ref[rows, :]).astype(bf16)
            trial = trial_ref[rows, :]
            out_ref[plane_rows(plane, 64), :] = jnp.concatenate(
                [trial[:16], value[:16], trial[16:], value[16:]], axis=0
            )
        return carry

    lax.fori_loop(0, NG // SPAN, backward, 0, unroll=True)


def exchange_of(before, after, owner, term, trial, table, mixed, kernel):
    return pl.pallas_call(
        exchange_body,
        out_shape=jax.ShapeDtypeStruct((2 * ROWS, 128), jnp.bfloat16),
        in_specs=[VMEM] * 8,
        out_specs=VMEM,
        scratch_shapes=[
            pltpu.VMEM((NG * NG, 128), jnp.bfloat16),
            pltpu.VMEM((NG * PITCH, 128), jnp.float32),
        ],
        compiler_params=pltpu.CompilerParams(vmem_limit_bytes=24 * 1024 * 1024),
        name="exchange",
    )(before, after, owner, term, trial, table, mixed, kernel)


def unpack_body(tiles_ref, flat_ref, token_ref):
    def part(step, carry):
        columns = pl.ds(pl.multiple_of(step * 16384, 16384), 16384)
        tiles = [tiles_ref[pl.ds(step * 256 + peer * 32 + 16, 16), :] for peer in range(8)]
        value = jnp.concatenate(tiles, axis=0).astype(jnp.float32).reshape(1, 16384)
        flat_ref[0:1, columns] = value.astype(jnp.bfloat16)
        return carry

    lax.fori_loop(0, 16, part, 0)
    token_ref[...] = tiles_ref[pl.ds(0, 16), :]


def unpacked(tiles):
    return pl.pallas_call(
        unpack_body,
        out_shape=(
            jax.ShapeDtypeStruct((1, G), jnp.bfloat16),
            jax.ShapeDtypeStruct((16, 128), jnp.bfloat16),
        ),
        in_specs=[VMEM],
        out_specs=(VMEM, VMEM),
        compiler_params=pltpu.CompilerParams(vmem_limit_bytes=16 * 1024 * 1024),
        name="unpack",
    )(tiles)


def intersection_body(tiles_ref, token_ref, lines_ref, copies_ref, wide):
    bf16 = jnp.bfloat16
    wide[...] = tiles_ref[...].astype(jnp.float32)
    total = jnp.zeros((128, 128), jnp.float32)
    for line in range(16):
        trial = wide[pl.ds(line, 128, stride=32), :].astype(bf16)
        value = wide[pl.ds(line + 16, 128, stride=32), :].astype(bf16)
        lines_ref[pl.ds(line * 128, 128), :] = value
        total = total + lax.dot_general(
            trial, value, (((1,), (1,)), ((), ())), preferred_element_type=jnp.float32
        )
    total = (total * (1.0 / math.sqrt(G))).astype(bf16)
    for peer in range(8):
        copies_ref[pl.ds(peer * 128, 128), :] = total


def intersection_of(tiles, token):
    return pl.pallas_call(
        intersection_body,
        out_shape=(
            jax.ShapeDtypeStruct((ROWS, 128), jnp.bfloat16),
            jax.ShapeDtypeStruct((8 * 128, 128), jnp.bfloat16),
        ),
        in_specs=[VMEM, pl.BlockSpec(memory_space=pl.ANY)],
        out_specs=(VMEM, VMEM),
        scratch_shapes=[pltpu.VMEM((2 * ROWS, 128), jnp.float32)],
        compiler_params=pltpu.CompilerParams(vmem_limit_bytes=16 * 1024 * 1024),
        name="intersection",
    )(tiles, token)


def summed_copies_body(tiles_ref, copies_ref):
    total = tiles_ref[0].astype(jnp.float32)
    for peer in range(1, 16):
        total = total + tiles_ref[peer].astype(jnp.float32)
    total = total.astype(jnp.bfloat16)
    for peer in range(16):
        copies_ref[peer] = total


def summed_copies(tiles):
    return pl.pallas_call(
        summed_copies_body,
        out_shape=jax.ShapeDtypeStruct((16, 64, 128), jnp.bfloat16),
        in_specs=[VMEM],
        out_specs=VMEM,
        compiler_params=pltpu.CompilerParams(vmem_limit_bytes=16 * 1024 * 1024),
        name="summed_copies",
    )(tiles)


def projected_body(lines_ref, tiles_ref, out_ref):
    halves = []
    for core in range(2):
        total = tiles_ref[core].astype(jnp.float32)
        for peer in range(1, 8):
            total = total + tiles_ref[2 * peer + core].astype(jnp.float32)
        halves.append(total)
    table = jnp.concatenate(halves, axis=0).astype(jnp.bfloat16)
    for line in range(16):
        rows = pl.ds(line * 128, 128)
        value = dot(table, lines_ref[rows, :]) * (-1.0 / math.sqrt(128))
        out_ref[:, rows] = value.astype(jnp.bfloat16)


def projected_of(lines, tiles):
    return pl.pallas_call(
        projected_body,
        out_shape=jax.ShapeDtypeStruct((128, ROWS), jnp.bfloat16),
        in_specs=[VMEM, VMEM],
        out_specs=VMEM,
        compiler_params=pltpu.CompilerParams(vmem_limit_bytes=16 * 1024 * 1024),
        name="projected",
    )(lines, tiles)


def passed_along(value, steps):
    count = lax.axis_size(BAND)
    return lax.ppermute(value, BAND, [(i, (i + steps) % count) for i in range(count)])


def sent_around(tiles, axes):
    return lax.all_to_all(tiles, axes, 0, 0, tiled=True)


def local(orbitals, trial, occupations):
    tables = [jnp.asarray(value) for value in constants()]
    own = packed_with_flag(orbitals, occupations)
    before, after = passed_along(own, 1), passed_along(own, -1)
    trial_rows = packed_after(trial, own)
    owner, term = own_term(own, *tables)
    both = exchange_of(before, after, owner, term, trial_rows, *tables)
    tiles = sent_around(both.reshape(128, 32, 128), BAND).reshape(2 * ROWS, 128)
    flat, token = unpacked(both)
    lines, copies = intersection_of(tiles, token)
    parts = sent_around(copies.reshape(16, 64, 128), ("y", "x", "core"))
    parts = sent_around(summed_copies(parts), ("z", "core"))
    return flat, projected_of(lines, parts)


def solution(mesh):
    finer = Mesh(mesh.devices.reshape(mesh.shape["spin"], 4, 2, 8, 2), SPIN_BAND)
    return jax.shard_map(
        local,
        mesh=finer,
        in_specs=(P(SPIN_BAND, None), P(SPIN_BAND, None), P(SPIN_BAND)),
        out_specs=(P(SPIN_BAND, None), P("spin", BAND)),
        check_vma=False,
    )
```

time: 153 us -> 101 us (0.66)
  other arithmetic: 26.1 us -> 0 us
  starting transfers between devices: 47.6 us -> 21.5 us
  Pallas kernels: 33 us -> 12.6 us
  waiting for transfers between devices: 22.5 us -> 33.7 us
  blocking collectives: 19.8 us -> 27.7 us
    unnamed x2 -> x0, other arithmetic: 24.8 us -> none
    pallas_call x2 -> x6, Pallas kernels: 31.3 us -> 10.2 us  [the longest x1 3.93 us: exchange_of(): pl.pallas_call(exchange_body, out_shape=jax.ShapeDtypeStruct((2 * ROWS, 1...]
    all_to_all x2 -> x1, starting transfers between devices: 34 us -> 18.1 us  [sent_around(): return lax.all_to_all(tiles, axes, 0, 0, tiled=True)]
    all_to_all x2, blocking collectives: 19.8 us -> 27.7 us  [sent_around(): return lax.all_to_all(tiles, axes, 0, 0, tiled=True)]
    all_to_all x2 -> x1, waiting for transfers between devices: 21.1 us -> 28.8 us  [sent_around(): return lax.all_to_all(tiles, axes, 0, 0, tiled=True)]
    ppermute x4 -> x2, starting transfers between devices: 10.5 us -> 3.32 us  [passed_along(): lax.ppermute(value, BAND, [(i, (i + steps) % count) for i in range(count)])]
    ppermute x4 -> x2, waiting for transfers between devices: 0.19 us -> 4.9 us  [passed_along(): lax.ppermute(value, BAND, [(i, (i + steps) % count) for i in range(count)])]
    ppermute x2 -> x0, starting transfers between devices: 3.06 us -> none  [swapped(): return lax.ppermute(value, 'core', [(0, 1), (1, 0)])]
  transfers between devices with their start and end apart: 8 -> 3, of which waited for: 3 -> 3; matrix products, arithmetic and copies ran while one was open for 10% -> 0% of each run, Pallas kernels for 20% -> 6%
where the time goes in v2:
time: 101 us; the launch traced here: 100 us
  waiting for transfers between devices  33.7 us (33%)
  blocking collectives  27.7 us (27%)
  starting transfers between devices  21.5 us (21%)
  Pallas kernels  12.6 us (12%)
  local copies, waits for them, and re-layouts  3.27 us (3%)
  between operations  1.5 us (1%)
    all_to_all x1, waiting for transfers between devices, sent_around(): return lax.all_to_all(tiles, axes, 0, 0, tiled=True)  28.8 us
    all_to_all x2, blocking collectives, sent_around(): return lax.all_to_all(tiles, axes, 0, 0, tiled=True)  27.7 us
    all_to_all x1, starting transfers between devices, sent_around(): return lax.all_to_all(tiles, axes, 0, 0, tiled=True)  18.1 us
    ppermute x2, waiting for transfers between devices, passed_along(): lax.ppermute(value, BAND, [(i, (i + steps) % count) for i in range(count)])  4.9 us
    pallas_call x1, Pallas kernels, exchange_of(): pl.pallas_call(exchange_body, out_shape=jax.ShapeDtypeStruct((2 * ROWS, 1...  3.93 us
    ppermute x2, starting transfers between devices, passed_along(): lax.ppermute(value, BAND, [(i, (i + steps) % count) for i in range(count)])  3.32 us
    unnamed x10, local copies, waits for them, and re-layouts  3.27 us
    pallas_call x1, Pallas kernels, unpacked(): pl.pallas_call(unpack_body, out_shape=(jax.ShapeDtypeStruct((1, G), jnp.b...  3.14 us
  transfers between devices with their start and end apart: 3, of which 3 were waited for; matrix products, arithmetic and copies ran while one was open for 0% of the time, Pallas kernels for 6%

profile of v2, /device:TPU:1, one launch (start us, length us, event | category | flops | bytes accessed | tf_op | source)
XLA Modules:
  0.0 100.3 jit_solution(4644413331115303775)
XLA Ops:
  0.6 0.0 copy-start
  1.4 0.0 copy-start.1
  1.4 1.2 %copy-done.1 = bf16[1,262144]{1,0:T(2,128)(2,1)S(1)} copy-done((bf16[1,262144]{1,0:T(2,128)(2,1)S(1)}, bf16[1,262144]{1,0:T(2,128)(2,1)}, u32[]{:S(2)}) %copy-start.1) | copy-done | bytes 524312
  2.7 0.1 pack_flagged.1.own_ref.earlier_ref
  2.8 3.3 %collective-permute-start.1 = (bf16[2064,128]{1,0:T(8,128)(2,1)S(1)}, bf16[2064,128]{1,0:T(8,128)(2,1)S(1)}, u32[]{:S(2)}, u32[]{:S(2)}) collective-permute-start(bf16[2064,128]{1,0:T(8,128)(2,1)S(1)} %pack_flagged.1.own_ref.earlier_ref), channel_id=1, source_target_pairs={{0,127},{1,0},{2,1},{3,2},{4,3},{5,4},{6,5},{7,6},{8,7},{9,8},{10,... | collective-permute-start | bytes 1585160 | tf_op jit(solution)/shard_map/ppermute | solution.py:367
  6.1 0.0 collective-permute-start
  6.1 0.0 copy-start.2
  6.1 1.2 %copy-done.2 = bf16[1,262144]{1,0:T(2,128)(2,1)S(1)} copy-done((bf16[1,262144]{1,0:T(2,128)(2,1)S(1)}, bf16[1,262144]{1,0:T(2,128)(2,1)}, u32[]{:S(2)}) %copy-start.2) | copy-done | bytes 524312
  7.4 0.0 copy-start.3
  7.4 0.0 copy-start.4
  7.4 0.1 pack.1.trial_ref
  7.5 0.0 copy-done
  7.5 0.8 copy-done.3
  8.3 0.1 copy-done.4
  8.3 2.8 %own_term.1 = (bf16[4096,128]{1,0:T(8,128)(2,1)S(1)}, f32[2048,128]{1,0:T(8,128)S(1)}) custom-call(bf16[2064,128]{1,0:T(8,128)(2,1)S(1)} %pack_flagged.1.own_ref.earlier_ref, bf16[256,256]{1,0:T(8,128)(2,1)S(1)} %copy-done.4, bf16[256,256]{1,0:T(8,128)(2,1)S(1)} %copy-done.3, f32[64,64,128]{2,1,0:T(8,128)S(1)} %copy-done), custom_call_target="tpu_custom_call" | custom-call | flops 10000000000 | bytes 4194304 | tf_op jit(solution)/shard_map/own_term/pallas_call | solution.py:196
  11.1 1.7 %collective-permute-done.1.next_ref = bf16[2064,128]{1,0:T(8,128)(2,1)S(1)} collective-permute-done((bf16[2064,128]{1,0:T(8,128)(2,1)S(1)}, bf16[2064,128]{1,0:T(8,128)(2,1)S(1)}, u32[]{:S(2)}, u32[]{:S(2)}) %collective-permute-start.1) | collective-permute-done | bytes 528416 | tf_op jit(solution)/shard_map/ppermute | solution.py:367
  12.8 3.2 %collective-permute-done.prev_ref = bf16[2064,128]{1,0:T(8,128)(2,1)S(1)} collective-permute-done((bf16[2064,128]{1,0:T(8,128)(2,1)S(1)}, bf16[2064,128]{1,0:T(8,128)(2,1)S(1)}, u32[]{:S(2)}, u32[]{:S(2)}) %collective-permute-start) | collective-permute-done | bytes 528416 | tf_op jit(solution)/shard_map/ppermute | solution.py:367
  16.0 3.9 %exchange.1.tiles_ref = bf16[4096,128]{1,0:T(8,128)(2,1)} custom-call(bf16[2064,128]{1,0:T(8,128)(2,1)S(1)} %collective-permute-done.prev_ref, bf16[2064,128]{1,0:T(8,128)(2,1)S(1)} %collective-permute-done.1.next_ref, bf16[4096,128]{1,0:T(8,128)(2,1)S(1)} %get-tuple-element.8.owner_ref, f32[2048,128]{1,0:T(8,128)S(1)} %get-tuple-element.9.term_ref, ...), custom_call_target="tpu_custom_call" | custom-call | tf_op jit(solution)/shard_map/exchange/pallas_call | solution.py:249
  19.9 18.1 %all-to-all-start = ((bf16[128,32,128]{2,1,0:T(8,128)(2,1)}), bf16[128,32,128]{2,1,0:T(8,128)(2,1)S(1)}, u32[]{:S(2)}, u32[]{:S(2)}) async-start(bf16[128,32,128]{2,1,0:T(8,128)(2,1)} %bitcast), calls=%async_computation | async-start | bytes 2097152 | tf_op jit(solution)/shard_map/all_to_all | solution.py:371
  38.1 3.1 %unpack.1 = (bf16[1,262144]{1,0:T(2,128)(2,1)}, bf16[16,128]{1,0:T(8,128)(2,1)S(1)}) custom-call(bf16[4096,128]{1,0:T(8,128)(2,1)} %exchange.1.tiles_ref), custom_call_target="tpu_custom_call" | custom-call | tf_op jit(solution)/shard_map/unpack/pallas_call | solution.py:276
  41.2 28.8 %all-to-all-done = bf16[128,32,128]{2,1,0:T(8,128)(2,1)S(1)} async-done(((bf16[128,32,128]{2,1,0:T(8,128)(2,1)}), bf16[128,32,128]{2,1,0:T(8,128)(2,1)S(1)}, u32[]{:S(2)}, u32[]{:S(2)}) %all-to-all-start) | async-done | bytes 1048608 | tf_op jit(solution)/shard_map/all_to_all | solution.py:371
  70.0 1.4 %intersection.1 = (bf16[2048,128]{1,0:T(8,128)(2,1)S(1)}, bf16[1024,128]{1,0:T(8,128)(2,1)S(1)}) custom-call(bf16[4096,128]{1,0:T(8,128)(2,1)S(1)} %bitcast.3, bf16[16,128]{1,0:T(8,128)(2,1)S(1)} %get-tuple-element.11.token_ref), custom_call_target="tpu_custom_call" | custom-call | tf_op jit(solution)/shard_map/intersection/pallas_call | solution.py:306
  71.4 12.1 %all_to_all.15.tiles_ref = bf16[16,64,128]{2,1,0:T(8,128)(2,1)S(1)} all-to-all(bf16[16,64,128]{2,1,0:T(8,128)(2,1)S(1)} %bitcast.4), channel_id=1, replica_groups=mesh['spin'=2,'y'=4,'x'=2,'z'=8,'core'=2] {'y','x','core'}, dimensions={0} | all-to-all | bytes 524288 | tf_op jit(solution)/shard_map/all_to_all | solution.py:371
  83.5 15.7 %all_to_all.16.tiles_ref = bf16[16,64,128]{2,1,0:T(8,128)(2,1)S(1)} all-to-all(bf16[16,64,128]{2,1,0:T(8,128)(2,1)S(1)} %summed_copies.1), channel_id=1, replica_groups=mesh['spin'=2,'y'=4,'x'=2,'z'=8,'core'=2] {'z','core'}, dimensions={0} | all-to-all | bytes 524288 | tf_op jit(solution)/shard_map/all_to_all | solution.py:371
  99.2 1.1 %projected.1 = bf16[128,2048]{1,0:T(8,128)(2,1)} custom-call(bf16[2048,128]{1,0:T(8,128)(2,1)S(1)} %get-tuple-element.12.lines_ref, bf16[16,64,128]{2,1,0:T(8,128)(2,1)S(1)} %all_to_all.16.tiles_ref), custom_call_target="tpu_custom_call" | custom-call | tf_op jit(solution)/shard_map/projected/pallas_call | solution.py:355
  (1 shorter events, 0.0 us)
Async XLA Ops:
  0.6 6.9 %copy-start = (f32[64,64,128]{2,1,0:T(8,128)S(1)}, f32[64,64,128]{2,1,0:T(8,128)}, u32[]{:S(2)}) copy-start(f32[64,64,128]{2,1,0:T(8,128)} %constant.8.clone.kernel_ref) | copy-start | bytes 6291460
  1.4 1.2 %copy-start.1 = (bf16[1,262144]{1,0:T(2,128)(2,1)S(1)}, bf16[1,262144]{1,0:T(2,128)(2,1)}, u32[]{:S(2)}) copy-start(bf16[1,262144]{1,0:T(2,128)(2,1)} %flat_ref.2) | copy-start | bytes 1572868
  2.8 10.0 %collective-permute-start.1 = (bf16[2064,128]{1,0:T(8,128)(2,1)S(1)}, bf16[2064,128]{1,0:T(8,128)(2,1)S(1)}, u32[]{:S(2)}, u32[]{:S(2)}) collective-permute-start(bf16[2064,128]{1,0:T(8,128)(2,1)S(1)} %pack_flagged.1.own_ref.earlier_ref), channel_id=1, source_target_pairs={{0,127},{1,0},{2,1},{3,2},{4,3},{5,4},{6,5},{7,6},{8,7},{9,8},{10,... | collective-permute-start | bytes 1585160 | tf_op jit(solution)/shard_map/ppermute | solution.py:367
  6.1 9.9 %collective-permute-start = (bf16[2064,128]{1,0:T(8,128)(2,1)S(1)}, bf16[2064,128]{1,0:T(8,128)(2,1)S(1)}, u32[]{:S(2)}, u32[]{:S(2)}) collective-permute-start(bf16[2064,128]{1,0:T(8,128)(2,1)S(1)} %pack_flagged.1.own_ref.earlier_ref), channel_id=1, source_target_pairs={{0,1},{1,2},{2,3},{3,4},{4,5},{5,6},{6,7},{7,8},{8,9},{9,10},{10,1... | collective-permute-start | bytes 1585160 | tf_op jit(solution)/shard_map/ppermute | solution.py:367
  6.1 1.2 %copy-start.2 = (bf16[1,262144]{1,0:T(2,128)(2,1)S(1)}, bf16[1,262144]{1,0:T(2,128)(2,1)}, u32[]{:S(2)}) copy-start(bf16[1,262144]{1,0:T(2,128)(2,1)} %flat_ref.3) | copy-start | bytes 1572868
  7.4 0.9 copy-start.3
  7.4 1.0 copy-start.4
  19.9 50.1 %all-to-all-start = ((bf16[128,32,128]{2,1,0:T(8,128)(2,1)}), bf16[128,32,128]{2,1,0:T(8,128)(2,1)S(1)}, u32[]{:S(2)}, u32[]{:S(2)}) async-start(bf16[128,32,128]{2,1,0:T(8,128)(2,1)} %bitcast), calls=%async_computation | async-start | bytes 2097152 | tf_op jit(solution)/shard_map/all_to_all | solution.py:371

commit v3 on v2

--- a/solution.py
+++ b/solution.py
@@ -21,7 +21,8 @@
 STEP = 4
 SPAN = 2 * STEP
 PITCH = 72
-OWN_FLOPS = 10**10
+PARTS = 8
+EXCHANGE_FLOPS = 10**11
 VMEM = pl.BlockSpec(memory_space=pltpu.VMEM)
 SMEM = pl.BlockSpec(memory_space=pltpu.SMEM)
 
@@ -63,46 +64,67 @@
     )
 
 
-def pack_body(flat_ref, tiles_ref):
-    def part(step, carry):
-        columns = pl.ds(pl.multiple_of(step * 16384, 16384), 16384)
-        rows = pl.ds(pl.multiple_of(step * 128, 128), 128)
-        tiles_ref[rows, :] = flat_ref[0:1, columns].reshape(128, 128)
-        return carry
-
-    lax.fori_loop(0, 16, part, 0)
-
-
-def pack_flagged_body(flat_ref, flag_ref, tiles_ref):
-    pack_body(flat_ref, tiles_ref)
+def pack_body(
+    own_hbm, trial_hbm, flag_ref, own_out, trial_out,
+    own_flat, trial_flat, own_tiles, trial_tiles, arrived, left, flag_left,
+):
+    width, height = G // PARTS, ROWS // PARTS
+
+    def copy_in(source, flat, which, part):
+        columns = pl.ds(part * width, width)
+        return pltpu.make_async_copy(
+            source.at[:, columns], flat.at[:, columns], arrived.at[which, part]
+        )
+
+    def copy_out(tiles, target, which, part):
+        rows = pl.ds(part * height, height)
+        return pltpu.make_async_copy(tiles.at[rows, :], target.at[rows, :], left.at[which, part])
+
+    arrays = (
+        (own_hbm, own_flat, own_tiles, own_out),
+        (trial_hbm, trial_flat, trial_tiles, trial_out),
+    )
+    for which, (source, flat, _, _) in enumerate(arrays):
+        for part in range(PARTS):
+            copy_in(source, flat, which, part).start()
     flag = jnp.full((16, 128), flag_ref[0], jnp.int32)
-    tiles_ref[pl.ds(ROWS, 16), :] = flag.astype(jnp.float32).astype(jnp.bfloat16)
-
-
-def pack_after_body(flat_ref, earlier_ref, tiles_ref):
-    pack_body(flat_ref, tiles_ref)
-
-
-def packed_after(flat, earlier):
-    return pl.pallas_call(
-        pack_after_body,
-        out_shape=jax.ShapeDtypeStruct((ROWS, 128), jnp.bfloat16),
-        in_specs=[VMEM, pl.BlockSpec(memory_space=pl.ANY)],
-        out_specs=VMEM,
-        compiler_params=pltpu.CompilerParams(vmem_limit_bytes=16 * 1024 * 1024),
+    last = pl.ds(ROWS, 16)
+    own_tiles[last, :] = flag.astype(jnp.float32).astype(jnp.bfloat16)
+    flag_copy = pltpu.make_async_copy(own_tiles.at[last, :], own_out.at[last, :], flag_left)
+    flag_copy.start()
+    for which, (source, flat, tiles, target) in enumerate(arrays):
+        for part in range(PARTS):
+            copy_in(source, flat, which, part).wait()
+            value = flat[0:1, pl.ds(part * width, width)].reshape(height, 128)
+            tiles[pl.ds(part * height, height), :] = value
+            copy_out(tiles, target, which, part).start()
+    flag_copy.wait()
+    for which, (_, _, tiles, target) in enumerate(arrays):
+        for part in range(PARTS):
+            copy_out(tiles, target, which, part).wait()
+
+
+def packed(orbitals, trial, occupations):
+    anywhere = pl.BlockSpec(memory_space=pltpu.HBM)
+    own = jax.ShapeDtypeStruct((ROWS + 16, 128), jnp.bfloat16)
+    other = jax.ShapeDtypeStruct((ROWS, 128), jnp.bfloat16)
+    return pl.pallas_call(
+        pack_body,
+        out_shape=(own, other),
+        in_specs=[anywhere, anywhere, SMEM],
+        out_specs=(anywhere, anywhere),
+        scratch_shapes=[
+            pltpu.VMEM((1, G), jnp.bfloat16),
+            pltpu.VMEM((1, G), jnp.bfloat16),
+            pltpu.VMEM(own.shape, jnp.bfloat16),
+            pltpu.VMEM(other.shape, jnp.bfloat16),
+            pltpu.SemaphoreType.DMA((2, PARTS)),
+            pltpu.SemaphoreType.DMA((2, PARTS)),
+            pltpu.SemaphoreType.DMA,
+        ],
+        compiler_params=pltpu.CompilerParams(vmem_limit_bytes=58 * 1024 * 1024),
         name="pack",
-    )(flat, earlier)
-
-
-def packed_with_flag(flat, flag):
-    return pl.pallas_call(
-        pack_flagged_body,
-        out_shape=jax.ShapeDtypeStruct((ROWS + 16, 128), jnp.bfloat16),
-        in_specs=[VMEM, SMEM],
-        out_specs=VMEM,
-        compiler_params=pltpu.CompilerParams(vmem_limit_bytes=16 * 1024 * 1024),
-        name="pack_flagged",
-    )(flat, flag)
+    )(orbitals, trial, occupations)
 
 
 def plane_rows(plane, height):
@@ -204,14 +226,14 @@
         scratch_shapes=[pltpu.VMEM((NG * PITCH, 128), jnp.float32)],
         compiler_params=pltpu.CompilerParams(vmem_limit_bytes=24 * 1024 * 1024),
         cost_estimate=pl.CostEstimate(
-            flops=OWN_FLOPS, bytes_accessed=4 * 1024 * 1024, transcendentals=0
+            flops=EXCHANGE_FLOPS, bytes_accessed=4 * 1024 * 1024, transcendentals=0
         ),
         name="own_term",
     )(own, table, mixed, kernel)
 
 
 def exchange_body(
-    prev_ref, next_ref, owner_ref, term_ref, trial_ref, table_ref, mixed_ref, kernel_ref,
+    prev_ref, next_ref, owner_ref, term_ref, table_ref, mixed_ref, kernel_ref,
     out_ref, visitors, grid,
 ):
     f32, bf16 = jnp.float32, jnp.bfloat16
@@ -236,130 +258,117 @@
             total = total + pltpu.roll(total, 64, 1)
             rows = plane_rows(plane, 32)
             value = (jnp.where(low, total[:32], total[32:]) + term_ref[rows, :]).astype(bf16)
-            trial = trial_ref[rows, :]
-            out_ref[plane_rows(plane, 64), :] = jnp.concatenate(
-                [trial[:16], value[:16], trial[16:], value[16:]], axis=0
-            )
+            out_ref[rows, :] = value
         return carry
 
     lax.fori_loop(0, NG // SPAN, backward, 0, unroll=True)
 
 
-def exchange_of(before, after, owner, term, trial, table, mixed, kernel):
+def exchange_of(before, after, owner, term, table, mixed, kernel):
     return pl.pallas_call(
         exchange_body,
-        out_shape=jax.ShapeDtypeStruct((2 * ROWS, 128), jnp.bfloat16),
-        in_specs=[VMEM] * 8,
+        out_shape=jax.ShapeDtypeStruct((ROWS, 128), jnp.bfloat16),
+        in_specs=[VMEM] * 7,
         out_specs=VMEM,
         scratch_shapes=[
             pltpu.VMEM((NG * NG, 128), jnp.bfloat16),
             pltpu.VMEM((NG * PITCH, 128), jnp.float32),
         ],
         compiler_params=pltpu.CompilerParams(vmem_limit_bytes=24 * 1024 * 1024),
+        cost_estimate=pl.CostEstimate(
+            flops=EXCHANGE_FLOPS, bytes_accessed=4 * 1024 * 1024, transcendentals=0
+        ),
         name="exchange",
-    )(before, after, owner, term, trial, table, mixed, kernel)
-
-
-def unpack_body(tiles_ref, flat_ref, token_ref):
+    )(before, after, owner, term, table, mixed, kernel)
+
+
+def unpack_body(tiles_ref, flat_ref):
     def part(step, carry):
         columns = pl.ds(pl.multiple_of(step * 16384, 16384), 16384)
-        tiles = [tiles_ref[pl.ds(step * 256 + peer * 32 + 16, 16), :] for peer in range(8)]
-        value = jnp.concatenate(tiles, axis=0).astype(jnp.float32).reshape(1, 16384)
+        rows = pl.ds(pl.multiple_of(step * 128, 128), 128)
+        value = tiles_ref[rows, :].astype(jnp.float32).reshape(1, 16384)
         flat_ref[0:1, columns] = value.astype(jnp.bfloat16)
         return carry
 
     lax.fori_loop(0, 16, part, 0)
-    token_ref[...] = tiles_ref[pl.ds(0, 16), :]
-
-
-def unpacked(tiles):
-    return pl.pallas_call(
-        unpack_body,
+
+
+def by_line_body(tiles_ref, out_ref, wide):
+    wide[...] = tiles_ref[...].astype(jnp.float32)
+    for line in range(16):
+        rows = wide[pl.ds(line, 128, stride=16), :]
+        out_ref[pl.ds(line * 128, 128), :] = rows.astype(jnp.bfloat16)
+
+
+def aside_body(tiles_ref, exchange_ref, lines_ref, flat_ref, wide):
+    by_line_body(tiles_ref, lines_ref, wide)
+    unpack_body(exchange_ref, flat_ref)
+
+
+def beside_slabs(tiles, exchange):
+    return pl.pallas_call(
+        aside_body,
         out_shape=(
+            jax.ShapeDtypeStruct((ROWS, 128), jnp.bfloat16),
             jax.ShapeDtypeStruct((1, G), jnp.bfloat16),
-            jax.ShapeDtypeStruct((16, 128), jnp.bfloat16),
         ),
-        in_specs=[VMEM],
+        in_specs=[VMEM, VMEM],
         out_specs=(VMEM, VMEM),
+        scratch_shapes=[pltpu.VMEM((ROWS, 128), jnp.float32)],
         compiler_params=pltpu.CompilerParams(vmem_limit_bytes=16 * 1024 * 1024),
-        name="unpack",
-    )(tiles)
-
-
-def intersection_body(tiles_ref, token_ref, lines_ref, copies_ref, wide):
-    bf16 = jnp.bfloat16
-    wide[...] = tiles_ref[...].astype(jnp.float32)
+        name="beside_slabs",
+    )(tiles.reshape(ROWS, 128), exchange)
+
+
+def intersection_body(tiles_ref, trial_ref, core_ref, lines_ref, mine_ref, other_ref, wide):
+    by_line_body(tiles_ref, lines_ref, wide)
     total = jnp.zeros((128, 128), jnp.float32)
     for line in range(16):
-        trial = wide[pl.ds(line, 128, stride=32), :].astype(bf16)
-        value = wide[pl.ds(line + 16, 128, stride=32), :].astype(bf16)
-        lines_ref[pl.ds(line * 128, 128), :] = value
+        rows = pl.ds(line * 128, 128)
         total = total + lax.dot_general(
-            trial, value, (((1,), (1,)), ((), ())), preferred_element_type=jnp.float32
+            trial_ref[rows, :], lines_ref[rows, :], (((1,), (1,)), ((), ())),
+            preferred_element_type=jnp.float32,
         )
-    total = (total * (1.0 / math.sqrt(G))).astype(bf16)
-    for peer in range(8):
-        copies_ref[pl.ds(peer * 128, 128), :] = total
-
-
-def intersection_of(tiles, token):
+    total = total * (1.0 / math.sqrt(G))
+    first = core_ref[0] == 0
+    mine_ref[...] = jnp.where(first, total[:64], total[64:])
+    other_ref[...] = jnp.where(first, total[64:], total[:64])
+
+
+def intersection_of(tiles, trial_lines, core):
+    half = jax.ShapeDtypeStruct((64, 128), jnp.float32)
     return pl.pallas_call(
         intersection_body,
-        out_shape=(
-            jax.ShapeDtypeStruct((ROWS, 128), jnp.bfloat16),
-            jax.ShapeDtypeStruct((8 * 128, 128), jnp.bfloat16),
-        ),
-        in_specs=[VMEM, pl.BlockSpec(memory_space=pl.ANY)],
-        out_specs=(VMEM, VMEM),
-        scratch_shapes=[pltpu.VMEM((2 * ROWS, 128), jnp.float32)],
+        out_shape=(jax.ShapeDtypeStruct((ROWS, 128), jnp.bfloat16), half, half),
+        in_specs=[VMEM, VMEM, SMEM],
+        out_specs=(VMEM, VMEM, VMEM),
+        scratch_shapes=[pltpu.VMEM((ROWS, 128), jnp.float32)],
         compiler_params=pltpu.CompilerParams(vmem_limit_bytes=16 * 1024 * 1024),
         name="intersection",
-    )(tiles, token)
-
-
-def summed_copies_body(tiles_ref, copies_ref):
-    total = tiles_ref[0].astype(jnp.float32)
-    for peer in range(1, 16):
-        total = total + tiles_ref[peer].astype(jnp.float32)
-    total = total.astype(jnp.bfloat16)
-    for peer in range(16):
-        copies_ref[peer] = total
-
-
-def summed_copies(tiles):
-    return pl.pallas_call(
-        summed_copies_body,
-        out_shape=jax.ShapeDtypeStruct((16, 64, 128), jnp.bfloat16),
-        in_specs=[VMEM],
-        out_specs=VMEM,
-        compiler_params=pltpu.CompilerParams(vmem_limit_bytes=16 * 1024 * 1024),
-        name="summed_copies",
-    )(tiles)
-
-
-def projected_body(lines_ref, tiles_ref, out_ref):
-    halves = []
-    for core in range(2):
-        total = tiles_ref[core].astype(jnp.float32)
-        for peer in range(1, 8):
-            total = total + tiles_ref[2 * peer + core].astype(jnp.float32)
-        halves.append(total)
-    table = jnp.concatenate(halves, axis=0).astype(jnp.bfloat16)
+    )(tiles.reshape(ROWS, 128), trial_lines, core)
+
+
+def projected_body(lines_ref, mine_ref, other_ref, core_ref, out_ref):
+    first = core_ref[0] == 0
+    mine, other = mine_ref[...].astype(jnp.float32), other_ref[...].astype(jnp.float32)
+    table = jnp.concatenate(
+        [jnp.where(first, mine, other), jnp.where(first, other, mine)], axis=0
+    ).astype(jnp.bfloat16)
     for line in range(16):
         rows = pl.ds(line * 128, 128)
         value = dot(table, lines_ref[rows, :]) * (-1.0 / math.sqrt(128))
         out_ref[:, rows] = value.astype(jnp.bfloat16)
 
 
-def projected_of(lines, tiles):
+def projected_of(lines, mine, other, core):
     return pl.pallas_call(
         projected_body,
         out_shape=jax.ShapeDtypeStruct((128, ROWS), jnp.bfloat16),
-        in_specs=[VMEM, VMEM],
+        in_specs=[VMEM, VMEM, VMEM, SMEM],
         out_specs=VMEM,
         compiler_params=pltpu.CompilerParams(vmem_limit_bytes=16 * 1024 * 1024),
         name="projected",
-    )(lines, tiles)
+    )(lines, mine, other, core)
 
 
 def passed_along(value, steps):
@@ -367,23 +376,35 @@
     return lax.ppermute(value, BAND, [(i, (i + steps) % count) for i in range(count)])
 
 
-def sent_around(tiles, axes):
-    return lax.all_to_all(tiles, axes, 0, 0, tiled=True)
+def swapped(value):
+    return lax.ppermute(value, "core", [(0, 1), (1, 0)])
+
+
+def summed_over(value, axes):
+    peers = lax.axis_size(axes)
+    copies = jnp.broadcast_to(value[None], (peers,) + value.shape)
+    tiles = lax.all_to_all(copies, axes, 0, 0, tiled=True)
+    return jnp.sum(tiles.astype(jnp.float32), axis=0).astype(jnp.bfloat16)
+
+
+def to_slabs(rows):
+    return lax.all_to_all(rows.reshape(128, 16, 128), BAND, 0, 0, tiled=True)
 
 
 def local(orbitals, trial, occupations):
     tables = [jnp.asarray(value) for value in constants()]
-    own = packed_with_flag(orbitals, occupations)
+    own, trial_rows = packed(orbitals, trial, occupations)
     before, after = passed_along(own, 1), passed_along(own, -1)
-    trial_rows = packed_after(trial, own)
-    owner, term = own_term(own, *tables)
-    both = exchange_of(before, after, owner, term, trial_rows, *tables)
-    tiles = sent_around(both.reshape(128, 32, 128), BAND).reshape(2 * ROWS, 128)
-    flat, token = unpacked(both)
-    lines, copies = intersection_of(tiles, token)
-    parts = sent_around(copies.reshape(16, 64, 128), ("y", "x", "core"))
-    parts = sent_around(summed_copies(parts), ("z", "core"))
-    return flat, projected_of(lines, parts)
+    trial_tiles = to_slabs(trial_rows)
+    exchange = exchange_of(before, after, *own_term(own, *tables), *tables)
+    exchange_tiles = to_slabs(exchange)
+    trial_lines, flat = beside_slabs(trial_tiles, exchange)
+    core = lax.axis_index("core").astype(jnp.int32).reshape(1)
+    lines, mine, other = intersection_of(exchange_tiles, trial_lines, core)
+    half = (mine + swapped(other)).astype(jnp.bfloat16)
+    half = summed_over(half, ("y", "x"))
+    half = summed_over(half, "z")
+    return flat, projected_of(lines, half, swapped(half), core)
 
 
 def solution(mesh):

time: 101 us -> 98.8 us (0.978)
  blocking collectives: 27.7 us -> 19.8 us
  starting transfers between devices: 21.5 us -> 28.4 us
  local copies, waits for them, and re-layouts: 3.27 us -> 1.1 us
  Pallas kernels: 12.6 us -> 14 us
    all_to_all x2, blocking collectives: 27.7 us -> 19.8 us  [summed_over(): tiles = lax.all_to_all(copies, axes, 0, 0, tiled=True)]
    ppermute x2, waiting for transfers between devices: 4.9 us -> 0.01 us  [passed_along(): lax.ppermute(value, BAND, [(i, (i + steps) % count) for i in range(count)])]
    all_to_all x1 -> x2, starting transfers between devices: 18.1 us -> 22 us  [to_slabs(): return lax.all_to_all(rows.reshape(128, 16, 128), BAND, 0, 0, tiled=True)]
    ppermute x0 -> x2, starting transfers between devices: none -> 3.06 us  [swapped(): return lax.ppermute(value, 'core', [(0, 1), (1, 0)])]
    all_to_all x1 -> x2, waiting for transfers between devices: 28.8 us -> 31.5 us  [to_slabs(): return lax.all_to_all(rows.reshape(128, 16, 128), BAND, 0, 0, tiled=True)]
    unnamed x10 -> x8, local copies, waits for them, and re-layouts: 3.27 us -> 1.06 us
    pallas_call x5 -> x3, Pallas kernels: 7.38 us -> 9.55 us  [the longest x1 3.56 us: exchange_of(): pl.pallas_call(exchange_body, out_shape=jax.ShapeDtypeStruct((ROWS, 128),...]
    ppermute x0 -> x2, waiting for transfers between devices: none -> 2.03 us  [swapped(): return lax.ppermute(value, 'core', [(0, 1), (1, 0)])]
  transfers between devices with their start and end apart: 3 -> 6, of which waited for: 3 -> 4; matrix products, arithmetic and copies ran while one was open for 0% -> 0% of each run, Pallas kernels for 6% -> 10%
where the time goes in v3:
time: 98.8 us; the launch traced here: 98.4 us
  waiting for transfers between devices  33.6 us (34%)
  starting transfers between devices  28.4 us (29%)
  blocking collectives  19.8 us (20%)
  Pallas kernels  14 us (14%)
  between operations  1.56 us (2%)
  local copies, waits for them, and re-layouts  1.1 us (1%)
    all_to_all x2, waiting for transfers between devices, to_slabs(): return lax.all_to_all(rows.reshape(128, 16, 128), BAND, 0, 0, tiled=True)  31.5 us
    all_to_all x2, starting transfers between devices, to_slabs(): return lax.all_to_all(rows.reshape(128, 16, 128), BAND, 0, 0, tiled=True)  22 us
    all_to_all x2, blocking collectives, summed_over(): tiles = lax.all_to_all(copies, axes, 0, 0, tiled=True)  19.8 us
    pallas_call x1, Pallas kernels, exchange_of(): pl.pallas_call(exchange_body, out_shape=jax.ShapeDtypeStruct((ROWS, 128),...  3.56 us
    pallas_call x1, Pallas kernels, beside_slabs(): pl.pallas_call(aside_body, out_shape=(jax.ShapeDtypeStruct((ROWS, 128), j...  3.46 us
    ppermute x2, starting transfers between devices, passed_along(): lax.ppermute(value, BAND, [(i, (i + steps) % count) for i in range(count)])  3.41 us
    ppermute x2, starting transfers between devices, swapped(): return lax.ppermute(value, 'core', [(0, 1), (1, 0)])  3.06 us
    pallas_call x1, Pallas kernels, own_term(): pl.pallas_call(own_body, out_shape=(jax.ShapeDtypeStruct((NG * NG, 128),...  2.66 us
  transfers between devices with their start and end apart: 6, of which 4 were waited for; matrix products, arithmetic and copies ran while one was open for 0% of the time, Pallas kernels for 10%

profile of v3, /device:TPU:1, one launch (start us, length us, event | category | flops | bytes accessed | tf_op | source)
XLA Modules:
  0.0 98.4 jit_solution(5681777693208161765)
XLA Ops:
  0.6 0.0 copy-start.2
  0.6 0.0 copy-start.3
  0.7 0.0 copy-start.1
  1.5 2.5 %pack.1 = (bf16[2064,128]{1,0:T(8,128)(2,1)}, bf16[2048,128]{1,0:T(8,128)(2,1)}) custom-call(bf16[1,262144]{1,0:T(2,128)(2,1)} %own_hbm.1, bf16[1,262144]{1,0:T(2,128)(2,1)} %trial_hbm.1, s32[1]{0:T(128)S(6)} %copy.8.flag_ref), custom_call_target="tpu_custom_call" | custom-call | tf_op jit(solution)/shard_map/pack/pallas_call | solution.py:111
  4.0 3.1 %collective-permute-start = (bf16[2064,128]{1,0:T(8,128)(2,1)}, bf16[2064,128]{1,0:T(8,128)(2,1)S(1)}, u32[]{:S(2)}, u32[]{:S(2)}) collective-permute-start(bf16[2064,128]{1,0:T(8,128)(2,1)} %get-tuple-element.12.own_ref), channel_id=1, source_target_pairs={{0,1},{1,2},{2,3},{3,4},{4,5},{5,6},{6,7},{7,8},{8,9},{9,10},{10,1... | collective-permute-start | bytes 1585160 | tf_op jit(solution)/shard_map/ppermute | solution.py:376
  7.1 0.3 collective-permute-start.1
  7.4 16.5 %all-to-all-start = ((bf16[128,16,128]{2,1,0:T(8,128)(2,1)}), bf16[128,16,128]{2,1,0:T(8,128)(2,1)}, u32[]{:S(2)}, u32[]{:S(2)}) async-start(bf16[128,16,128]{2,1,0:T(8,128)(2,1)} %bitcast.6), calls=%async_computation | async-start | bytes 1048576 | tf_op jit(solution)/shard_map/all_to_all | solution.py:391
  23.9 0.0 copy-done.2
  23.9 0.0 copy-done.3
  23.9 0.0 copy-done.1
  23.9 0.0 copy-start
  23.9 1.0 %copy-done = bf16[2064,128]{1,0:T(8,128)(2,1)S(1)} copy-done((bf16[2064,128]{1,0:T(8,128)(2,1)S(1)}, bf16[2064,128]{1,0:T(8,128)(2,1)}, u32[]{:S(2)}) %copy-start) | copy-done | bytes 528408
  25.0 2.7 %own_term.1 = (bf16[4096,128]{1,0:T(8,128)(2,1)S(1)}, f32[2048,128]{1,0:T(8,128)S(1)}) custom-call(bf16[2064,128]{1,0:T(8,128)(2,1)S(1)} %copy-done, bf16[256,256]{1,0:T(8,128)(2,1)S(1)} %copy-done.2, bf16[256,256]{1,0:T(8,128)(2,1)S(1)} %copy-done.3, f32[64,64,128]{2,1,0:T(8,128)S(1)} %copy-done.1), custom_call_target="tpu_custom_call" | custom-call | flops 99999997952 | bytes 4194304 | tf_op jit(solution)/shard_map/own_term/pallas_call | solution.py:218
  27.6 0.0 collective-permute-done.prev_ref
  27.7 0.0 collective-permute-done.1.next_ref
  27.7 3.6 %exchange.1.exchange_ref = bf16[2048,128]{1,0:T(8,128)(2,1)} custom-call(bf16[2064,128]{1,0:T(8,128)(2,1)S(1)} %collective-permute-done.prev_ref, bf16[2064,128]{1,0:T(8,128)(2,1)S(1)} %collective-permute-done.1.next_ref, bf16[4096,128]{1,0:T(8,128)(2,1)S(1)} %get-tuple-element.13.owner_ref, f32[2048,128]{1,0:T(8,128)S(1)} %get-tuple-element.14.term_ref, ...), custom_call_target="tpu_custom_call" | custom-call | flops 99999997952 | bytes 4194304 | tf_op jit(solution)/shard_map/exchange/pallas_call | solution.py:268
  31.2 13.8 %all-to-all-done = bf16[128,16,128]{2,1,0:T(8,128)(2,1)} async-done(((bf16[128,16,128]{2,1,0:T(8,128)(2,1)}), bf16[128,16,128]{2,1,0:T(8,128)(2,1)}, u32[]{:S(2)}, u32[]{:S(2)}) %all-to-all-start) | async-done | bytes 524320 | tf_op jit(solution)/shard_map/all_to_all | solution.py:391
  45.0 5.5 %all-to-all-start.1 = ((bf16[128,16,128]{2,1,0:T(8,128)(2,1)}), bf16[128,16,128]{2,1,0:T(8,128)(2,1)S(1)}, u32[]{:S(2)}, u32[]{:S(2)}) async-start(bf16[128,16,128]{2,1,0:T(8,128)(2,1)} %bitcast.2), calls=%async_computation.1 | async-start | bytes 1048576 | tf_op jit(solution)/shard_map/all_to_all | solution.py:391
  50.5 3.5 %beside_slabs.1 = (bf16[2048,128]{1,0:T(8,128)(2,1)S(1)}, bf16[1,262144]{1,0:T(2,128)(2,1)}) custom-call(bf16[2048,128]{1,0:T(8,128)(2,1)} %bitcast.1.tiles_ref, bf16[2048,128]{1,0:T(8,128)(2,1)} %exchange.1.exchange_ref), custom_call_target="tpu_custom_call" | custom-call | tf_op jit(solution)/shard_map/beside_slabs/pallas_call | solution.py:309
  54.0 17.7 %all-to-all-done.1 = bf16[128,16,128]{2,1,0:T(8,128)(2,1)S(1)} async-done(((bf16[128,16,128]{2,1,0:T(8,128)(2,1)}), bf16[128,16,128]{2,1,0:T(8,128)(2,1)S(1)}, u32[]{:S(2)}, u32[]{:S(2)}) %all-to-all-start.1) | async-done | bytes 524320 | tf_op jit(solution)/shard_map/all_to_all | solution.py:391
  71.7 0.6 intersection.1
  72.4 0.1 collective-permute-start.2
  72.5 1.2 %collective-permute-done.2 = f32[64,128]{1,0:T(8,128)S(1)} collective-permute-done((f32[64,128]{1,0:T(8,128)S(1)}, f32[64,128]{1,0:T(8,128)S(1)}, u32[]{:S(2)}, u32[]{:S(2)}) %collective-permute-start.2) | collective-permute-done | bytes 32800 | tf_op jit(solution)/shard_map/ppermute | solution.py:380
  73.7 9.4 %all_to_all.20 = bf16[8,64,128]{2,1,0:T(8,128)(2,1)S(1)} all-to-all(bf16[8,64,128]{2,1,0:T(8,128)(2,1)S(1)} %broadcast_in_dim.4), channel_id=1, replica_groups=mesh['spin'=2,'y'=4,'x'=2,'z'=8,'core'=2] {'y','x'}, dimensions={0} | all-to-all | bytes 262144 | tf_op jit(solution)/shard_map/all_to_all | solution.py:386
  83.2 10.3 %all_to_all.21 = bf16[8,64,128]{2,1,0:T(8,128)(2,1)S(1)} all-to-all(bf16[8,64,128]{2,1,0:T(8,128)(2,1)S(1)} %broadcast_in_dim.5), channel_id=1, replica_groups=mesh['spin'=2,'y'=4,'x'=2,'z'=8,'core'=2] {'z'}, dimensions={0} | all-to-all | bytes 262144 | tf_op jit(solution)/shard_map/all_to_all | solution.py:386
  93.5 3.0 %collective-permute-start.3 = (bf16[64,128]{1,0:T(8,128)(2,1)S(1)}, bf16[64,128]{1,0:T(8,128)(2,1)S(1)}, u32[]{:S(2)}, u32[]{:S(2)}) collective-permute-start(bf16[64,128]{1,0:T(8,128)(2,1)S(1)} %reduce_sum.25.mine_ref), channel_id=1, source_target_pairs={{0,1},{1,0},{2,3},{3,2},{4,5},{5,4},{6,7},{7,6},{8,9},{9,8},{10,11... | collective-permute-start | bytes 49160 | tf_op jit(solution)/shard_map/ppermute | solution.py:380
  96.5 0.8 collective-permute-done.3.other_ref
  97.3 1.1 %projected.1 = bf16[128,2048]{1,0:T(8,128)(2,1)} custom-call(bf16[2048,128]{1,0:T(8,128)(2,1)S(1)} %get-tuple-element.17.lines_ref, bf16[64,128]{1,0:T(8,128)(2,1)S(1)} %reduce_sum.25.mine_ref, bf16[64,128]{1,0:T(8,128)(2,1)S(1)} %collective-permute-done.3.other_ref, s32[1]{0:T(128)} %bitcast.4.core_ref), custom_call_target="tpu_custom_call" | custom-call | tf_op jit(solution)/shard_map/projected/pallas_call | solution.py:364
  (5 shorter events, 0.1 us)
Async XLA Ops:
  0.6 23.3 %copy-start.2 = (bf16[256,256]{1,0:T(8,128)(2,1)S(1)}, bf16[256,256]{1,0:T(8,128)(2,1)}, u32[]{:S(2)}) copy-start(bf16[256,256]{1,0:T(8,128)(2,1)} %constant.14.clone.table_ref) | copy-start | bytes 393220
  0.6 23.3 %copy-start.3 = (bf16[256,256]{1,0:T(8,128)(2,1)S(1)}, bf16[256,256]{1,0:T(8,128)(2,1)}, u32[]{:S(2)}) copy-start(bf16[256,256]{1,0:T(8,128)(2,1)} %constant.15.clone.mixed_ref) | copy-start | bytes 393220
  0.7 23.3 %copy-start.1 = (f32[64,64,128]{2,1,0:T(8,128)S(1)}, f32[64,64,128]{2,1,0:T(8,128)}, u32[]{:S(2)}) copy-start(f32[64,64,128]{2,1,0:T(8,128)} %constant.16.clone.kernel_ref) | copy-start | bytes 6291460
  4.0 23.7 %collective-permute-start = (bf16[2064,128]{1,0:T(8,128)(2,1)}, bf16[2064,128]{1,0:T(8,128)(2,1)S(1)}, u32[]{:S(2)}, u32[]{:S(2)}) collective-permute-start(bf16[2064,128]{1,0:T(8,128)(2,1)} %get-tuple-element.12.own_ref), channel_id=1, source_target_pairs={{0,1},{1,2},{2,3},{3,4},{4,5},{5,6},{6,7},{7,8},{8,9},{9,10},{10,1... | collective-permute-start | bytes 1585160 | tf_op jit(solution)/shard_map/ppermute | solution.py:376
  7.1 20.6 %collective-permute-start.1 = (bf16[2064,128]{1,0:T(8,128)(2,1)}, bf16[2064,128]{1,0:T(8,128)(2,1)S(1)}, u32[]{:S(2)}, u32[]{:S(2)}) collective-permute-start(bf16[2064,128]{1,0:T(8,128)(2,1)} %get-tuple-element.12.own_ref), channel_id=1, source_target_pairs={{0,127},{1,0},{2,1},{3,2},{4,3},{5,4},{6,5},{7,6},{8,7},{9,8},{10,... | collective-permute-start | bytes 1585160 | tf_op jit(solution)/shard_map/ppermute | solution.py:376
  7.4 37.6 %all-to-all-start = ((bf16[128,16,128]{2,1,0:T(8,128)(2,1)}), bf16[128,16,128]{2,1,0:T(8,128)(2,1)}, u32[]{:S(2)}, u32[]{:S(2)}) async-start(bf16[128,16,128]{2,1,0:T(8,128)(2,1)} %bitcast.6), calls=%async_computation | async-start | bytes 1048576 | tf_op jit(solution)/shard_map/all_to_all | solution.py:391
  23.9 1.0 %copy-start = (bf16[2064,128]{1,0:T(8,128)(2,1)S(1)}, bf16[2064,128]{1,0:T(8,128)(2,1)}, u32[]{:S(2)}) copy-start(bf16[2064,128]{1,0:T(8,128)(2,1)} %get-tuple-element.12.own_ref) | copy-start | bytes 1585156
  45.0 26.7 %all-to-all-start.1 = ((bf16[128,16,128]{2,1,0:T(8,128)(2,1)}), bf16[128,16,128]{2,1,0:T(8,128)(2,1)S(1)}, u32[]{:S(2)}, u32[]{:S(2)}) async-start(bf16[128,16,128]{2,1,0:T(8,128)(2,1)} %bitcast.2), calls=%async_computation.1 | async-start | bytes 1048576 | tf_op jit(solution)/shard_map/all_to_all | solution.py:391
  72.4 1.3 %collective-permute-start.2 = (f32[64,128]{1,0:T(8,128)S(1)}, f32[64,128]{1,0:T(8,128)S(1)}, u32[]{:S(2)}, u32[]{:S(2)}) collective-permute-start(f32[64,128]{1,0:T(8,128)S(1)} %get-tuple-element.19), channel_id=1, source_target_pairs={{0,1},{1,0},{2,3},{3,2},{4,5},{5,4},{6,7},{7,6},{8,9},{9,8},{10,11... | collective-permute-start | bytes 98312 | tf_op jit(solution)/shard_map/ppermute | solution.py:380
  93.5 3.8 %collective-permute-start.3 = (bf16[64,128]{1,0:T(8,128)(2,1)S(1)}, bf16[64,128]{1,0:T(8,128)(2,1)S(1)}, u32[]{:S(2)}, u32[]{:S(2)}) collective-permute-start(bf16[64,128]{1,0:T(8,128)(2,1)S(1)} %reduce_sum.25.mine_ref), channel_id=1, source_target_pairs={{0,1},{1,0},{2,3},{3,2},{4,5},{5,4},{6,7},{7,6},{8,9},{9,8},{10,11... | collective-permute-start | bytes 49160 | tf_op jit(solution)/shard_map/ppermute | solution.py:380

commit v4 on v2

--- a/solution.py
+++ b/solution.py
@@ -21,7 +21,8 @@
 STEP = 4
 SPAN = 2 * STEP
 PITCH = 72
-OWN_FLOPS = 10**10
+WIDE = 40
+NEAR_FLOPS = 10**10
 VMEM = pl.BlockSpec(memory_space=pltpu.VMEM)
 SMEM = pl.BlockSpec(memory_space=pltpu.SMEM)
 
@@ -171,69 +172,79 @@
     return lax.broadcasted_iota(jnp.int32, (height, 128), 1) < 64
 
 
-def own_body(own_ref, table_ref, mixed_ref, kernel_ref, owner_ref, term_ref, grid):
+def near_body(
+    own_ref, near_ref, table_ref, mixed_ref, kernel_ref, owner_ref, term_ref, visitors, grid
+):
     f32, bf16 = jnp.float32, jnp.bfloat16
     low = low_lanes(NG // 2)
 
     def density_of(plane):
-        mine = both_halves(own_ref[plane_rows(plane, 32), :].astype(f32), low)
-        owner_ref[plane_rows(plane, 64), :] = mine.astype(bf16)
-        return (mine * mine).astype(bf16)
+        own, near = (ref[plane_rows(plane, 32), :].astype(f32) for ref in (own_ref, near_ref))
+        own_turned, near_turned = (pltpu.roll(value, 64, 1) for value in (own, near))
+        mine = jnp.concatenate(
+            [jnp.where(low, own, own_turned), jnp.where(low, own_turned, own)], axis=0
+        )
+        pairs = jnp.concatenate(
+            [jnp.where(low, own, near_turned), jnp.where(low, own_turned, near)], axis=0
+        )
+        wide = plane_rows(plane, 64)
+        owner_ref[wide, :] = mine.astype(bf16)
+        visitors[wide, :] = pairs.astype(bf16)
+        return (mine * pairs).astype(bf16)
 
     potentials = passes_there(density_of, table_ref, mixed_ref, kernel_ref, grid)
-    fill = fill_of(own_ref)
+    fill = jnp.where(low_lanes(NG), fill_of(own_ref), fill_of(near_ref))
 
     def backward(step, carry):
         for plane, potential in potentials(step):
-            total = potential * (owner_ref[plane_rows(plane, 64), :].astype(f32) * fill)
+            total = potential * (visitors[plane_rows(plane, 64), :].astype(f32) * fill)
+            total = total + pltpu.roll(total, 64, 1)
             term_ref[plane_rows(plane, 32), :] = jnp.where(low, total[:32], total[32:])
         return carry
 
     lax.fori_loop(0, NG // SPAN, backward, 0, unroll=True)
 
 
-def own_term(own, table, mixed, kernel):
-    return pl.pallas_call(
-        own_body,
+def near_term(own, near, table, mixed, kernel):
+    return pl.pallas_call(
+        near_body,
         out_shape=(
             jax.ShapeDtypeStruct((NG * NG, 128), jnp.bfloat16),
             jax.ShapeDtypeStruct((ROWS, 128), jnp.float32),
         ),
-        in_specs=[VMEM] * 4,
+        in_specs=[VMEM] * 5,
         out_specs=(VMEM, VMEM),
-        scratch_shapes=[pltpu.VMEM((NG * PITCH, 128), jnp.float32)],
+        scratch_shapes=[
+            pltpu.VMEM((NG * NG, 128), jnp.bfloat16),
+            pltpu.VMEM((NG * PITCH, 128), jnp.float32),
+        ],
         compiler_params=pltpu.CompilerParams(vmem_limit_bytes=24 * 1024 * 1024),
         cost_estimate=pl.CostEstimate(
-            flops=OWN_FLOPS, bytes_accessed=4 * 1024 * 1024, transcendentals=0
+            flops=NEAR_FLOPS, bytes_accessed=4 * 1024 * 1024, transcendentals=0
         ),
-        name="own_term",
-    )(own, table, mixed, kernel)
+        name="near_term",
+    )(own, near, table, mixed, kernel)
 
 
 def exchange_body(
-    prev_ref, next_ref, owner_ref, term_ref, trial_ref, table_ref, mixed_ref, kernel_ref,
+    far_ref, owner_ref, term_ref, trial_ref, table_ref, mixed_ref, kernel_ref,
     out_ref, visitors, grid,
 ):
     f32, bf16 = jnp.float32, jnp.bfloat16
     low = low_lanes(NG // 2)
 
     def density_of(plane):
-        before, after = (ref[plane_rows(plane, 32), :].astype(f32) for ref in (prev_ref, next_ref))
-        before_turned, after_turned = (pltpu.roll(value, 64, 1) for value in (before, after))
-        pairs = jnp.concatenate(
-            [jnp.where(low, before, after_turned), jnp.where(low, before_turned, after)], axis=0
-        )
+        far = both_halves(far_ref[plane_rows(plane, 32), :].astype(f32), low)
         wide = plane_rows(plane, 64)
-        visitors[wide, :] = pairs.astype(bf16)
-        return (pairs * owner_ref[wide, :].astype(f32)).astype(bf16)
+        visitors[wide, :] = far.astype(bf16)
+        return (far * owner_ref[wide, :].astype(f32)).astype(bf16)
 
     potentials = passes_there(density_of, table_ref, mixed_ref, kernel_ref, grid)
-    fill = jnp.where(low_lanes(NG), fill_of(prev_ref), fill_of(next_ref))
+    fill = fill_of(far_ref)
 
     def backward(step, carry):
         for plane, potential in potentials(step):
             total = potential * (visitors[plane_rows(plane, 64), :].astype(f32) * fill)
-            total = total + pltpu.roll(total, 64, 1)
             rows = plane_rows(plane, 32)
             value = (jnp.where(low, total[:32], total[32:]) + term_ref[rows, :]).astype(bf16)
             trial = trial_ref[rows, :]
@@ -245,11 +256,11 @@
     lax.fori_loop(0, NG // SPAN, backward, 0, unroll=True)
 
 
-def exchange_of(before, after, owner, term, trial, table, mixed, kernel):
+def exchange_of(far, owner, term, trial, table, mixed, kernel):
     return pl.pallas_call(
         exchange_body,
         out_shape=jax.ShapeDtypeStruct((2 * ROWS, 128), jnp.bfloat16),
-        in_specs=[VMEM] * 8,
+        in_specs=[VMEM] * 7,
         out_specs=VMEM,
         scratch_shapes=[
             pltpu.VMEM((NG * NG, 128), jnp.bfloat16),
@@ -257,7 +268,7 @@
         ],
         compiler_params=pltpu.CompilerParams(vmem_limit_bytes=24 * 1024 * 1024),
         name="exchange",
-    )(before, after, owner, term, trial, table, mixed, kernel)
+    )(far, owner, term, trial, table, mixed, kernel)
 
 
 def unpack_body(tiles_ref, flat_ref, token_ref):
@@ -286,104 +297,92 @@
     )(tiles)
 
 
-def intersection_body(tiles_ref, token_ref, lines_ref, copies_ref, wide):
+def intersection_body(tiles_ref, token_ref, core_ref, lines_ref, mine_ref, other_ref, wide):
     bf16 = jnp.bfloat16
-    wide[...] = tiles_ref[...].astype(jnp.float32)
+    for peer in range(128):
+        wide[pl.ds(peer * WIDE, 32), :] = tiles_ref[pl.ds(peer * 32, 32), :].astype(jnp.float32)
     total = jnp.zeros((128, 128), jnp.float32)
     for line in range(16):
-        trial = wide[pl.ds(line, 128, stride=32), :].astype(bf16)
-        value = wide[pl.ds(line + 16, 128, stride=32), :].astype(bf16)
+        trial = wide[pl.ds(line, 128, stride=WIDE), :].astype(bf16)
+        value = wide[pl.ds(line + 16, 128, stride=WIDE), :].astype(bf16)
         lines_ref[pl.ds(line * 128, 128), :] = value
         total = total + lax.dot_general(
             trial, value, (((1,), (1,)), ((), ())), preferred_element_type=jnp.float32
         )
-    total = (total * (1.0 / math.sqrt(G))).astype(bf16)
-    for peer in range(8):
-        copies_ref[pl.ds(peer * 128, 128), :] = total
-
-
-def intersection_of(tiles, token):
+    total = total * (1.0 / math.sqrt(G))
+    first = core_ref[0] == 0
+    mine_ref[...] = jnp.where(first, total[:64], total[64:])
+    other_ref[...] = jnp.where(first, total[64:], total[:64])
+
+
+def intersection_of(tiles, token, core):
+    half = jax.ShapeDtypeStruct((64, 128), jnp.float32)
     return pl.pallas_call(
         intersection_body,
-        out_shape=(
-            jax.ShapeDtypeStruct((ROWS, 128), jnp.bfloat16),
-            jax.ShapeDtypeStruct((8 * 128, 128), jnp.bfloat16),
-        ),
-        in_specs=[VMEM, pl.BlockSpec(memory_space=pl.ANY)],
-        out_specs=(VMEM, VMEM),
-        scratch_shapes=[pltpu.VMEM((2 * ROWS, 128), jnp.float32)],
+        out_shape=(jax.ShapeDtypeStruct((ROWS, 128), jnp.bfloat16), half, half),
+        in_specs=[VMEM, pl.BlockSpec(memory_space=pl.ANY), SMEM],
+        out_specs=(VMEM, VMEM, VMEM),
+        scratch_shapes=[pltpu.VMEM((128 * WIDE, 128), jnp.float32)],
         compiler_params=pltpu.CompilerParams(vmem_limit_bytes=16 * 1024 * 1024),
         name="intersection",
-    )(tiles, token)
-
-
-def summed_copies_body(tiles_ref, copies_ref):
-    total = tiles_ref[0].astype(jnp.float32)
-    for peer in range(1, 16):
-        total = total + tiles_ref[peer].astype(jnp.float32)
-    total = total.astype(jnp.bfloat16)
-    for peer in range(16):
-        copies_ref[peer] = total
-
-
-def summed_copies(tiles):
-    return pl.pallas_call(
-        summed_copies_body,
-        out_shape=jax.ShapeDtypeStruct((16, 64, 128), jnp.bfloat16),
-        in_specs=[VMEM],
-        out_specs=VMEM,
-        compiler_params=pltpu.CompilerParams(vmem_limit_bytes=16 * 1024 * 1024),
-        name="summed_copies",
-    )(tiles)
-
-
-def projected_body(lines_ref, tiles_ref, out_ref):
-    halves = []
-    for core in range(2):
-        total = tiles_ref[core].astype(jnp.float32)
-        for peer in range(1, 8):
-            total = total + tiles_ref[2 * peer + core].astype(jnp.float32)
-        halves.append(total)
-    table = jnp.concatenate(halves, axis=0).astype(jnp.bfloat16)
+    )(tiles, token, core)
+
+
+def projected_body(lines_ref, mine_ref, other_ref, core_ref, out_ref):
+    first = core_ref[0] == 0
+    mine, other = mine_ref[...].astype(jnp.float32), other_ref[...].astype(jnp.float32)
+    table = jnp.concatenate(
+        [jnp.where(first, mine, other), jnp.where(first, other, mine)], axis=0
+    ).astype(jnp.bfloat16)
     for line in range(16):
         rows = pl.ds(line * 128, 128)
         value = dot(table, lines_ref[rows, :]) * (-1.0 / math.sqrt(128))
         out_ref[:, rows] = value.astype(jnp.bfloat16)
 
 
-def projected_of(lines, tiles):
+def projected_of(lines, mine, other, core):
     return pl.pallas_call(
         projected_body,
         out_shape=jax.ShapeDtypeStruct((128, ROWS), jnp.bfloat16),
-        in_specs=[VMEM, VMEM],
+        in_specs=[VMEM, VMEM, VMEM, SMEM],
         out_specs=VMEM,
         compiler_params=pltpu.CompilerParams(vmem_limit_bytes=16 * 1024 * 1024),
         name="projected",
-    )(lines, tiles)
-
-
-def passed_along(value, steps):
+    )(lines, mine, other, core)
+
+
+def from_far(value):
     count = lax.axis_size(BAND)
-    return lax.ppermute(value, BAND, [(i, (i + steps) % count) for i in range(count)])
-
-
-def sent_around(tiles, axes):
-    return lax.all_to_all(tiles, axes, 0, 0, tiled=True)
+    pairs = [(i, (i - 1 if i % 2 == 0 else i + 1) % count) for i in range(count)]
+    return lax.ppermute(value, BAND, pairs)
+
+
+def swapped(value):
+    return lax.ppermute(value, "core", [(0, 1), (1, 0)])
+
+
+def summed_over(value, axes):
+    peers = lax.axis_size(axes)
+    copies = jnp.broadcast_to(value[None], (peers,) + value.shape)
+    tiles = lax.all_to_all(copies, axes, 0, 0, tiled=True)
+    return jnp.sum(tiles.astype(jnp.float32), axis=0).astype(jnp.bfloat16)
 
 
 def local(orbitals, trial, occupations):
     tables = [jnp.asarray(value) for value in constants()]
     own = packed_with_flag(orbitals, occupations)
-    before, after = passed_along(own, 1), passed_along(own, -1)
+    far, near = from_far(own), swapped(own)
     trial_rows = packed_after(trial, own)
-    owner, term = own_term(own, *tables)
-    both = exchange_of(before, after, owner, term, trial_rows, *tables)
-    tiles = sent_around(both.reshape(128, 32, 128), BAND).reshape(2 * ROWS, 128)
+    owner, term = near_term(own, near, *tables)
+    both = exchange_of(far, owner, term, trial_rows, *tables)
+    tiles = lax.all_to_all(both.reshape(128, 32, 128), BAND, 0, 0, tiled=True)
     flat, token = unpacked(both)
-    lines, copies = intersection_of(tiles, token)
-    parts = sent_around(copies.reshape(16, 64, 128), ("y", "x", "core"))
-    parts = sent_around(summed_copies(parts), ("z", "core"))
-    return flat, projected_of(lines, parts)
+    core = lax.axis_index("core").astype(jnp.int32).reshape(1)
+    lines, mine, other = intersection_of(tiles.reshape(2 * ROWS, 128), token, core)
+    half = (mine + swapped(other)).astype(jnp.bfloat16)
+    half = summed_over(half, ("y", "x"))
+    half = summed_over(half, "z")
+    return flat, projected_of(lines, half, swapped(half), core)
 
 
 def solution(mesh):

time: 101 us -> 95.8 us (0.949)
  blocking collectives: 27.7 us -> 20.6 us
  starting transfers between devices: 21.5 us -> 23.9 us
    all_to_all x2, blocking collectives: 27.7 us -> 20.6 us  [summed_over(): tiles = lax.all_to_all(copies, axes, 0, 0, tiled=True)]
    ppermute x2 -> x4, starting transfers between devices: 3.32 us -> 6.43 us  [the longest x3 6.43 us: swapped(): return lax.ppermute(value, 'core', [(0, 1), (1, 0)])]
    ppermute x2 -> x4, waiting for transfers between devices: 4.9 us -> 5.75 us  [the longest x1 3.54 us: from_far(): return lax.ppermute(value, BAND, pairs)]
    pallas_call x2 -> x1, Pallas kernels: 2.82 us -> 2.9 us  [near_term(): pl.pallas_call(near_body, out_shape=(jax.ShapeDtypeStruct((NG * NG, 128),...]
  transfers between devices with their start and end apart: 3 -> 5, of which waited for: 3 -> 5; matrix products, arithmetic and copies ran while one was open for 0% -> 0% of each run, Pallas kernels for 6% -> 6%
where the time goes in v4:
time: 95.8 us; the launch traced here: 95.4 us
  waiting for transfers between devices  34.4 us (36%)
  starting transfers between devices  23.9 us (25%)
  blocking collectives  20.6 us (22%)
  Pallas kernels  11.7 us (12%)
  local copies, waits for them, and re-layouts  3.14 us (3%)
  between operations  1.51 us (2%)
    all_to_all x1, waiting for transfers between devices, local(): tiles = lax.all_to_all(both.reshape(128, 32, 128), BAND, 0, 0, tiled=True)  28.6 us
    all_to_all x2, blocking collectives, summed_over(): tiles = lax.all_to_all(copies, axes, 0, 0, tiled=True)  20.6 us
    all_to_all x1, starting transfers between devices, local(): tiles = lax.all_to_all(both.reshape(128, 32, 128), BAND, 0, 0, tiled=True)  17.5 us
    ppermute x3, starting transfers between devices, swapped(): return lax.ppermute(value, 'core', [(0, 1), (1, 0)])  6.43 us
    pallas_call x1, Pallas kernels, exchange_of(): pl.pallas_call(exchange_body, out_shape=jax.ShapeDtypeStruct((2 * ROWS, 1...  3.78 us
    ppermute x1, waiting for transfers between devices, from_far(): return lax.ppermute(value, BAND, pairs)  3.54 us
    pallas_call x1, Pallas kernels, unpacked(): pl.pallas_call(unpack_body, out_shape=(jax.ShapeDtypeStruct((1, G), jnp.b...  3.15 us
    unnamed x10, local copies, waits for them, and re-layouts  3.1 us
  transfers between devices with their start and end apart: 5, of which 5 were waited for; matrix products, arithmetic and copies ran while one was open for 0% of the time, Pallas kernels for 6%

profile of v4, /device:TPU:1, one launch (start us, length us, event | category | flops | bytes accessed | tf_op | source)
XLA Modules:
  0.0 95.4 jit_solution(243266978462801839)
XLA Ops:
  0.6 0.0 copy-start
  1.4 0.0 copy-start.1
  1.4 1.2 %copy-done.1 = bf16[1,262144]{1,0:T(2,128)(2,1)S(1)} copy-done((bf16[1,262144]{1,0:T(2,128)(2,1)S(1)}, bf16[1,262144]{1,0:T(2,128)(2,1)}, u32[]{:S(2)}) %copy-start.1) | copy-done | bytes 524312
  2.7 0.1 pack_flagged.1.own_ref.earlier_ref
  2.8 3.3 %collective-permute-start.1 = (bf16[2064,128]{1,0:T(8,128)(2,1)S(1)}, bf16[2064,128]{1,0:T(8,128)(2,1)S(1)}, u32[]{:S(2)}, u32[]{:S(2)}) collective-permute-start(bf16[2064,128]{1,0:T(8,128)(2,1)S(1)} %pack_flagged.1.own_ref.earlier_ref), channel_id=1, source_target_pairs={{0,1},{1,0},{2,3},{3,2},{4,5},{5,4},{6,7},{7,6},{8,9},{9,8},{10,11... | collective-permute-start | bytes 1585160 | tf_op jit(solution)/shard_map/ppermute | solution.py:361
  6.1 0.0 collective-permute-start
  6.1 0.0 copy-start.2
  6.1 1.2 %copy-done.2 = bf16[1,262144]{1,0:T(2,128)(2,1)S(1)} copy-done((bf16[1,262144]{1,0:T(2,128)(2,1)S(1)}, bf16[1,262144]{1,0:T(2,128)(2,1)}, u32[]{:S(2)}) %copy-start.2) | copy-done | bytes 524312
  7.4 0.0 copy-start.3
  7.4 0.0 copy-start.4
  7.4 0.1 pack.1.trial_ref
  7.5 0.2 collective-permute-done.1.near_ref
  7.7 0.0 copy-done
  7.7 0.6 copy-done.3
  8.3 0.1 copy-done.4
  8.3 2.9 %near_term.1 = (bf16[4096,128]{1,0:T(8,128)(2,1)S(1)}, f32[2048,128]{1,0:T(8,128)S(1)}) custom-call(bf16[2064,128]{1,0:T(8,128)(2,1)S(1)} %pack_flagged.1.own_ref.earlier_ref, bf16[2064,128]{1,0:T(8,128)(2,1)S(1)} %collective-permute-done.1.near_ref, bf16[256,256]{1,0:T(8,128)(2,1)S(1)} %copy-done.3, bf16[256,256]{1,0:T(8,128)(2,1)S(1)} %copy-done.4, ...), custom_call_target="tpu_custom_call" | custom-call | flops 10000000000 | bytes 4194304 | tf_op jit(solution)/shard_map/near_term/pallas_call | solution.py:209
  11.2 3.5 %collective-permute-done.far_ref = bf16[2064,128]{1,0:T(8,128)(2,1)S(1)} collective-permute-done((bf16[2064,128]{1,0:T(8,128)(2,1)S(1)}, bf16[2064,128]{1,0:T(8,128)(2,1)S(1)}, u32[]{:S(2)}, u32[]{:S(2)}) %collective-permute-start) | collective-permute-done | bytes 528416 | tf_op jit(solution)/shard_map/ppermute | solution.py:357
  14.8 3.8 %exchange.1.tiles_ref = bf16[4096,128]{1,0:T(8,128)(2,1)} custom-call(bf16[2064,128]{1,0:T(8,128)(2,1)S(1)} %collective-permute-done.far_ref, bf16[4096,128]{1,0:T(8,128)(2,1)S(1)} %get-tuple-element.9.owner_ref, f32[2048,128]{1,0:T(8,128)S(1)} %get-tuple-element.10.term_ref, bf16[2048,128]{1,0:T(8,128)(2,1)S(1)} %pack.1.trial_ref, ...), custom_call_target="tpu_custom_call" | custom-call | tf_op jit(solution)/shard_map/exchange/pallas_call | solution.py:260
  18.6 17.5 %all-to-all-start = ((bf16[128,32,128]{2,1,0:T(8,128)(2,1)}), bf16[128,32,128]{2,1,0:T(8,128)(2,1)S(1)}, u32[]{:S(2)}, u32[]{:S(2)}) async-start(bf16[128,32,128]{2,1,0:T(8,128)(2,1)} %bitcast), calls=%async_computation | async-start | bytes 2097152 | tf_op jit(solution)/shard_map/all_to_all | solution.py:378
  36.1 3.1 %unpack.1 = (bf16[1,262144]{1,0:T(2,128)(2,1)}, bf16[16,128]{1,0:T(8,128)(2,1)S(1)}) custom-call(bf16[4096,128]{1,0:T(8,128)(2,1)} %exchange.1.tiles_ref), custom_call_target="tpu_custom_call" | custom-call | tf_op jit(solution)/shard_map/unpack/pallas_call | solution.py:287
  39.2 28.6 %all-to-all-done = bf16[128,32,128]{2,1,0:T(8,128)(2,1)S(1)} async-done(((bf16[128,32,128]{2,1,0:T(8,128)(2,1)}), bf16[128,32,128]{2,1,0:T(8,128)(2,1)S(1)}, u32[]{:S(2)}, u32[]{:S(2)}) %all-to-all-start) | async-done | bytes 1048608 | tf_op jit(solution)/shard_map/all_to_all | solution.py:378
  67.9 0.6 intersection.1
  68.4 0.1 collective-permute-start.2
  68.5 1.2 %collective-permute-done.2 = f32[64,128]{1,0:T(8,128)S(1)} collective-permute-done((f32[64,128]{1,0:T(8,128)S(1)}, f32[64,128]{1,0:T(8,128)S(1)}, u32[]{:S(2)}, u32[]{:S(2)}) %collective-permute-start.2) | collective-permute-done | bytes 32800 | tf_op jit(solution)/shard_map/ppermute | solution.py:361
  69.8 10.0 %all_to_all.15 = bf16[8,64,128]{2,1,0:T(8,128)(2,1)S(1)} all-to-all(bf16[8,64,128]{2,1,0:T(8,128)(2,1)S(1)} %broadcast_in_dim.4), channel_id=1, replica_groups=mesh['spin'=2,'y'=4,'x'=2,'z'=8,'core'=2] {'y','x'}, dimensions={0} | all-to-all | bytes 262144 | tf_op jit(solution)/shard_map/all_to_all | solution.py:367
  79.9 10.6 %all_to_all.16 = bf16[8,64,128]{2,1,0:T(8,128)(2,1)S(1)} all-to-all(bf16[8,64,128]{2,1,0:T(8,128)(2,1)S(1)} %broadcast_in_dim.5), channel_id=1, replica_groups=mesh['spin'=2,'y'=4,'x'=2,'z'=8,'core'=2] {'z'}, dimensions={0} | all-to-all | bytes 262144 | tf_op jit(solution)/shard_map/all_to_all | solution.py:367
  90.5 3.0 %collective-permute-start.3 = (bf16[64,128]{1,0:T(8,128)(2,1)S(1)}, bf16[64,128]{1,0:T(8,128)(2,1)S(1)}, u32[]{:S(2)}, u32[]{:S(2)}) collective-permute-start(bf16[64,128]{1,0:T(8,128)(2,1)S(1)} %reduce_sum.25.mine_ref), channel_id=1, source_target_pairs={{0,1},{1,0},{2,3},{3,2},{4,5},{5,4},{6,7},{7,6},{8,9},{9,8},{10,11... | collective-permute-start | bytes 49160 | tf_op jit(solution)/shard_map/ppermute | solution.py:361
  93.5 0.8 collective-permute-done.3.other_ref
  94.3 1.1 %projected.1 = bf16[128,2048]{1,0:T(8,128)(2,1)} custom-call(bf16[2048,128]{1,0:T(8,128)(2,1)S(1)} %get-tuple-element.13.lines_ref, bf16[64,128]{1,0:T(8,128)(2,1)S(1)} %reduce_sum.25.mine_ref, bf16[64,128]{1,0:T(8,128)(2,1)S(1)} %collective-permute-done.3.other_ref, s32[1]{0:T(128)} %bitcast.2.core_ref), custom_call_target="tpu_custom_call" | custom-call | tf_op jit(solution)/shard_map/projected/pallas_call | solution.py:344
  (5 shorter events, 0.1 us)
Async XLA Ops:
  0.6 7.0 %copy-start = (f32[64,64,128]{2,1,0:T(8,128)S(1)}, f32[64,64,128]{2,1,0:T(8,128)}, u32[]{:S(2)}) copy-start(f32[64,64,128]{2,1,0:T(8,128)} %constant.16.clone.kernel_ref) | copy-start | bytes 6291460
  1.4 1.2 %copy-start.1 = (bf16[1,262144]{1,0:T(2,128)(2,1)S(1)}, bf16[1,262144]{1,0:T(2,128)(2,1)}, u32[]{:S(2)}) copy-start(bf16[1,262144]{1,0:T(2,128)(2,1)} %flat_ref.2) | copy-start | bytes 1572868
  2.8 4.9 %collective-permute-start.1 = (bf16[2064,128]{1,0:T(8,128)(2,1)S(1)}, bf16[2064,128]{1,0:T(8,128)(2,1)S(1)}, u32[]{:S(2)}, u32[]{:S(2)}) collective-permute-start(bf16[2064,128]{1,0:T(8,128)(2,1)S(1)} %pack_flagged.1.own_ref.earlier_ref), channel_id=1, source_target_pairs={{0,1},{1,0},{2,3},{3,2},{4,5},{5,4},{6,7},{7,6},{8,9},{9,8},{10,11... | collective-permute-start | bytes 1585160 | tf_op jit(solution)/shard_map/ppermute | solution.py:361
  6.1 8.7 %collective-permute-start = (bf16[2064,128]{1,0:T(8,128)(2,1)S(1)}, bf16[2064,128]{1,0:T(8,128)(2,1)S(1)}, u32[]{:S(2)}, u32[]{:S(2)}) collective-permute-start(bf16[2064,128]{1,0:T(8,128)(2,1)S(1)} %pack_flagged.1.own_ref.earlier_ref), channel_id=1, source_target_pairs={{0,127},{1,2},{2,1},{3,4},{4,3},{5,6},{6,5},{7,8},{8,7},{9,10},{10... | collective-permute-start | bytes 1585160 | tf_op jit(solution)/shard_map/ppermute | solution.py:357
  6.1 1.2 %copy-start.2 = (bf16[1,262144]{1,0:T(2,128)(2,1)S(1)}, bf16[1,262144]{1,0:T(2,128)(2,1)}, u32[]{:S(2)}) copy-start(bf16[1,262144]{1,0:T(2,128)(2,1)} %flat_ref.3) | copy-start | bytes 1572868
  7.4 0.9 copy-start.3
  7.4 1.0 %copy-start.4 = (bf16[256,256]{1,0:T(8,128)(2,1)S(1)}, bf16[256,256]{1,0:T(8,128)(2,1)}, u32[]{:S(2)}) copy-start(bf16[256,256]{1,0:T(8,128)(2,1)} %constant.15.clone.mixed_ref) | copy-start | bytes 393220
  18.6 49.3 %all-to-all-start = ((bf16[128,32,128]{2,1,0:T(8,128)(2,1)}), bf16[128,32,128]{2,1,0:T(8,128)(2,1)S(1)}, u32[]{:S(2)}, u32[]{:S(2)}) async-start(bf16[128,32,128]{2,1,0:T(8,128)(2,1)} %bitcast), calls=%async_computation | async-start | bytes 2097152 | tf_op jit(solution)/shard_map/all_to_all | solution.py:378
  68.4 1.3 %collective-permute-start.2 = (f32[64,128]{1,0:T(8,128)S(1)}, f32[64,128]{1,0:T(8,128)S(1)}, u32[]{:S(2)}, u32[]{:S(2)}) collective-permute-start(f32[64,128]{1,0:T(8,128)S(1)} %get-tuple-element.15), channel_id=1, source_target_pairs={{0,1},{1,0},{2,3},{3,2},{4,5},{5,4},{6,7},{7,6},{8,9},{9,8},{10,11... | collective-permute-start | bytes 98312 | tf_op jit(solution)/shard_map/ppermute | solution.py:361
  90.5 3.8 %collective-permute-start.3 = (bf16[64,128]{1,0:T(8,128)(2,1)S(1)}, bf16[64,128]{1,0:T(8,128)(2,1)S(1)}, u32[]{:S(2)}, u32[]{:S(2)}) collective-permute-start(bf16[64,128]{1,0:T(8,128)(2,1)S(1)} %reduce_sum.25.mine_ref), channel_id=1, source_target_pairs={{0,1},{1,0},{2,3},{3,2},{4,5},{5,4},{6,7},{7,6},{8,9},{9,8},{10,11... | collective-permute-start | bytes 49160 | tf_op jit(solution)/shard_map/ppermute | solution.py:361

commit v5 on v4

--- a/solution.py
+++ b/solution.py
@@ -33,18 +33,43 @@
     return (np.cos(phases) + np.sin(phases)).astype(np.float32).astype(ml_dtypes.bfloat16)
 
 
-def screened_kernel():
-    modes = np.arange(NG)
-    modes = np.where(2 * modes < NG, modes, modes - NG)
-    squares = (modes * (2.0 * math.pi / NG)) ** 2
-    norm_sq = squares[:, None, None] + squares[None, :, None] + squares[None, None, :]
-    bounded = np.where(norm_sq > 0, norm_sq, 1.0)
-    screened = np.where(
-        norm_sq > 0,
-        4.0 * math.pi / bounded * (1.0 - np.exp(-bounded / (4.0 * OMEGA * OMEGA))),
-        math.pi / (OMEGA * OMEGA),
-    )
-    return (screened / NG**3).astype(np.float32)
+def squared_modes(index):
+    modes = jnp.where(2 * index < NG, index, index - NG)
+    wavenum = modes.astype(jnp.float32) * (2.0 * math.pi / NG)
+    return wavenum * wavenum
+
+
+def screened_body(earlier_ref, kernel_ref):
+    first = squared_modes(lax.broadcasted_iota(jnp.int32, (NG, 128), 0))
+    third = squared_modes(lax.rem(lax.broadcasted_iota(jnp.int32, (NG, 128), 1), NG))
+
+    def one_line(line, carry):
+        second = 2 * lax.rem(line, NG // 2) + lax.div(line, NG // 2)
+        norm_sq = first + squared_modes(jnp.full((NG, 128), second, jnp.int32)) + third
+        bounded = jnp.where(norm_sq > 0, norm_sq, 1.0)
+        screened = jnp.where(
+            norm_sq > 0,
+            4.0 * math.pi / bounded * (1.0 - jnp.exp(-bounded / (4.0 * OMEGA * OMEGA))),
+            math.pi / (OMEGA * OMEGA),
+        )
+        kernel_ref[line] = screened * (1.0 / G)
+        return carry
+
+    lax.fori_loop(0, NG, one_line, 0, unroll=2)
+
+
+def screened_kernel(earlier):
+    return pl.pallas_call(
+        screened_body,
+        out_shape=jax.ShapeDtypeStruct((NG, NG, 128), jnp.float32),
+        in_specs=[pl.BlockSpec(memory_space=pl.ANY)],
+        out_specs=VMEM,
+        compiler_params=pltpu.CompilerParams(vmem_limit_bytes=16 * 1024 * 1024),
+        cost_estimate=pl.CostEstimate(
+            flops=NEAR_FLOPS, bytes_accessed=2 * 1024 * 1024, transcendentals=0
+        ),
+        name="screened_kernel",
+    )(earlier)
 
 
 def repeated(table):
@@ -54,8 +79,7 @@
 def constants():
     table = cas_table()
     mixed = table[ORDER][:, ORDER]
-    kernel = screened_kernel().transpose(1, 0, 2)[ORDER]
-    return repeated(table), repeated(mixed), np.concatenate([kernel, kernel], axis=2)
+    return repeated(table), repeated(mixed)
 
 
 def dot(left, right):
@@ -107,6 +131,8 @@
 
 
 def plane_rows(plane, height):
+    if isinstance(plane, int):
+        return pl.ds(plane * height, height)
     return pl.ds(pl.multiple_of(plane * height, height), height)
 
 
@@ -114,6 +140,8 @@
     bf16 = jnp.bfloat16
 
     def pitched(plane):
+        if isinstance(plane, int):
+            return pl.ds(plane * PITCH, NG)
         return pl.ds(pl.multiple_of(plane * PITCH, 8), NG)
 
     def beside(parts):
@@ -228,10 +256,12 @@
 
 def exchange_body(
     far_ref, owner_ref, term_ref, trial_ref, table_ref, mixed_ref, kernel_ref,
-    out_ref, visitors, grid,
+    out_ref, visitors, grid, tiles, trial_left, left,
 ):
     f32, bf16 = jnp.float32, jnp.bfloat16
     low = low_lanes(NG // 2)
+    trial_copy = pltpu.make_async_copy(trial_ref, out_ref.at[:, pl.ds(0, 16), :], trial_left)
+    trial_copy.start()
 
     def density_of(plane):
         far = both_halves(far_ref[plane_rows(plane, 32), :].astype(f32), low)
@@ -242,29 +272,35 @@
     potentials = passes_there(density_of, table_ref, mixed_ref, kernel_ref, grid)
     fill = fill_of(far_ref)
 
-    def backward(step, carry):
+    def tile_copy(step):
+        peers = pl.ds(step * 2 * SPAN, 2 * SPAN)
+        return pltpu.make_async_copy(
+            tiles.at[peers], out_ref.at[peers, pl.ds(16, 16), :], left.at[step]
+        )
+
+    for step in range(NG // SPAN):
         for plane, potential in potentials(step):
             total = potential * (visitors[plane_rows(plane, 64), :].astype(f32) * fill)
-            rows = plane_rows(plane, 32)
-            value = (jnp.where(low, total[:32], total[32:]) + term_ref[rows, :]).astype(bf16)
-            trial = trial_ref[rows, :]
-            out_ref[plane_rows(plane, 64), :] = jnp.concatenate(
-                [trial[:16], value[:16], trial[16:], value[16:]], axis=0
-            )
-        return carry
-
-    lax.fori_loop(0, NG // SPAN, backward, 0, unroll=True)
+            value = jnp.where(low, total[:32], total[32:]) + term_ref[plane_rows(plane, 32), :]
+            tiles[pl.ds(2 * plane, 2)] = value.astype(bf16).reshape(2, 16, 128)
+        tile_copy(step).start()
+    trial_copy.wait()
+    for step in range(NG // SPAN):
+        tile_copy(step).wait()
 
 
 def exchange_of(far, owner, term, trial, table, mixed, kernel):
     return pl.pallas_call(
         exchange_body,
-        out_shape=jax.ShapeDtypeStruct((2 * ROWS, 128), jnp.bfloat16),
+        out_shape=jax.ShapeDtypeStruct((128, 32, 128), jnp.bfloat16),
         in_specs=[VMEM] * 7,
-        out_specs=VMEM,
+        out_specs=pl.BlockSpec(memory_space=pltpu.HBM),
         scratch_shapes=[
             pltpu.VMEM((NG * NG, 128), jnp.bfloat16),
             pltpu.VMEM((NG * PITCH, 128), jnp.float32),
+            pltpu.VMEM((128, 16, 128), jnp.bfloat16),
+            pltpu.SemaphoreType.DMA,
+            pltpu.SemaphoreType.DMA((NG // SPAN,)),
         ],
         compiler_params=pltpu.CompilerParams(vmem_limit_bytes=24 * 1024 * 1024),
         name="exchange",
@@ -328,16 +364,25 @@
     )(tiles, token, core)
 
 
-def projected_body(lines_ref, mine_ref, other_ref, core_ref, out_ref):
+def projected_body(lines_ref, mine_ref, other_ref, core_ref, out_ref, result, left):
     first = core_ref[0] == 0
     mine, other = mine_ref[...].astype(jnp.float32), other_ref[...].astype(jnp.float32)
     table = jnp.concatenate(
         [jnp.where(first, mine, other), jnp.where(first, other, mine)], axis=0
     ).astype(jnp.bfloat16)
-    for line in range(16):
-        rows = pl.ds(line * 128, 128)
-        value = dot(table, lines_ref[rows, :]) * (-1.0 / math.sqrt(128))
-        out_ref[:, rows] = value.astype(jnp.bfloat16)
+
+    def copy(part):
+        columns = pl.ds(part * 512, 512)
+        return pltpu.make_async_copy(result.at[:, columns], out_ref.at[:, columns], left.at[part])
+
+    for part in range(4):
+        for line in range(part * 4, part * 4 + 4):
+            rows = pl.ds(line * 128, 128)
+            value = dot(table, lines_ref[rows, :]) * (-1.0 / math.sqrt(128))
+            result[:, rows] = value.astype(jnp.bfloat16)
+        copy(part).start()
+    for part in range(4):
+        copy(part).wait()
 
 
 def projected_of(lines, mine, other, core):
@@ -345,7 +390,11 @@
         projected_body,
         out_shape=jax.ShapeDtypeStruct((128, ROWS), jnp.bfloat16),
         in_specs=[VMEM, VMEM, VMEM, SMEM],
-        out_specs=VMEM,
+        out_specs=pl.BlockSpec(memory_space=pltpu.HBM),
+        scratch_shapes=[
+            pltpu.VMEM((128, ROWS), jnp.bfloat16),
+            pltpu.SemaphoreType.DMA((4,)),
+        ],
         compiler_params=pltpu.CompilerParams(vmem_limit_bytes=16 * 1024 * 1024),
         name="projected",
     )(lines, mine, other, core)
@@ -369,14 +418,14 @@
 
 
 def local(orbitals, trial, occupations):
-    tables = [jnp.asarray(value) for value in constants()]
     own = packed_with_flag(orbitals, occupations)
+    tables = [jnp.asarray(value) for value in constants()] + [screened_kernel(own)]
     far, near = from_far(own), swapped(own)
     trial_rows = packed_after(trial, own)
     owner, term = near_term(own, near, *tables)
-    both = exchange_of(far, owner, term, trial_rows, *tables)
-    tiles = lax.all_to_all(both.reshape(128, 32, 128), BAND, 0, 0, tiled=True)
-    flat, token = unpacked(both)
+    both = exchange_of(far, owner, term, trial_rows.reshape(128, 16, 128), *tables)
+    tiles = lax.all_to_all(both, BAND, 0, 0, tiled=True)
+    flat, token = unpacked(both.reshape(2 * ROWS, 128))
     core = lax.axis_index("core").astype(jnp.int32).reshape(1)
     lines, mine, other = intersection_of(tiles.reshape(2 * ROWS, 128), token, core)
     half = (mine + swapped(other)).astype(jnp.bfloat16)

time: 95.8 us -> 95.3 us (level)
  local copies, waits for them, and re-layouts: 3.14 us -> 1.27 us
  Pallas kernels: 11.7 us -> 12.9 us
    unnamed x10 -> x8, local copies, waits for them, and re-layouts: 3.1 us -> 1.24 us
    pallas_call x1 -> x2, Pallas kernels: 3.78 us -> 5 us  [the longest x1 3.51 us: exchange_of(): pl.pallas_call(exchange_body, out_shape=jax.ShapeDtypeStruct((128, 32, 12...]
  transfers between devices with their start and end apart: 5 -> 5, of which waited for: 5 -> 4; matrix products, arithmetic and copies ran while one was open for 0% -> 0% of each run, Pallas kernels for 6% -> 8%
where the time goes in v5:
time: 95.3 us; the launch traced here: 94.9 us
  waiting for transfers between devices  34.7 us (36%)
  starting transfers between devices  23.9 us (25%)
  blocking collectives  20.6 us (22%)
  Pallas kernels  12.9 us (14%)
  between operations  1.41 us (1%)
  local copies, waits for them, and re-layouts  1.27 us (1%)
    all_to_all x1, waiting for transfers between devices, local(): tiles = lax.all_to_all(both, BAND, 0, 0, tiled=True)  28.6 us
    all_to_all x2, blocking collectives, summed_over(): tiles = lax.all_to_all(copies, axes, 0, 0, tiled=True)  20.6 us
    all_to_all x1, starting transfers between devices, local(): tiles = lax.all_to_all(both, BAND, 0, 0, tiled=True)  17.5 us
    ppermute x3, starting transfers between devices, swapped(): return lax.ppermute(value, 'core', [(0, 1), (1, 0)])  6.43 us
    ppermute x1, waiting for transfers between devices, from_far(): return lax.ppermute(value, BAND, pairs)  4.02 us
    pallas_call x1, Pallas kernels, exchange_of(): pl.pallas_call(exchange_body, out_shape=jax.ShapeDtypeStruct((128, 32, 12...  3.51 us
    pallas_call x1, Pallas kernels, unpacked(): pl.pallas_call(unpack_body, out_shape=(jax.ShapeDtypeStruct((1, G), jnp.b...  3.15 us
    pallas_call x1, Pallas kernels, near_term(): pl.pallas_call(near_body, out_shape=(jax.ShapeDtypeStruct((NG * NG, 128),...  2.92 us
  transfers between devices with their start and end apart: 5, of which 4 were waited for; matrix products, arithmetic and copies ran while one was open for 0% of the time, Pallas kernels for 8%

profile of v5, /device:TPU:1, one launch (start us, length us, event | category | flops | bytes accessed | tf_op | source)
XLA Modules:
  0.0 94.9 jit_solution(18039301981121288346)
XLA Ops:
  1.3 0.0 copy-start
  1.3 1.2 %copy-done = bf16[1,262144]{1,0:T(2,128)(2,1)S(1)} copy-done((bf16[1,262144]{1,0:T(2,128)(2,1)S(1)}, bf16[1,262144]{1,0:T(2,128)(2,1)}, u32[]{:S(2)}) %copy-start) | copy-done | bytes 524312
  2.5 0.0 copy-start.1
  2.5 0.1 pack_flagged.1.earlier_ref.own_ref
  2.6 3.3 %collective-permute-start.1 = (bf16[2064,128]{1,0:T(8,128)(2,1)S(1)}, bf16[2064,128]{1,0:T(8,128)(2,1)S(1)}, u32[]{:S(2)}, u32[]{:S(2)}) collective-permute-start(bf16[2064,128]{1,0:T(8,128)(2,1)S(1)} %pack_flagged.1.earlier_ref.own_ref), channel_id=1, source_target_pairs={{0,1},{1,0},{2,3},{3,2},{4,5},{5,4},{6,7},{7,6},{8,9},{9,8},{10,11... | collective-permute-start | bytes 1585160 | tf_op jit(solution)/shard_map/ppermute | solution.py:410
  6.0 0.0 collective-permute-start
  6.0 0.0 copy-done.1
  6.0 0.1 pack.1
  6.1 0.0 copy-start.2
  6.1 0.0 copy-start.3
  6.1 1.5 %screened_kernel.1.kernel_ref = f32[64,64,128]{2,1,0:T(8,128)S(1)} custom-call(bf16[2064,128]{1,0:T(8,128)(2,1)S(1)} %pack_flagged.1.earlier_ref.own_ref), custom_call_target="tpu_custom_call" | custom-call | flops 10000000000 | bytes 2097152 | tf_op jit(solution)/shard_map/screened_kernel/pallas_call | solution.py:62
  7.7 0.0 collective-permute-done.1.near_ref
  7.7 0.0 copy-done.2
  7.7 0.0 copy-done.3
  7.7 2.9 %near_term.1 = (bf16[4096,128]{1,0:T(8,128)(2,1)S(1)}, f32[2048,128]{1,0:T(8,128)S(1)}) custom-call(bf16[2064,128]{1,0:T(8,128)(2,1)S(1)} %pack_flagged.1.earlier_ref.own_ref, bf16[2064,128]{1,0:T(8,128)(2,1)S(1)} %collective-permute-done.1.near_ref, bf16[256,256]{1,0:T(8,128)(2,1)S(1)} %copy-done.2, bf16[256,256]{1,0:T(8,128)(2,1)S(1)} %copy-done.3, ...), custom_call_target="tpu_custom_call" | custom-call | flops 10000000000 | bytes 4194304 | tf_op jit(solution)/shard_map/near_term/pallas_call | solution.py:237
  10.6 4.0 %collective-permute-done.far_ref = bf16[2064,128]{1,0:T(8,128)(2,1)S(1)} collective-permute-done((bf16[2064,128]{1,0:T(8,128)(2,1)S(1)}, bf16[2064,128]{1,0:T(8,128)(2,1)S(1)}, u32[]{:S(2)}, u32[]{:S(2)}) %collective-permute-start) | collective-permute-done | bytes 528416 | tf_op jit(solution)/shard_map/ppermute | solution.py:406
  14.6 3.5 %exchange.1 = bf16[128,32,128]{2,1,0:T(8,128)(2,1)} custom-call(bf16[2064,128]{1,0:T(8,128)(2,1)S(1)} %collective-permute-done.far_ref, bf16[4096,128]{1,0:T(8,128)(2,1)S(1)} %get-tuple-element.9.owner_ref, f32[2048,128]{1,0:T(8,128)S(1)} %get-tuple-element.10.term_ref, bf16[128,16,128]{2,1,0:T(8,128)(2,1)S(1)} %bitcast.5, bf16[256,256]{1,0:T(8,128)(2,1)S(1)} %copy-done.2, ...), custom_call_target="tpu_custom_call" | custom-call | tf_op jit(solution)/shard_map/exchange/pallas_call | solution.py:293
  18.1 17.5 %all-to-all-start = ((bf16[128,32,128]{2,1,0:T(8,128)(2,1)}), bf16[128,32,128]{2,1,0:T(8,128)(2,1)S(1)}, u32[]{:S(2)}, u32[]{:S(2)}) async-start(bf16[128,32,128]{2,1,0:T(8,128)(2,1)} %exchange.1), calls=%async_computation | async-start | bytes 2097152 | tf_op jit(solution)/shard_map/all_to_all | solution.py:427
  35.6 3.1 %unpack.1 = (bf16[1,262144]{1,0:T(2,128)(2,1)}, bf16[16,128]{1,0:T(8,128)(2,1)S(1)}) custom-call(bf16[4096,128]{1,0:T(8,128)(2,1)} %bitcast.1.tiles_ref), custom_call_target="tpu_custom_call" | custom-call | tf_op jit(solution)/shard_map/unpack/pallas_call | solution.py:323
  38.8 28.6 %all-to-all-done = bf16[128,32,128]{2,1,0:T(8,128)(2,1)S(1)} async-done(((bf16[128,32,128]{2,1,0:T(8,128)(2,1)}), bf16[128,32,128]{2,1,0:T(8,128)(2,1)S(1)}, u32[]{:S(2)}, u32[]{:S(2)}) %all-to-all-start) | async-done | bytes 1048608 | tf_op jit(solution)/shard_map/all_to_all | solution.py:427
  67.4 0.6 intersection.1
  68.0 0.1 collective-permute-start.2
  68.1 1.2 %collective-permute-done.2 = f32[64,128]{1,0:T(8,128)S(1)} collective-permute-done((f32[64,128]{1,0:T(8,128)S(1)}, f32[64,128]{1,0:T(8,128)S(1)}, u32[]{:S(2)}, u32[]{:S(2)}) %collective-permute-start.2) | collective-permute-done | bytes 32800 | tf_op jit(solution)/shard_map/ppermute | solution.py:410
  69.3 10.0 %all_to_all.15 = bf16[8,64,128]{2,1,0:T(8,128)(2,1)S(1)} all-to-all(bf16[8,64,128]{2,1,0:T(8,128)(2,1)S(1)} %broadcast_in_dim.4), channel_id=1, replica_groups=mesh['spin'=2,'y'=4,'x'=2,'z'=8,'core'=2] {'y','x'}, dimensions={0} | all-to-all | bytes 262144 | tf_op jit(solution)/shard_map/all_to_all | solution.py:416
  79.4 10.6 %all_to_all.16 = bf16[8,64,128]{2,1,0:T(8,128)(2,1)S(1)} all-to-all(bf16[8,64,128]{2,1,0:T(8,128)(2,1)S(1)} %broadcast_in_dim.5), channel_id=1, replica_groups=mesh['spin'=2,'y'=4,'x'=2,'z'=8,'core'=2] {'z'}, dimensions={0} | all-to-all | bytes 262144 | tf_op jit(solution)/shard_map/all_to_all | solution.py:416
  90.0 3.0 %collective-permute-start.3 = (bf16[64,128]{1,0:T(8,128)(2,1)S(1)}, bf16[64,128]{1,0:T(8,128)(2,1)S(1)}, u32[]{:S(2)}, u32[]{:S(2)}) collective-permute-start(bf16[64,128]{1,0:T(8,128)(2,1)S(1)} %reduce_sum.25.mine_ref), channel_id=1, source_target_pairs={{0,1},{1,0},{2,3},{3,2},{4,5},{5,4},{6,7},{7,6},{8,9},{9,8},{10,11... | collective-permute-start | bytes 49160 | tf_op jit(solution)/shard_map/ppermute | solution.py:410
  93.1 0.8 collective-permute-done.3.other_ref
  93.9 1.0 %projected.1 = bf16[128,2048]{1,0:T(8,128)(2,1)} custom-call(bf16[2048,128]{1,0:T(8,128)(2,1)S(1)} %get-tuple-element.13.lines_ref, bf16[64,128]{1,0:T(8,128)(2,1)S(1)} %reduce_sum.25.mine_ref, bf16[64,128]{1,0:T(8,128)(2,1)S(1)} %collective-permute-done.3.other_ref, s32[1]{0:T(128)} %bitcast.3.core_ref), custom_call_target="tpu_custom_call" | custom-call | tf_op jit(solution)/shard_map/projected/pallas_call | solution.py:389
  (5 shorter events, 0.1 us)
Async XLA Ops:
  1.3 1.2 %copy-start = (bf16[1,262144]{1,0:T(2,128)(2,1)S(1)}, bf16[1,262144]{1,0:T(2,128)(2,1)}, u32[]{:S(2)}) copy-start(bf16[1,262144]{1,0:T(2,128)(2,1)} %flat_ref.2) | copy-start | bytes 1572868
  2.5 3.5 %copy-start.1 = (bf16[1,262144]{1,0:T(2,128)(2,1)S(1)}, bf16[1,262144]{1,0:T(2,128)(2,1)}, u32[]{:S(2)}) copy-start(bf16[1,262144]{1,0:T(2,128)(2,1)} %flat_ref.3) | copy-start | bytes 1572868
  2.6 5.0 %collective-permute-start.1 = (bf16[2064,128]{1,0:T(8,128)(2,1)S(1)}, bf16[2064,128]{1,0:T(8,128)(2,1)S(1)}, u32[]{:S(2)}, u32[]{:S(2)}) collective-permute-start(bf16[2064,128]{1,0:T(8,128)(2,1)S(1)} %pack_flagged.1.earlier_ref.own_ref), channel_id=1, source_target_pairs={{0,1},{1,0},{2,3},{3,2},{4,5},{5,4},{6,7},{7,6},{8,9},{9,8},{10,11... | collective-permute-start | bytes 1585160 | tf_op jit(solution)/shard_map/ppermute | solution.py:410
  6.0 8.7 %collective-permute-start = (bf16[2064,128]{1,0:T(8,128)(2,1)S(1)}, bf16[2064,128]{1,0:T(8,128)(2,1)S(1)}, u32[]{:S(2)}, u32[]{:S(2)}) collective-permute-start(bf16[2064,128]{1,0:T(8,128)(2,1)S(1)} %pack_flagged.1.earlier_ref.own_ref), channel_id=1, source_target_pairs={{0,127},{1,2},{2,1},{3,4},{4,3},{5,6},{6,5},{7,8},{8,7},{9,10},{10... | collective-permute-start | bytes 1585160 | tf_op jit(solution)/shard_map/ppermute | solution.py:406
  6.1 1.5 %copy-start.2 = (bf16[256,256]{1,0:T(8,128)(2,1)S(1)}, bf16[256,256]{1,0:T(8,128)(2,1)}, u32[]{:S(2)}) copy-start(bf16[256,256]{1,0:T(8,128)(2,1)} %constant.12.clone.table_ref) | copy-start | bytes 393220
  6.1 1.5 %copy-start.3 = (bf16[256,256]{1,0:T(8,128)(2,1)S(1)}, bf16[256,256]{1,0:T(8,128)(2,1)}, u32[]{:S(2)}) copy-start(bf16[256,256]{1,0:T(8,128)(2,1)} %constant.13.clone.mixed_ref) | copy-start | bytes 393220
  18.1 49.3 %all-to-all-start = ((bf16[128,32,128]{2,1,0:T(8,128)(2,1)}), bf16[128,32,128]{2,1,0:T(8,128)(2,1)S(1)}, u32[]{:S(2)}, u32[]{:S(2)}) async-start(bf16[128,32,128]{2,1,0:T(8,128)(2,1)} %exchange.1), calls=%async_computation | async-start | bytes 2097152 | tf_op jit(solution)/shard_map/all_to_all | solution.py:427
  68.0 1.3 %collective-permute-start.2 = (f32[64,128]{1,0:T(8,128)S(1)}, f32[64,128]{1,0:T(8,128)S(1)}, u32[]{:S(2)}, u32[]{:S(2)}) collective-permute-start(f32[64,128]{1,0:T(8,128)S(1)} %get-tuple-element.15), channel_id=1, source_target_pairs={{0,1},{1,0},{2,3},{3,2},{4,5},{5,4},{6,7},{7,6},{8,9},{9,8},{10,11... | collective-permute-start | bytes 98312 | tf_op jit(solution)/shard_map/ppermute | solution.py:410
  90.0 3.8 %collective-permute-start.3 = (bf16[64,128]{1,0:T(8,128)(2,1)S(1)}, bf16[64,128]{1,0:T(8,128)(2,1)S(1)}, u32[]{:S(2)}, u32[]{:S(2)}) collective-permute-start(bf16[64,128]{1,0:T(8,128)(2,1)S(1)} %reduce_sum.25.mine_ref), channel_id=1, source_target_pairs={{0,1},{1,0},{2,3},{3,2},{4,5},{5,4},{6,7},{7,6},{8,9},{9,8},{10,11... | collective-permute-start | bytes 49160 | tf_op jit(solution)/shard_map/ppermute | solution.py:410

commit v6 on v5

--- a/solution.py
+++ b/solution.py
@@ -22,6 +22,7 @@
 SPAN = 2 * STEP
 PITCH = 72
 WIDE = 40
+HALF = NG // 2
 NEAR_FLOPS = 10**10
 VMEM = pl.BlockSpec(memory_space=pltpu.VMEM)
 SMEM = pl.BlockSpec(memory_space=pltpu.SMEM)
@@ -79,7 +80,9 @@
 def constants():
     table = cas_table()
     mixed = table[ORDER][:, ORDER]
-    return repeated(table), repeated(mixed)
+    crossed = np.concatenate([table[HALF:, HALF:], table[HALF:, :HALF]], axis=1)
+    halves = np.concatenate([table[:HALF], crossed], axis=0)
+    return repeated(table), repeated(mixed), repeated(halves)
 
 
 def dot(left, right):
@@ -100,7 +103,7 @@
 
 def pack_flagged_body(flat_ref, flag_ref, tiles_ref):
     pack_body(flat_ref, tiles_ref)
-    flag = jnp.full((16, 128), flag_ref[0], jnp.int32)
+    flag = jnp.broadcast_to(flag_ref[...], (16, 128))
     tiles_ref[pl.ds(ROWS, 16), :] = flag.astype(jnp.float32).astype(jnp.bfloat16)
 
 
@@ -123,11 +126,11 @@
     return pl.pallas_call(
         pack_flagged_body,
         out_shape=jax.ShapeDtypeStruct((ROWS + 16, 128), jnp.bfloat16),
-        in_specs=[VMEM, SMEM],
+        in_specs=[VMEM, VMEM],
         out_specs=VMEM,
         compiler_params=pltpu.CompilerParams(vmem_limit_bytes=16 * 1024 * 1024),
         name="pack_flagged",
-    )(flat, flag)
+    )(flat, flag.reshape(1, 1))
 
 
 def plane_rows(plane, height):
@@ -136,22 +139,25 @@
     return pl.ds(pl.multiple_of(plane * height, height), height)
 
 
+def pitched(plane):
+    if isinstance(plane, int):
+        return pl.ds(plane * PITCH, NG)
+    return pl.ds(pl.multiple_of(plane * PITCH, 8), NG)
+
+
+def beside(parts):
+    return jnp.concatenate(
+        [jnp.concatenate(parts[:STEP], axis=0), jnp.concatenate(parts[STEP:], axis=0)], axis=1
+    )
+
+
+def part_of(values, part):
+    rows = slice(part % STEP * NG, part % STEP * NG + NG)
+    return values[rows, :128] if part < STEP else values[rows, 128:]
+
+
 def passes_there(density_of, table_ref, mixed_ref, kernel_ref, grid):
     bf16 = jnp.bfloat16
-
-    def pitched(plane):
-        if isinstance(plane, int):
-            return pl.ds(plane * PITCH, NG)
-        return pl.ds(pl.multiple_of(plane * PITCH, 8), NG)
-
-    def beside(parts):
-        return jnp.concatenate(
-            [jnp.concatenate(parts[:STEP], axis=0), jnp.concatenate(parts[STEP:], axis=0)], axis=1
-        )
-
-    def part_of(values, part):
-        rows = slice(part % STEP * NG, part % STEP * NG + NG)
-        return values[rows, :128] if part < STEP else values[rows, 128:]
 
     def forward(step, carry):
         planes = [step * SPAN + part for part in range(SPAN)]
@@ -191,9 +197,14 @@
     return ref[pl.ds(ROWS, 16), :].astype(jnp.float32)[:1] * -FRACTION
 
 
-def both_halves(value, low):
-    turned = pltpu.roll(value, 64, 1)
-    return jnp.concatenate([jnp.where(low, value, turned), jnp.where(low, turned, value)], axis=0)
+def two_planes(ref, plane, low):
+    first, second = (
+        ref[plane_rows(index, 32), :].astype(jnp.float32) for index in (plane, plane + HALF)
+    )
+    first_turned, second_turned = (pltpu.roll(value, 64, 1) for value in (first, second))
+    return jnp.concatenate(
+        [jnp.where(low, first, second_turned), jnp.where(low, first_turned, second)], axis=0
+    )
 
 
 def low_lanes(height):
@@ -216,12 +227,13 @@
             [jnp.where(low, own, near_turned), jnp.where(low, own_turned, near)], axis=0
         )
         wide = plane_rows(plane, 64)
-        owner_ref[wide, :] = mine.astype(bf16)
         visitors[wide, :] = pairs.astype(bf16)
         return (mine * pairs).astype(bf16)
 
     potentials = passes_there(density_of, table_ref, mixed_ref, kernel_ref, grid)
     fill = jnp.where(low_lanes(NG), fill_of(own_ref), fill_of(near_ref))
+    for plane in range(HALF):
+        owner_ref[plane_rows(plane, 64), :] = two_planes(own_ref, plane, low).astype(bf16)
 
     def backward(step, carry):
         for plane, potential in potentials(step):
@@ -237,7 +249,7 @@
     return pl.pallas_call(
         near_body,
         out_shape=(
-            jax.ShapeDtypeStruct((NG * NG, 128), jnp.bfloat16),
+            jax.ShapeDtypeStruct((HALF * NG, 128), jnp.bfloat16),
             jax.ShapeDtypeStruct((ROWS, 128), jnp.float32),
         ),
         in_specs=[VMEM] * 5,
@@ -255,56 +267,98 @@
 
 
 def exchange_body(
-    far_ref, owner_ref, term_ref, trial_ref, table_ref, mixed_ref, kernel_ref,
+    far_ref, owner_ref, term_ref, trial_ref, table_ref, mixed_ref, halves_ref, kernel_ref,
     out_ref, visitors, grid, tiles, trial_left, left,
 ):
     f32, bf16 = jnp.float32, jnp.bfloat16
-    low = low_lanes(NG // 2)
+    low = low_lanes(HALF)
     trial_copy = pltpu.make_async_copy(trial_ref, out_ref.at[:, pl.ds(0, 16), :], trial_left)
     trial_copy.start()
 
-    def density_of(plane):
-        far = both_halves(far_ref[plane_rows(plane, 32), :].astype(f32), low)
-        wide = plane_rows(plane, 64)
-        visitors[wide, :] = far.astype(bf16)
-        return (far * owner_ref[wide, :].astype(f32)).astype(bf16)
-
-    potentials = passes_there(density_of, table_ref, mixed_ref, kernel_ref, grid)
+    for step in range(HALF // SPAN):
+        planes = [step * SPAN + part for part in range(SPAN)]
+        densities = []
+        for plane in planes:
+            far = two_planes(far_ref, plane, low)
+            wide = plane_rows(plane, 64)
+            visitors[wide, :] = far.astype(bf16)
+            densities.append((far * owner_ref[wide, :].astype(f32)).astype(bf16))
+        values = dot(beside(densities), table_ref[...]).astype(bf16)
+        values = dot(mixed_ref[...], values)
+        for part, plane in enumerate(planes):
+            grid[pitched(plane), :] = part_of(values, part)
+
+    def crossed(value):
+        return jnp.concatenate([value, pltpu.roll(value, 64, 1)], axis=0).astype(bf16)
+
+    def joined(value):
+        return jnp.where(low, value[:HALF], value[HALF:])
+
+    for step in range(NG // SPAN):
+        lines = [step * SPAN + part for part in range(SPAN)]
+        rows = [pl.ds(line, HALF, stride=PITCH) for line in lines]
+        values = dot(halves_ref[...], beside([crossed(grid[row, :]) for row in rows]))
+        values = beside(
+            [
+                crossed(joined(part_of(values, part)) * joined(kernel_ref[line]))
+                for part, line in enumerate(lines)
+            ]
+        )
+        values = dot(halves_ref[...], values)
+        for part, row in enumerate(rows):
+            grid[row, :] = joined(part_of(values, part))
+
     fill = fill_of(far_ref)
 
-    def tile_copy(step):
-        peers = pl.ds(step * 2 * SPAN, 2 * SPAN)
-        return pltpu.make_async_copy(
-            tiles.at[peers], out_ref.at[peers, pl.ds(16, 16), :], left.at[step]
-        )
-
-    for step in range(NG // SPAN):
-        for plane, potential in potentials(step):
-            total = potential * (visitors[plane_rows(plane, 64), :].astype(f32) * fill)
-            value = jnp.where(low, total[:32], total[32:]) + term_ref[plane_rows(plane, 32), :]
-            tiles[pl.ds(2 * plane, 2)] = value.astype(bf16).reshape(2, 16, 128)
-        tile_copy(step).start()
+    def tile_copies(step):
+        copies = []
+        for half in range(2):
+            peers = pl.ds(step * 2 * SPAN + half * NG, 2 * SPAN)
+            copies.append(
+                pltpu.make_async_copy(
+                    tiles.at[peers], out_ref.at[peers, pl.ds(16, 16), :], left.at[half, step]
+                )
+            )
+        return copies
+
+    for step in range(HALF // SPAN):
+        planes = [step * SPAN + part for part in range(SPAN)]
+        values = beside([grid[pitched(plane), :].astype(bf16) for plane in planes])
+        values = dot(mixed_ref[...], values).astype(bf16)
+        values = dot(values, table_ref[...])
+        for part, plane in enumerate(planes):
+            weight = visitors[plane_rows(plane, 64), :].astype(f32) * fill
+            total = part_of(values, part) * weight
+            turned = pltpu.roll(total, 64, 1)
+            first = jnp.where(low, total[:HALF], turned[HALF:])
+            second = jnp.where(low, turned[:HALF], total[HALF:])
+            for index, value in ((plane, first), (plane + HALF, second)):
+                value = value + term_ref[plane_rows(index, 32), :]
+                tiles[pl.ds(2 * index, 2)] = value.astype(bf16).reshape(2, 16, 128)
+        for copy in tile_copies(step):
+            copy.start()
     trial_copy.wait()
-    for step in range(NG // SPAN):
-        tile_copy(step).wait()
-
-
-def exchange_of(far, owner, term, trial, table, mixed, kernel):
+    for step in range(HALF // SPAN):
+        for copy in tile_copies(step):
+            copy.wait()
+
+
+def exchange_of(far, owner, term, trial, table, mixed, halves, kernel):
     return pl.pallas_call(
         exchange_body,
         out_shape=jax.ShapeDtypeStruct((128, 32, 128), jnp.bfloat16),
-        in_specs=[VMEM] * 7,
+        in_specs=[VMEM] * 8,
         out_specs=pl.BlockSpec(memory_space=pltpu.HBM),
         scratch_shapes=[
-            pltpu.VMEM((NG * NG, 128), jnp.bfloat16),
-            pltpu.VMEM((NG * PITCH, 128), jnp.float32),
+            pltpu.VMEM((HALF * NG, 128), jnp.bfloat16),
+            pltpu.VMEM((HALF * PITCH, 128), jnp.float32),
             pltpu.VMEM((128, 16, 128), jnp.bfloat16),
             pltpu.SemaphoreType.DMA,
-            pltpu.SemaphoreType.DMA((NG // SPAN,)),
+            pltpu.SemaphoreType.DMA((2, HALF // SPAN)),
         ],
         compiler_params=pltpu.CompilerParams(vmem_limit_bytes=24 * 1024 * 1024),
         name="exchange",
-    )(far, owner, term, trial, table, mixed, kernel)
+    )(far, owner, term, trial, table, mixed, halves, kernel)
 
 
 def unpack_body(tiles_ref, flat_ref, token_ref):
@@ -419,11 +473,13 @@
 
 def local(orbitals, trial, occupations):
     own = packed_with_flag(orbitals, occupations)
-    tables = [jnp.asarray(value) for value in constants()] + [screened_kernel(own)]
+    table, mixed, halves = (jnp.asarray(value) for value in constants())
+    kernel = screened_kernel(own)
     far, near = from_far(own), swapped(own)
     trial_rows = packed_after(trial, own)
-    owner, term = near_term(own, near, *tables)
-    both = exchange_of(far, owner, term, trial_rows.reshape(128, 16, 128), *tables)
+    owner, term = near_term(own, near, table, mixed, kernel)
+    trial_tiles = trial_rows.reshape(128, 16, 128)
+    both = exchange_of(far, owner, term, trial_tiles, table, mixed, halves, kernel)
     tiles = lax.all_to_all(both, BAND, 0, 0, tiled=True)
     flat, token = unpacked(both.reshape(2 * ROWS, 128))
     core = lax.axis_index("core").astype(jnp.int32).reshape(1)

time: 95.3 us -> 94.9 us (level)
  no operation moved by 1% of the time
where the time goes in v6:
time: 94.9 us; the launch traced here: 94.5 us
  waiting for transfers between devices  34.7 us (37%)
  starting transfers between devices  23.9 us (25%)
  blocking collectives  20.6 us (22%)
  Pallas kernels  12.6 us (13%)
  between operations  1.41 us (1%)
  local copies, waits for them, and re-layouts  1.28 us (1%)
    all_to_all x1, waiting for transfers between devices, local(): tiles = lax.all_to_all(both, BAND, 0, 0, tiled=True)  28.6 us
    all_to_all x2, blocking collectives, summed_over(): tiles = lax.all_to_all(copies, axes, 0, 0, tiled=True)  20.6 us
    all_to_all x1, starting transfers between devices, local(): tiles = lax.all_to_all(both, BAND, 0, 0, tiled=True)  17.5 us
    ppermute x3, starting transfers between devices, swapped(): return lax.ppermute(value, 'core', [(0, 1), (1, 0)])  6.37 us
    ppermute x1, waiting for transfers between devices, from_far(): return lax.ppermute(value, BAND, pairs)  4 us
    pallas_call x1, Pallas kernels, unpacked(): pl.pallas_call(unpack_body, out_shape=(jax.ShapeDtypeStruct((1, G), jnp.b...  3.15 us
    pallas_call x1, Pallas kernels, exchange_of(): pl.pallas_call(exchange_body, out_shape=jax.ShapeDtypeStruct((128, 32, 12...  3.12 us
    pallas_call x1, Pallas kernels, near_term(): pl.pallas_call(near_body, out_shape=(jax.ShapeDtypeStruct((HALF * NG, 128...  2.93 us
  transfers between devices with their start and end apart: 5, of which 4 were waited for; matrix products, arithmetic and copies ran while one was open for 0% of the time, Pallas kernels for 8%

profile of v6, /device:TPU:1, one launch (start us, length us, event | category | flops | bytes accessed | tf_op | source)
XLA Modules:
  0.0 94.5 jit_solution(5427396702032761242)
XLA Ops:
  1.3 0.0 copy-start
  1.3 1.2 %copy-done = bf16[1,262144]{1,0:T(2,128)(2,1)S(1)} copy-done((bf16[1,262144]{1,0:T(2,128)(2,1)S(1)}, bf16[1,262144]{1,0:T(2,128)(2,1)}, u32[]{:S(2)}) %copy-start) | copy-done | bytes 524312
  2.5 0.0 copy-start.1
  2.5 0.2 pack_flagged.1.earlier_ref.own_ref
  2.7 3.3 %collective-permute-start.1 = (bf16[2064,128]{1,0:T(8,128)(2,1)S(1)}, bf16[2064,128]{1,0:T(8,128)(2,1)S(1)}, u32[]{:S(2)}, u32[]{:S(2)}) collective-permute-start(bf16[2064,128]{1,0:T(8,128)(2,1)S(1)} %pack_flagged.1.earlier_ref.own_ref), channel_id=1, source_target_pairs={{0,1},{1,0},{2,3},{3,2},{4,5},{5,4},{6,7},{7,6},{8,9},{9,8},{10,11... | collective-permute-start | bytes 1585160 | tf_op jit(solution)/shard_map/ppermute | solution.py:464
  6.0 0.0 collective-permute-start
  6.0 0.0 copy-done.1
  6.0 0.1 pack.1
  6.1 0.0 copy-start.2
  6.1 0.0 copy-start.3
  6.1 1.5 %screened_kernel.1.kernel_ref = f32[64,64,128]{2,1,0:T(8,128)S(1)} custom-call(bf16[2064,128]{1,0:T(8,128)(2,1)S(1)} %pack_flagged.1.earlier_ref.own_ref), custom_call_target="tpu_custom_call" | custom-call | flops 10000000000 | bytes 2097152 | tf_op jit(solution)/shard_map/screened_kernel/pallas_call | solution.py:63
  7.6 0.0 copy-start.4
  7.7 0.0 collective-permute-done.1.near_ref
  7.7 0.0 copy-done.2
  7.7 0.0 copy-done.3
  7.7 2.9 %near_term.1 = (bf16[2048,128]{1,0:T(8,128)(2,1)S(1)}, f32[2048,128]{1,0:T(8,128)S(1)}) custom-call(bf16[2064,128]{1,0:T(8,128)(2,1)S(1)} %pack_flagged.1.earlier_ref.own_ref, bf16[2064,128]{1,0:T(8,128)(2,1)S(1)} %collective-permute-done.1.near_ref, bf16[256,256]{1,0:T(8,128)(2,1)S(1)} %copy-done.2, bf16[256,256]{1,0:T(8,128)(2,1)S(1)} %copy-done.3, ...), custom_call_target="tpu_custom_call" | custom-call | flops 10000000000 | bytes 4194304 | tf_op jit(solution)/shard_map/near_term/pallas_call | solution.py:249
  10.6 4.0 %collective-permute-done.far_ref = bf16[2064,128]{1,0:T(8,128)(2,1)S(1)} collective-permute-done((bf16[2064,128]{1,0:T(8,128)(2,1)S(1)}, bf16[2064,128]{1,0:T(8,128)(2,1)S(1)}, u32[]{:S(2)}, u32[]{:S(2)}) %collective-permute-start) | collective-permute-done | bytes 528416 | tf_op jit(solution)/shard_map/ppermute | solution.py:460
  14.6 0.0 copy-done.4
  14.6 3.1 %exchange.1 = bf16[128,32,128]{2,1,0:T(8,128)(2,1)} custom-call(bf16[2064,128]{1,0:T(8,128)(2,1)S(1)} %collective-permute-done.far_ref, bf16[2048,128]{1,0:T(8,128)(2,1)S(1)} %get-tuple-element.9.owner_ref, f32[2048,128]{1,0:T(8,128)S(1)} %get-tuple-element.10.term_ref, bf16[128,16,128]{2,1,0:T(8,128)(2,1)S(1)} %bitcast.7, bf16[256,256]{1,0:T(8,128)(2,1)S(1)} %copy-done.2, ...), custom_call_target="tpu_custom_call" | custom-call | tf_op jit(solution)/shard_map/exchange/pallas_call | solution.py:347
  17.8 17.5 %all-to-all-start = ((bf16[128,32,128]{2,1,0:T(8,128)(2,1)}), bf16[128,32,128]{2,1,0:T(8,128)(2,1)S(1)}, u32[]{:S(2)}, u32[]{:S(2)}) async-start(bf16[128,32,128]{2,1,0:T(8,128)(2,1)} %exchange.1), calls=%async_computation | async-start | bytes 2097152 | tf_op jit(solution)/shard_map/all_to_all | solution.py:483
  35.3 3.1 %unpack.1 = (bf16[1,262144]{1,0:T(2,128)(2,1)}, bf16[16,128]{1,0:T(8,128)(2,1)S(1)}) custom-call(bf16[4096,128]{1,0:T(8,128)(2,1)} %bitcast.2.tiles_ref), custom_call_target="tpu_custom_call" | custom-call | tf_op jit(solution)/shard_map/unpack/pallas_call | solution.py:377
  38.4 28.6 %all-to-all-done = bf16[128,32,128]{2,1,0:T(8,128)(2,1)S(1)} async-done(((bf16[128,32,128]{2,1,0:T(8,128)(2,1)}), bf16[128,32,128]{2,1,0:T(8,128)(2,1)S(1)}, u32[]{:S(2)}, u32[]{:S(2)}) %all-to-all-start) | async-done | bytes 1048608 | tf_op jit(solution)/shard_map/all_to_all | solution.py:483
  67.1 0.6 intersection.1
  67.6 0.1 collective-permute-start.2
  67.7 1.2 %collective-permute-done.2 = f32[64,128]{1,0:T(8,128)S(1)} collective-permute-done((f32[64,128]{1,0:T(8,128)S(1)}, f32[64,128]{1,0:T(8,128)S(1)}, u32[]{:S(2)}, u32[]{:S(2)}) %collective-permute-start.2) | collective-permute-done | bytes 32800 | tf_op jit(solution)/shard_map/ppermute | solution.py:464
  69.0 10.0 %all_to_all.15 = bf16[8,64,128]{2,1,0:T(8,128)(2,1)S(1)} all-to-all(bf16[8,64,128]{2,1,0:T(8,128)(2,1)S(1)} %broadcast_in_dim.4), channel_id=1, replica_groups=mesh['spin'=2,'y'=4,'x'=2,'z'=8,'core'=2] {'y','x'}, dimensions={0} | all-to-all | bytes 262144 | tf_op jit(solution)/shard_map/all_to_all | solution.py:470
  79.1 10.6 %all_to_all.16 = bf16[8,64,128]{2,1,0:T(8,128)(2,1)S(1)} all-to-all(bf16[8,64,128]{2,1,0:T(8,128)(2,1)S(1)} %broadcast_in_dim.5), channel_id=1, replica_groups=mesh['spin'=2,'y'=4,'x'=2,'z'=8,'core'=2] {'z'}, dimensions={0} | all-to-all | bytes 262144 | tf_op jit(solution)/shard_map/all_to_all | solution.py:470
  89.7 3.0 %collective-permute-start.3 = (bf16[64,128]{1,0:T(8,128)(2,1)S(1)}, bf16[64,128]{1,0:T(8,128)(2,1)S(1)}, u32[]{:S(2)}, u32[]{:S(2)}) collective-permute-start(bf16[64,128]{1,0:T(8,128)(2,1)S(1)} %reduce_sum.25.mine_ref), channel_id=1, source_target_pairs={{0,1},{1,0},{2,3},{3,2},{4,5},{5,4},{6,7},{7,6},{8,9},{9,8},{10,11... | collective-permute-start | bytes 49160 | tf_op jit(solution)/shard_map/ppermute | solution.py:464
  92.7 0.8 collective-permute-done.3.other_ref
  93.5 1.0 %projected.1 = bf16[128,2048]{1,0:T(8,128)(2,1)} custom-call(bf16[2048,128]{1,0:T(8,128)(2,1)S(1)} %get-tuple-element.13.lines_ref, bf16[64,128]{1,0:T(8,128)(2,1)S(1)} %reduce_sum.25.mine_ref, bf16[64,128]{1,0:T(8,128)(2,1)S(1)} %collective-permute-done.3.other_ref, s32[1]{0:T(128)} %bitcast.4.core_ref), custom_call_target="tpu_custom_call" | custom-call | tf_op jit(solution)/shard_map/projected/pallas_call | solution.py:443
  (5 shorter events, 0.1 us)
Async XLA Ops:
  1.3 1.2 %copy-start = (bf16[1,262144]{1,0:T(2,128)(2,1)S(1)}, bf16[1,262144]{1,0:T(2,128)(2,1)}, u32[]{:S(2)}) copy-start(bf16[1,262144]{1,0:T(2,128)(2,1)} %flat_ref.2) | copy-start | bytes 1572868
  2.5 3.5 %copy-start.1 = (bf16[1,262144]{1,0:T(2,128)(2,1)S(1)}, bf16[1,262144]{1,0:T(2,128)(2,1)}, u32[]{:S(2)}) copy-start(bf16[1,262144]{1,0:T(2,128)(2,1)} %flat_ref.3) | copy-start | bytes 1572868
  2.7 5.0 %collective-permute-start.1 = (bf16[2064,128]{1,0:T(8,128)(2,1)S(1)}, bf16[2064,128]{1,0:T(8,128)(2,1)S(1)}, u32[]{:S(2)}, u32[]{:S(2)}) collective-permute-start(bf16[2064,128]{1,0:T(8,128)(2,1)S(1)} %pack_flagged.1.earlier_ref.own_ref), channel_id=1, source_target_pairs={{0,1},{1,0},{2,3},{3,2},{4,5},{5,4},{6,7},{7,6},{8,9},{9,8},{10,11... | collective-permute-start | bytes 1585160 | tf_op jit(solution)/shard_map/ppermute | solution.py:464
  6.0 8.7 %collective-permute-start = (bf16[2064,128]{1,0:T(8,128)(2,1)S(1)}, bf16[2064,128]{1,0:T(8,128)(2,1)S(1)}, u32[]{:S(2)}, u32[]{:S(2)}) collective-permute-start(bf16[2064,128]{1,0:T(8,128)(2,1)S(1)} %pack_flagged.1.earlier_ref.own_ref), channel_id=1, source_target_pairs={{0,127},{1,2},{2,1},{3,4},{4,3},{5,6},{6,5},{7,8},{8,7},{9,10},{10... | collective-permute-start | bytes 1585160 | tf_op jit(solution)/shard_map/ppermute | solution.py:460
  6.1 1.6 %copy-start.2 = (bf16[256,256]{1,0:T(8,128)(2,1)S(1)}, bf16[256,256]{1,0:T(8,128)(2,1)}, u32[]{:S(2)}) copy-start(bf16[256,256]{1,0:T(8,128)(2,1)} %constant.14.clone.table_ref) | copy-start | bytes 393220
  6.1 1.6 %copy-start.3 = (bf16[256,256]{1,0:T(8,128)(2,1)S(1)}, bf16[256,256]{1,0:T(8,128)(2,1)}, u32[]{:S(2)}) copy-start(bf16[256,256]{1,0:T(8,128)(2,1)} %constant.15.clone.mixed_ref) | copy-start | bytes 393220
  7.6 7.0 %copy-start.4 = (bf16[256,256]{1,0:T(8,128)(2,1)S(1)}, bf16[256,256]{1,0:T(8,128)(2,1)}, u32[]{:S(2)}) copy-start(bf16[256,256]{1,0:T(8,128)(2,1)} %constant.16.clone.halves_ref) | copy-start | bytes 393220
  17.8 49.3 %all-to-all-start = ((bf16[128,32,128]{2,1,0:T(8,128)(2,1)}), bf16[128,32,128]{2,1,0:T(8,128)(2,1)S(1)}, u32[]{:S(2)}, u32[]{:S(2)}) async-start(bf16[128,32,128]{2,1,0:T(8,128)(2,1)} %exchange.1), calls=%async_computation | async-start | bytes 2097152 | tf_op jit(solution)/shard_map/all_to_all | solution.py:483
  67.6 1.3 %collective-permute-start.2 = (f32[64,128]{1,0:T(8,128)S(1)}, f32[64,128]{1,0:T(8,128)S(1)}, u32[]{:S(2)}, u32[]{:S(2)}) collective-permute-start(f32[64,128]{1,0:T(8,128)S(1)} %get-tuple-element.15), channel_id=1, source_target_pairs={{0,1},{1,0},{2,3},{3,2},{4,5},{5,4},{6,7},{7,6},{8,9},{9,8},{10,11... | collective-permute-start | bytes 98312 | tf_op jit(solution)/shard_map/ppermute | solution.py:464
  89.7 3.8 %collective-permute-start.3 = (bf16[64,128]{1,0:T(8,128)(2,1)S(1)}, bf16[64,128]{1,0:T(8,128)(2,1)S(1)}, u32[]{:S(2)}, u32[]{:S(2)}) collective-permute-start(bf16[64,128]{1,0:T(8,128)(2,1)S(1)} %reduce_sum.25.mine_ref), channel_id=1, source_target_pairs={{0,1},{1,0},{2,3},{3,2},{4,5},{5,4},{6,7},{7,6},{8,9},{9,8},{10,11... | collective-permute-start | bytes 49160 | tf_op jit(solution)/shard_map/ppermute | solution.py:464

commit v7 on v6

--- a/solution.py
+++ b/solution.py
@@ -17,6 +17,7 @@
 OMEGA = 1.0
 BAND = ("y", "x", "z", "core")
 SPIN_BAND = ("spin",) + BAND
+SLABS = ("z", "y", "x", "core")
 ORDER = np.concatenate([np.arange(0, NG, 2), np.arange(1, NG, 2)])
 STEP = 4
 SPAN = 2 * STEP
@@ -120,6 +121,21 @@
         compiler_params=pltpu.CompilerParams(vmem_limit_bytes=16 * 1024 * 1024),
         name="pack",
     )(flat, earlier)
+
+
+def again_body(tiles_ref, again_ref):
+    again_ref[...] = tiles_ref[...]
+
+
+def copied(tiles):
+    return pl.pallas_call(
+        again_body,
+        out_shape=jax.ShapeDtypeStruct(tiles.shape, tiles.dtype),
+        in_specs=[VMEM],
+        out_specs=VMEM,
+        compiler_params=pltpu.CompilerParams(vmem_limit_bytes=16 * 1024 * 1024),
+        name="again",
+    )(tiles)
 
 
 def packed_with_flag(flat, flag):
@@ -272,8 +288,14 @@
 ):
     f32, bf16 = jnp.float32, jnp.bfloat16
     low = low_lanes(HALF)
-    trial_copy = pltpu.make_async_copy(trial_ref, out_ref.at[:, pl.ds(0, 16), :], trial_left)
-    trial_copy.start()
+    trial_copies = [
+        pltpu.make_async_copy(
+            trial_ref.at[row], out_ref.at[:, row, :, pl.ds(0, 16), :], trial_left.at[row]
+        )
+        for row in range(8)
+    ]
+    for copy in trial_copies:
+        copy.start()
 
     for step in range(HALF // SPAN):
         planes = [step * SPAN + part for part in range(SPAN)]
@@ -311,15 +333,12 @@
     fill = fill_of(far_ref)
 
     def tile_copies(step):
-        copies = []
-        for half in range(2):
-            peers = pl.ds(step * 2 * SPAN + half * NG, 2 * SPAN)
-            copies.append(
-                pltpu.make_async_copy(
-                    tiles.at[peers], out_ref.at[peers, pl.ds(16, 16), :], left.at[half, step]
-                )
+        return [
+            pltpu.make_async_copy(
+                tiles.at[:, row], out_ref.at[:, row, :, pl.ds(16, 16), :], left.at[row]
             )
-        return copies
+            for row in (step, step + 4)
+        ]
 
     for step in range(HALF // SPAN):
         planes = [step * SPAN + part for part in range(SPAN)]
@@ -334,10 +353,11 @@
             second = jnp.where(low, turned[:HALF], total[HALF:])
             for index, value in ((plane, first), (plane + HALF, second)):
                 value = value + term_ref[plane_rows(index, 32), :]
-                tiles[pl.ds(2 * index, 2)] = value.astype(bf16).reshape(2, 16, 128)
+                tiles[index % 8, index // 8] = value.astype(bf16).reshape(2, 16, 128)
         for copy in tile_copies(step):
             copy.start()
-    trial_copy.wait()
+    for copy in trial_copies:
+        copy.wait()
     for step in range(HALF // SPAN):
         for copy in tile_copies(step):
             copy.wait()
@@ -346,15 +366,15 @@
 def exchange_of(far, owner, term, trial, table, mixed, halves, kernel):
     return pl.pallas_call(
         exchange_body,
-        out_shape=jax.ShapeDtypeStruct((128, 32, 128), jnp.bfloat16),
+        out_shape=jax.ShapeDtypeStruct((8, 8, 2, 32, 128), jnp.bfloat16),
         in_specs=[VMEM] * 8,
         out_specs=pl.BlockSpec(memory_space=pltpu.HBM),
         scratch_shapes=[
             pltpu.VMEM((HALF * NG, 128), jnp.bfloat16),
             pltpu.VMEM((HALF * PITCH, 128), jnp.float32),
-            pltpu.VMEM((128, 16, 128), jnp.bfloat16),
-            pltpu.SemaphoreType.DMA,
-            pltpu.SemaphoreType.DMA((2, HALF // SPAN)),
+            pltpu.VMEM((8, 8, 2, 16, 128), jnp.bfloat16),
+            pltpu.SemaphoreType.DMA((8,)),
+            pltpu.SemaphoreType.DMA((8,)),
         ],
         compiler_params=pltpu.CompilerParams(vmem_limit_bytes=24 * 1024 * 1024),
         name="exchange",
@@ -364,13 +384,16 @@
 def unpack_body(tiles_ref, flat_ref, token_ref):
     def part(step, carry):
         columns = pl.ds(pl.multiple_of(step * 16384, 16384), 16384)
-        tiles = [tiles_ref[pl.ds(step * 256 + peer * 32 + 16, 16), :] for peer in range(8)]
+        row, first = lax.div(step, 2), 4 * lax.rem(step, 2)
+        tiles = [
+            tiles_ref[first + peer // 2, row, peer % 2, pl.ds(16, 16), :] for peer in range(8)
+        ]
         value = jnp.concatenate(tiles, axis=0).astype(jnp.float32).reshape(1, 16384)
         flat_ref[0:1, columns] = value.astype(jnp.bfloat16)
         return carry
 
     lax.fori_loop(0, 16, part, 0)
-    token_ref[...] = tiles_ref[pl.ds(0, 16), :]
+    token_ref[...] = tiles_ref[0, 0, 0, pl.ds(0, 16), :]
 
 
 def unpacked(tiles):
@@ -390,7 +413,9 @@
 def intersection_body(tiles_ref, token_ref, core_ref, lines_ref, mine_ref, other_ref, wide):
     bf16 = jnp.bfloat16
     for peer in range(128):
-        wide[pl.ds(peer * WIDE, 32), :] = tiles_ref[pl.ds(peer * 32, 32), :].astype(jnp.float32)
+        orbital = (peer // 2 % 8 * 8 + peer // 16) * 2 + peer % 2
+        rows = pl.ds(orbital * WIDE, 32)
+        wide[rows, :] = tiles_ref[pl.ds(peer * 32, 32), :].astype(jnp.float32)
     total = jnp.zeros((128, 128), jnp.float32)
     for line in range(16):
         trial = wide[pl.ds(line, 128, stride=WIDE), :].astype(bf16)
@@ -473,19 +498,21 @@
 
 def local(orbitals, trial, occupations):
     own = packed_with_flag(orbitals, occupations)
+    far = from_far(own)
+    again = copied(own)
+    near = swapped(again)
+    trial_rows = packed_after(trial, again)
     table, mixed, halves = (jnp.asarray(value) for value in constants())
-    kernel = screened_kernel(own)
-    far, near = from_far(own), swapped(own)
-    trial_rows = packed_after(trial, own)
+    kernel = screened_kernel(again)
     owner, term = near_term(own, near, table, mixed, kernel)
-    trial_tiles = trial_rows.reshape(128, 16, 128)
+    trial_tiles = trial_rows.reshape(8, 8, 2, 16, 128)
     both = exchange_of(far, owner, term, trial_tiles, table, mixed, halves, kernel)
-    tiles = lax.all_to_all(both, BAND, 0, 0, tiled=True)
-    flat, token = unpacked(both.reshape(2 * ROWS, 128))
+    tiles = lax.all_to_all(both.reshape(128, 32, 128), SLABS, 0, 0, tiled=True)
+    flat, token = unpacked(both)
     core = lax.axis_index("core").astype(jnp.int32).reshape(1)
     lines, mine, other = intersection_of(tiles.reshape(2 * ROWS, 128), token, core)
     half = (mine + swapped(other)).astype(jnp.bfloat16)
-    half = summed_over(half, ("y", "x"))
+    half = summed_over(half, ("x", "y"))
     half = summed_over(half, "z")
     return flat, projected_of(lines, half, swapped(half), core)
 

time: 94.9 us -> 94.8 us (level)
  waiting for transfers between devices: 34.7 us -> 29.2 us
  starting transfers between devices: 23.9 us -> 29.1 us
  Pallas kernels: 12.6 us -> 13.8 us
  blocking collectives: 20.6 us -> 19.6 us
    ppermute x3, starting transfers between devices: 6.37 us -> 13.9 us  [swapped(): return lax.ppermute(value, 'core', [(0, 1), (1, 0)])]
    all_to_all x1, starting transfers between devices: 17.5 us -> 12.2 us  [local(): tiles = lax.all_to_all(both.reshape(128, 32, 128), SLABS, 0, 0, tiled=True)]
    ppermute x1, waiting for transfers between devices: 4 us -> 0.01 us  [from_far(): return lax.ppermute(value, BAND, pairs)]
    ppermute x1, starting transfers between devices: 0.01 us -> 3.06 us  [from_far(): return lax.ppermute(value, BAND, pairs)]
    pallas_call x1 -> x2, Pallas kernels: 3.12 us -> 4.29 us  [the longest x1 4.25 us: exchange_of(): pl.pallas_call(exchange_body, out_shape=jax.ShapeDtypeStruct((8, 8, 2, 32...]
    all_to_all x1, waiting for transfers between devices: 28.6 us -> 27.5 us  [local(): tiles = lax.all_to_all(both.reshape(128, 32, 128), SLABS, 0, 0, tiled=True)]
    all_to_all x2, blocking collectives: 20.6 us -> 19.6 us  [summed_over(): tiles = lax.all_to_all(copies, axes, 0, 0, tiled=True)]
  transfers between devices with their start and end apart: 5 -> 5, of which waited for: 4 -> 3; matrix products, arithmetic and copies ran while one was open for 0% -> 0% of each run, Pallas kernels for 8% -> 8%
where the time goes in v7:
time: 94.8 us; the launch traced here: 94.5 us
  waiting for transfers between devices  29.2 us (31%)
  starting transfers between devices  29.1 us (31%)
  blocking collectives  19.6 us (21%)
  Pallas kernels  13.8 us (15%)
  between operations  1.42 us (1%)
  local copies, waits for them, and re-layouts  1.28 us (1%)
    all_to_all x1, waiting for transfers between devices, local(): tiles = lax.all_to_all(both.reshape(128, 32, 128), SLABS, 0, 0, tiled=True)  27.5 us
    all_to_all x2, blocking collectives, summed_over(): tiles = lax.all_to_all(copies, axes, 0, 0, tiled=True)  19.6 us
    ppermute x3, starting transfers between devices, swapped(): return lax.ppermute(value, 'core', [(0, 1), (1, 0)])  13.9 us
    all_to_all x1, starting transfers between devices, local(): tiles = lax.all_to_all(both.reshape(128, 32, 128), SLABS, 0, 0, tiled=True)  12.2 us
    pallas_call x1, Pallas kernels, exchange_of(): pl.pallas_call(exchange_body, out_shape=jax.ShapeDtypeStruct((8, 8, 2, 32...  4.25 us
    pallas_call x1, Pallas kernels, unpacked(): pl.pallas_call(unpack_body, out_shape=(jax.ShapeDtypeStruct((1, G), jnp.b...  3.19 us
    ppermute x1, starting transfers between devices, from_far(): return lax.ppermute(value, BAND, pairs)  3.06 us
    pallas_call x1, Pallas kernels, near_term(): pl.pallas_call(near_body, out_shape=(jax.ShapeDtypeStruct((HALF * NG, 128...  2.93 us
  transfers between devices with their start and end apart: 5, of which 3 were waited for; matrix products, arithmetic and copies ran while one was open for 0% of the time, Pallas kernels for 8%

profile of v7, /device:TPU:1, one launch (start us, length us, event | category | flops | bytes accessed | tf_op | source)
XLA Modules:
  0.0 94.5 jit_solution(6992109398897148460)
XLA Ops:
  1.3 0.0 copy-start
  1.3 1.2 %copy-done = bf16[1,262144]{1,0:T(2,128)(2,1)S(1)} copy-done((bf16[1,262144]{1,0:T(2,128)(2,1)S(1)}, bf16[1,262144]{1,0:T(2,128)(2,1)}, u32[]{:S(2)}) %copy-start) | copy-done | bytes 524312
  2.5 0.0 copy-start.1
  2.5 0.2 pack_flagged.1.tiles_ref.own_ref
  2.7 3.1 %collective-permute-start = (bf16[2064,128]{1,0:T(8,128)(2,1)S(1)}, bf16[2064,128]{1,0:T(8,128)(2,1)S(1)}, u32[]{:S(2)}, u32[]{:S(2)}) collective-permute-start(bf16[2064,128]{1,0:T(8,128)(2,1)S(1)} %pack_flagged.1.tiles_ref.own_ref), channel_id=1, source_target_pairs={{0,127},{1,2},{2,1},{3,4},{4,3},{5,6},{6,5},{7,8},{8,7},{9,10},{10... | collective-permute-start | bytes 1585160 | tf_op jit(solution)/shard_map/ppermute | solution.py:485
  5.8 8.8 %collective-permute-start.1 = (bf16[2064,128]{1,0:T(8,128)(2,1)S(1)}, bf16[2064,128]{1,0:T(8,128)(2,1)S(1)}, u32[]{:S(2)}, u32[]{:S(2)}) collective-permute-start(bf16[2064,128]{1,0:T(8,128)(2,1)S(1)} %again.1.earlier_ref), channel_id=1, source_target_pairs={{0,1},{1,0},{2,3},{3,2},{4,5},{5,4},{6,7},{7,6},{8,9},{9,8},{10,11... | collective-permute-start | bytes 1585160 | tf_op jit(solution)/shard_map/ppermute | solution.py:489
  14.6 0.0 copy-done.1
  14.6 0.1 pack.1
  14.7 0.0 copy-start.2
  14.7 0.0 copy-start.3
  14.7 1.5 %screened_kernel.1.kernel_ref = f32[64,64,128]{2,1,0:T(8,128)S(1)} custom-call(bf16[2064,128]{1,0:T(8,128)(2,1)S(1)} %again.1.earlier_ref), custom_call_target="tpu_custom_call" | custom-call | flops 10000000000 | bytes 2097152 | tf_op jit(solution)/shard_map/screened_kernel/pallas_call | solution.py:64
  16.2 0.0 copy-start.4
  16.2 0.0 collective-permute-done.1.near_ref
  16.3 0.0 copy-done.2
  16.3 0.0 copy-done.3
  16.3 2.9 %near_term.1 = (bf16[2048,128]{1,0:T(8,128)(2,1)S(1)}, f32[2048,128]{1,0:T(8,128)S(1)}) custom-call(bf16[2064,128]{1,0:T(8,128)(2,1)S(1)} %pack_flagged.1.tiles_ref.own_ref, bf16[2064,128]{1,0:T(8,128)(2,1)S(1)} %collective-permute-done.1.near_ref, bf16[256,256]{1,0:T(8,128)(2,1)S(1)} %copy-done.2, bf16[256,256]{1,0:T(8,128)(2,1)S(1)} %copy-done.3, ...), custom_call_target="tpu_custom_call" | custom-call | flops 10000000000 | bytes 4194304 | tf_op jit(solution)/shard_map/near_term/pallas_call | solution.py:265
  19.2 0.0 collective-permute-done.far_ref
  19.2 0.0 copy-done.4
  19.2 4.2 %exchange.1.tiles_ref = bf16[8,8,2,32,128]{4,3,2,1,0:T(8,128)(2,1)} custom-call(bf16[2064,128]{1,0:T(8,128)(2,1)S(1)} %collective-permute-done.far_ref, bf16[2048,128]{1,0:T(8,128)(2,1)S(1)} %get-tuple-element.9.owner_ref, f32[2048,128]{1,0:T(8,128)S(1)} %get-tuple-element.10.term_ref, bf16[8,8,2,16,128]{4,3,2,1,0:T(8,128)(2,1)S(1)} %bitcast.7, ...), custom_call_target="tpu_custom_call" | custom-call | tf_op jit(solution)/shard_map/exchange/pallas_call | solution.py:367
  23.5 12.2 %all-to-all-start = ((bf16[128,32,128]{2,1,0:T(8,128)(2,1)}), bf16[128,32,128]{2,1,0:T(8,128)(2,1)S(1)}, u32[]{:S(2)}, u32[]{:S(2)}) async-start(bf16[128,32,128]{2,1,0:T(8,128)(2,1)} %bitcast.2), calls=%async_computation | async-start | bytes 2097152 | tf_op jit(solution)/shard_map/all_to_all | solution.py:510
  35.7 3.2 %unpack.1 = (bf16[1,262144]{1,0:T(2,128)(2,1)}, bf16[16,128]{1,0:T(8,128)(2,1)S(1)}) custom-call(bf16[8,8,2,32,128]{4,3,2,1,0:T(8,128)(2,1)} %exchange.1.tiles_ref), custom_call_target="tpu_custom_call" | custom-call | tf_op jit(solution)/shard_map/unpack/pallas_call | solution.py:400
  38.9 27.5 %all-to-all-done = bf16[128,32,128]{2,1,0:T(8,128)(2,1)S(1)} async-done(((bf16[128,32,128]{2,1,0:T(8,128)(2,1)}), bf16[128,32,128]{2,1,0:T(8,128)(2,1)S(1)}, u32[]{:S(2)}, u32[]{:S(2)}) %all-to-all-start) | async-done | bytes 1048608 | tf_op jit(solution)/shard_map/all_to_all | solution.py:510
  66.4 0.6 intersection.1
  66.9 2.1 %collective-permute-start.2 = (f32[64,128]{1,0:T(8,128)S(1)}, f32[64,128]{1,0:T(8,128)S(1)}, u32[]{:S(2)}, u32[]{:S(2)}) collective-permute-start(f32[64,128]{1,0:T(8,128)S(1)} %get-tuple-element.15), channel_id=1, source_target_pairs={{0,1},{1,0},{2,3},{3,2},{4,5},{5,4},{6,7},{7,6},{8,9},{9,8},{10,11... | collective-permute-start | bytes 98312 | tf_op jit(solution)/shard_map/ppermute | solution.py:489
  69.0 0.9 collective-permute-done.2
  69.9 9.3 %all_to_all.15 = bf16[8,64,128]{2,1,0:T(8,128)(2,1)S(1)} all-to-all(bf16[8,64,128]{2,1,0:T(8,128)(2,1)S(1)} %broadcast_in_dim.4), channel_id=1, replica_groups=mesh['spin'=2,'y'=4,'x'=2,'z'=8,'core'=2] {'x','y'}, dimensions={0} | all-to-all | bytes 262144 | tf_op jit(solution)/shard_map/all_to_all | solution.py:495
  79.3 10.3 %all_to_all.16 = bf16[8,64,128]{2,1,0:T(8,128)(2,1)S(1)} all-to-all(bf16[8,64,128]{2,1,0:T(8,128)(2,1)S(1)} %broadcast_in_dim.5), channel_id=1, replica_groups=mesh['spin'=2,'y'=4,'x'=2,'z'=8,'core'=2] {'z'}, dimensions={0} | all-to-all | bytes 262144 | tf_op jit(solution)/shard_map/all_to_all | solution.py:495
  89.6 3.0 %collective-permute-start.3 = (bf16[64,128]{1,0:T(8,128)(2,1)S(1)}, bf16[64,128]{1,0:T(8,128)(2,1)S(1)}, u32[]{:S(2)}, u32[]{:S(2)}) collective-permute-start(bf16[64,128]{1,0:T(8,128)(2,1)S(1)} %reduce_sum.25.mine_ref), channel_id=1, source_target_pairs={{0,1},{1,0},{2,3},{3,2},{4,5},{5,4},{6,7},{7,6},{8,9},{9,8},{10,11... | collective-permute-start | bytes 49160 | tf_op jit(solution)/shard_map/ppermute | solution.py:489
  92.6 0.8 collective-permute-done.3.other_ref
  93.5 1.0 %projected.1 = bf16[128,2048]{1,0:T(8,128)(2,1)} custom-call(bf16[2048,128]{1,0:T(8,128)(2,1)S(1)} %get-tuple-element.13.lines_ref, bf16[64,128]{1,0:T(8,128)(2,1)S(1)} %reduce_sum.25.mine_ref, bf16[64,128]{1,0:T(8,128)(2,1)S(1)} %collective-permute-done.3.other_ref, s32[1]{0:T(128)} %bitcast.4.core_ref), custom_call_target="tpu_custom_call" | custom-call | tf_op jit(solution)/shard_map/projected/pallas_call | solution.py:468
  (6 shorter events, 0.1 us)
Async XLA Ops:
  1.3 1.2 %copy-start = (bf16[1,262144]{1,0:T(2,128)(2,1)S(1)}, bf16[1,262144]{1,0:T(2,128)(2,1)}, u32[]{:S(2)}) copy-start(bf16[1,262144]{1,0:T(2,128)(2,1)} %flat_ref.2) | copy-start | bytes 1572868
  2.5 12.1 %copy-start.1 = (bf16[1,262144]{1,0:T(2,128)(2,1)S(1)}, bf16[1,262144]{1,0:T(2,128)(2,1)}, u32[]{:S(2)}) copy-start(bf16[1,262144]{1,0:T(2,128)(2,1)} %flat_ref.3) | copy-start | bytes 1572868
  2.7 16.5 %collective-permute-start = (bf16[2064,128]{1,0:T(8,128)(2,1)S(1)}, bf16[2064,128]{1,0:T(8,128)(2,1)S(1)}, u32[]{:S(2)}, u32[]{:S(2)}) collective-permute-start(bf16[2064,128]{1,0:T(8,128)(2,1)S(1)} %pack_flagged.1.tiles_ref.own_ref), channel_id=1, source_target_pairs={{0,127},{1,2},{2,1},{3,4},{4,3},{5,6},{6,5},{7,8},{8,7},{9,10},{10... | collective-permute-start | bytes 1585160 | tf_op jit(solution)/shard_map/ppermute | solution.py:485
  5.8 10.5 %collective-permute-start.1 = (bf16[2064,128]{1,0:T(8,128)(2,1)S(1)}, bf16[2064,128]{1,0:T(8,128)(2,1)S(1)}, u32[]{:S(2)}, u32[]{:S(2)}) collective-permute-start(bf16[2064,128]{1,0:T(8,128)(2,1)S(1)} %again.1.earlier_ref), channel_id=1, source_target_pairs={{0,1},{1,0},{2,3},{3,2},{4,5},{5,4},{6,7},{7,6},{8,9},{9,8},{10,11... | collective-permute-start | bytes 1585160 | tf_op jit(solution)/shard_map/ppermute | solution.py:489
  14.7 1.6 %copy-start.2 = (bf16[256,256]{1,0:T(8,128)(2,1)S(1)}, bf16[256,256]{1,0:T(8,128)(2,1)}, u32[]{:S(2)}) copy-start(bf16[256,256]{1,0:T(8,128)(2,1)} %constant.14.clone.table_ref) | copy-start | bytes 393220
  14.7 1.6 %copy-start.3 = (bf16[256,256]{1,0:T(8,128)(2,1)S(1)}, bf16[256,256]{1,0:T(8,128)(2,1)}, u32[]{:S(2)}) copy-start(bf16[256,256]{1,0:T(8,128)(2,1)} %constant.15.clone.mixed_ref) | copy-start | bytes 393220
  16.2 3.0 %copy-start.4 = (bf16[256,256]{1,0:T(8,128)(2,1)S(1)}, bf16[256,256]{1,0:T(8,128)(2,1)}, u32[]{:S(2)}) copy-start(bf16[256,256]{1,0:T(8,128)(2,1)} %constant.16.clone.halves_ref) | copy-start | bytes 393220
  23.5 42.9 %all-to-all-start = ((bf16[128,32,128]{2,1,0:T(8,128)(2,1)}), bf16[128,32,128]{2,1,0:T(8,128)(2,1)S(1)}, u32[]{:S(2)}, u32[]{:S(2)}) async-start(bf16[128,32,128]{2,1,0:T(8,128)(2,1)} %bitcast.2), calls=%async_computation | async-start | bytes 2097152 | tf_op jit(solution)/shard_map/all_to_all | solution.py:510
  66.9 2.9 %collective-permute-start.2 = (f32[64,128]{1,0:T(8,128)S(1)}, f32[64,128]{1,0:T(8,128)S(1)}, u32[]{:S(2)}, u32[]{:S(2)}) collective-permute-start(f32[64,128]{1,0:T(8,128)S(1)} %get-tuple-element.15), channel_id=1, source_target_pairs={{0,1},{1,0},{2,3},{3,2},{4,5},{5,4},{6,7},{7,6},{8,9},{9,8},{10,11... | collective-permute-start | bytes 98312 | tf_op jit(solution)/shard_map/ppermute | solution.py:489
  89.6 3.8 %collective-permute-start.3 = (bf16[64,128]{1,0:T(8,128)(2,1)S(1)}, bf16[64,128]{1,0:T(8,128)(2,1)S(1)}, u32[]{:S(2)}, u32[]{:S(2)}) collective-permute-start(bf16[64,128]{1,0:T(8,128)(2,1)S(1)} %reduce_sum.25.mine_ref), channel_id=1, source_target_pairs={{0,1},{1,0},{2,3},{3,2},{4,5},{5,4},{6,7},{7,6},{8,9},{9,8},{10,11... | collective-permute-start | bytes 49160 | tf_op jit(solution)/shard_map/ppermute | solution.py:489

commit v8 on v6

--- a/solution.py
+++ b/solution.py
@@ -107,19 +107,38 @@
     tiles_ref[pl.ds(ROWS, 16), :] = flag.astype(jnp.float32).astype(jnp.bfloat16)
 
 
-def pack_after_body(flat_ref, earlier_ref, tiles_ref):
-    pack_body(flat_ref, tiles_ref)
+def pack_after_body(flat_ref, earlier_ref, both_ref):
+    both_ref[...] = flat_ref[...].reshape(256, 128).reshape(16, 16, 128)
 
 
 def packed_after(flat, earlier):
     return pl.pallas_call(
         pack_after_body,
-        out_shape=jax.ShapeDtypeStruct((ROWS, 128), jnp.bfloat16),
-        in_specs=[VMEM, pl.BlockSpec(memory_space=pl.ANY)],
-        out_specs=VMEM,
+        grid=(8,),
+        out_shape=jax.ShapeDtypeStruct((128, 32, 128), jnp.bfloat16),
+        in_specs=[
+            pl.BlockSpec((1, G // 8), lambda part: (0, part)),
+            pl.BlockSpec(memory_space=pl.ANY),
+        ],
+        out_specs=pl.BlockSpec((16, 16, 128), lambda part: (part, 0, 0)),
         compiler_params=pltpu.CompilerParams(vmem_limit_bytes=16 * 1024 * 1024),
         name="pack",
     )(flat, earlier)
+
+
+def again_body(tiles_ref, again_ref):
+    again_ref[...] = tiles_ref[...]
+
+
+def copied(tiles):
+    return pl.pallas_call(
+        again_body,
+        out_shape=jax.ShapeDtypeStruct(tiles.shape, tiles.dtype),
+        in_specs=[VMEM],
+        out_specs=VMEM,
+        compiler_params=pltpu.CompilerParams(vmem_limit_bytes=16 * 1024 * 1024),
+        name="again",
+    )(tiles)
 
 
 def packed_with_flag(flat, flag):
@@ -267,13 +286,11 @@
 
 
 def exchange_body(
-    far_ref, owner_ref, term_ref, trial_ref, table_ref, mixed_ref, halves_ref, kernel_ref,
-    out_ref, visitors, grid, tiles, trial_left, left,
+    far_ref, owner_ref, term_ref, both_ref, table_ref, mixed_ref, halves_ref, kernel_ref,
+    out_ref, visitors, grid, tiles, left,
 ):
     f32, bf16 = jnp.float32, jnp.bfloat16
     low = low_lanes(HALF)
-    trial_copy = pltpu.make_async_copy(trial_ref, out_ref.at[:, pl.ds(0, 16), :], trial_left)
-    trial_copy.start()
 
     for step in range(HALF // SPAN):
         planes = [step * SPAN + part for part in range(SPAN)]
@@ -337,28 +354,27 @@
                 tiles[pl.ds(2 * index, 2)] = value.astype(bf16).reshape(2, 16, 128)
         for copy in tile_copies(step):
             copy.start()
-    trial_copy.wait()
     for step in range(HALF // SPAN):
         for copy in tile_copies(step):
             copy.wait()
 
 
-def exchange_of(far, owner, term, trial, table, mixed, halves, kernel):
+def exchange_of(far, owner, term, both, table, mixed, halves, kernel):
     return pl.pallas_call(
         exchange_body,
         out_shape=jax.ShapeDtypeStruct((128, 32, 128), jnp.bfloat16),
-        in_specs=[VMEM] * 8,
+        in_specs=[VMEM] * 3 + [pl.BlockSpec(memory_space=pltpu.HBM)] + [VMEM] * 4,
         out_specs=pl.BlockSpec(memory_space=pltpu.HBM),
+        input_output_aliases={3: 0},
         scratch_shapes=[
             pltpu.VMEM((HALF * NG, 128), jnp.bfloat16),
             pltpu.VMEM((HALF * PITCH, 128), jnp.float32),
             pltpu.VMEM((128, 16, 128), jnp.bfloat16),
-            pltpu.SemaphoreType.DMA,
             pltpu.SemaphoreType.DMA((2, HALF // SPAN)),
         ],
         compiler_params=pltpu.CompilerParams(vmem_limit_bytes=24 * 1024 * 1024),
         name="exchange",
-    )(far, owner, term, trial, table, mixed, halves, kernel)
+    )(far, owner, term, both, table, mixed, halves, kernel)
 
 
 def unpack_body(tiles_ref, flat_ref, token_ref):
@@ -473,19 +489,20 @@
 
 def local(orbitals, trial, occupations):
     own = packed_with_flag(orbitals, occupations)
+    far = from_far(own)
+    again = copied(own)
+    near = swapped(again)
     table, mixed, halves = (jnp.asarray(value) for value in constants())
-    kernel = screened_kernel(own)
-    far, near = from_far(own), swapped(own)
-    trial_rows = packed_after(trial, own)
+    kernel = screened_kernel(again)
+    both = packed_after(trial, kernel)
     owner, term = near_term(own, near, table, mixed, kernel)
-    trial_tiles = trial_rows.reshape(128, 16, 128)
-    both = exchange_of(far, owner, term, trial_tiles, table, mixed, halves, kernel)
+    both = exchange_of(far, owner, term, both, table, mixed, halves, kernel)
     tiles = lax.all_to_all(both, BAND, 0, 0, tiled=True)
     flat, token = unpacked(both.reshape(2 * ROWS, 128))
     core = lax.axis_index("core").astype(jnp.int32).reshape(1)
     lines, mine, other = intersection_of(tiles.reshape(2 * ROWS, 128), token, core)
     half = (mine + swapped(other)).astype(jnp.bfloat16)
-    half = summed_over(half, ("y", "x"))
+    half = summed_over(half, ("x", "y"))
     half = summed_over(half, "z")
     return flat, projected_of(lines, half, swapped(half), core)
 

time: 94.9 us -> 94 us (level)
  waiting for transfers between devices: 34.7 us -> 30.7 us
  Pallas kernels: 12.6 us -> 15.1 us
    all_to_all x1, starting transfers between devices: 17.5 us -> 9.71 us  [local(): tiles = lax.all_to_all(both, BAND, 0, 0, tiled=True)]
    ppermute x3, starting transfers between devices: 6.37 us -> 11.9 us  [swapped(): return lax.ppermute(value, 'core', [(0, 1), (1, 0)])]
    ppermute x1, waiting for transfers between devices: 4 us -> 0.01 us  [from_far(): return lax.ppermute(value, BAND, pairs)]
    ppermute x1, starting transfers between devices: 0.01 us -> 3.06 us  [from_far(): return lax.ppermute(value, BAND, pairs)]
    pallas_call x1 -> x2, Pallas kernels: 0.13 us -> 2.68 us  [the longest x1 2.64 us: packed_after(): pl.pallas_call(pack_after_body, grid=(8,), out_shape=jax.ShapeDtypeStruct...]
  transfers between devices with their start and end apart: 5 -> 5, of which waited for: 4 -> 3; matrix products, arithmetic and copies ran while one was open for 0% -> 0% of each run, Pallas kernels for 8% -> 11%
where the time goes in v8:
time: 94 us; the launch traced here: 93.7 us
  waiting for transfers between devices  30.7 us (33%)
  starting transfers between devices  24.6 us (26%)
  blocking collectives  20.5 us (22%)
  Pallas kernels  15.1 us (16%)
  between operations  1.42 us (2%)
  local copies, waits for them, and re-layouts  1.28 us (1%)
    all_to_all x1, waiting for transfers between devices, local(): tiles = lax.all_to_all(both, BAND, 0, 0, tiled=True)  28.6 us
    all_to_all x2, blocking collectives, summed_over(): tiles = lax.all_to_all(copies, axes, 0, 0, tiled=True)  20.5 us
    ppermute x3, starting transfers between devices, swapped(): return lax.ppermute(value, 'core', [(0, 1), (1, 0)])  11.9 us
    all_to_all x1, starting transfers between devices, local(): tiles = lax.all_to_all(both, BAND, 0, 0, tiled=True)  9.71 us
    pallas_call x1, Pallas kernels, unpacked(): pl.pallas_call(unpack_body, out_shape=(jax.ShapeDtypeStruct((1, G), jnp.b...  3.15 us
    pallas_call x1, Pallas kernels, exchange_of(): pl.pallas_call(exchange_body, out_shape=jax.ShapeDtypeStruct((128, 32, 12...  3.12 us
    ppermute x1, starting transfers between devices, from_far(): return lax.ppermute(value, BAND, pairs)  3.06 us
    pallas_call x1, Pallas kernels, near_term(): pl.pallas_call(near_body, out_shape=(jax.ShapeDtypeStruct((HALF * NG, 128...  2.92 us
  transfers between devices with their start and end apart: 5, of which 3 were waited for; matrix products, arithmetic and copies ran while one was open for 0% of the time, Pallas kernels for 11%

profile of v8, /device:TPU:1, one launch (start us, length us, event | category | flops | bytes accessed | tf_op | source)
XLA Modules:
  0.0 93.7 jit_solution(13225093924627859533)
XLA Ops:
  1.3 0.0 copy-start
  1.3 1.2 %copy-done = bf16[1,262144]{1,0:T(2,128)(2,1)S(1)} copy-done((bf16[1,262144]{1,0:T(2,128)(2,1)S(1)}, bf16[1,262144]{1,0:T(2,128)(2,1)}, u32[]{:S(2)}) %copy-start) | copy-done | bytes 524312
  2.5 0.2 pack_flagged.1.tiles_ref.own_ref
  2.7 3.1 %collective-permute-start = (bf16[2064,128]{1,0:T(8,128)(2,1)S(1)}, bf16[2064,128]{1,0:T(8,128)(2,1)S(1)}, u32[]{:S(2)}, u32[]{:S(2)}) collective-permute-start(bf16[2064,128]{1,0:T(8,128)(2,1)S(1)} %pack_flagged.1.tiles_ref.own_ref), channel_id=1, source_target_pairs={{0,127},{1,2},{2,1},{3,4},{4,3},{5,6},{6,5},{7,8},{8,7},{9,10},{10... | collective-permute-start | bytes 1585160 | tf_op jit(solution)/shard_map/ppermute | solution.py:476
  5.8 0.0 copy-start.1
  5.8 8.8 %collective-permute-start.1 = (bf16[2064,128]{1,0:T(8,128)(2,1)S(1)}, bf16[2064,128]{1,0:T(8,128)(2,1)S(1)}, u32[]{:S(2)}, u32[]{:S(2)}) collective-permute-start(bf16[2064,128]{1,0:T(8,128)(2,1)S(1)} %again.1.earlier_ref), channel_id=1, source_target_pairs={{0,1},{1,0},{2,3},{3,2},{4,5},{5,4},{6,7},{7,6},{8,9},{9,8},{10,11... | collective-permute-start | bytes 1585160 | tf_op jit(solution)/shard_map/ppermute | solution.py:480
  14.6 1.5 %screened_kernel.1.kernel_ref.earlier_ref = f32[64,64,128]{2,1,0:T(8,128)S(1)} custom-call(bf16[2064,128]{1,0:T(8,128)(2,1)S(1)} %again.1.earlier_ref), custom_call_target="tpu_custom_call" | custom-call | flops 10000000000 | bytes 2097152 | tf_op jit(solution)/shard_map/screened_kernel/pallas_call | solution.py:63
  16.1 0.0 copy-done.1
  16.1 0.0 copy-start.2
  16.1 0.0 copy-start.3
  16.1 2.6 %pack.1.both_ref = bf16[128,32,128]{2,1,0:T(8,128)(2,1)} custom-call(bf16[1,262144]{1,0:T(2,128)(2,1)S(1)} %copy-done.1, f32[64,64,128]{2,1,0:T(8,128)S(1)} %screened_kernel.1.kernel_ref.earlier_ref), custom_call_target="tpu_custom_call" | custom-call | tf_op jit(solution)/shard_map/pack/pallas_call | solution.py:115
  18.8 0.0 copy-start.4
  18.8 0.0 collective-permute-done.1.near_ref
  18.8 0.0 copy-done.2
  18.8 0.0 copy-done.3
  18.8 2.9 %near_term.1 = (bf16[2048,128]{1,0:T(8,128)(2,1)S(1)}, f32[2048,128]{1,0:T(8,128)S(1)}) custom-call(bf16[2064,128]{1,0:T(8,128)(2,1)S(1)} %pack_flagged.1.tiles_ref.own_ref, bf16[2064,128]{1,0:T(8,128)(2,1)S(1)} %collective-permute-done.1.near_ref, bf16[256,256]{1,0:T(8,128)(2,1)S(1)} %copy-done.2, bf16[256,256]{1,0:T(8,128)(2,1)S(1)} %copy-done.3, ...), custom_call_target="tpu_custom_call" | custom-call | flops 10000000000 | bytes 4194304 | tf_op jit(solution)/shard_map/near_term/pallas_call | solution.py:268
  21.7 0.0 collective-permute-done.far_ref
  21.7 0.0 copy-done.4
  21.7 3.1 %exchange.1 = bf16[128,32,128]{2,1,0:T(8,128)(2,1)} custom-call(bf16[2064,128]{1,0:T(8,128)(2,1)S(1)} %collective-permute-done.far_ref, bf16[2048,128]{1,0:T(8,128)(2,1)S(1)} %get-tuple-element.9.owner_ref, f32[2048,128]{1,0:T(8,128)S(1)} %get-tuple-element.10.term_ref, bf16[128,32,128]{2,1,0:T(8,128)(2,1)} %pack.1.both_ref, ...), custom_call_target="tpu_custom_call", output_to_operand_aliasing={{}: (3, {})} | custom-call | tf_op jit(solution)/shard_map/exchange/pallas_call | solution.py:363
  24.9 9.7 %all-to-all-start = ((bf16[128,32,128]{2,1,0:T(8,128)(2,1)}), bf16[128,32,128]{2,1,0:T(8,128)(2,1)S(1)}, u32[]{:S(2)}, u32[]{:S(2)}) async-start(bf16[128,32,128]{2,1,0:T(8,128)(2,1)} %exchange.1), calls=%async_computation | async-start | bytes 2097152 | tf_op jit(solution)/shard_map/all_to_all | solution.py:500
  34.6 3.1 %unpack.1 = (bf16[1,262144]{1,0:T(2,128)(2,1)}, bf16[16,128]{1,0:T(8,128)(2,1)S(1)}) custom-call(bf16[4096,128]{1,0:T(8,128)(2,1)} %bitcast.1.tiles_ref), custom_call_target="tpu_custom_call" | custom-call | tf_op jit(solution)/shard_map/unpack/pallas_call | solution.py:393
  37.7 28.6 %all-to-all-done = bf16[128,32,128]{2,1,0:T(8,128)(2,1)S(1)} async-done(((bf16[128,32,128]{2,1,0:T(8,128)(2,1)}), bf16[128,32,128]{2,1,0:T(8,128)(2,1)S(1)}, u32[]{:S(2)}, u32[]{:S(2)}) %all-to-all-start) | async-done | bytes 1048608 | tf_op jit(solution)/shard_map/all_to_all | solution.py:500
  66.4 0.6 intersection.1
  66.9 0.1 collective-permute-start.2
  67.0 1.2 %collective-permute-done.2 = f32[64,128]{1,0:T(8,128)S(1)} collective-permute-done((f32[64,128]{1,0:T(8,128)S(1)}, f32[64,128]{1,0:T(8,128)S(1)}, u32[]{:S(2)}, u32[]{:S(2)}) %collective-permute-start.2) | collective-permute-done | bytes 32800 | tf_op jit(solution)/shard_map/ppermute | solution.py:480
  68.3 9.9 %all_to_all.15 = bf16[8,64,128]{2,1,0:T(8,128)(2,1)S(1)} all-to-all(bf16[8,64,128]{2,1,0:T(8,128)(2,1)S(1)} %broadcast_in_dim.4), channel_id=1, replica_groups=mesh['spin'=2,'y'=4,'x'=2,'z'=8,'core'=2] {'x','y'}, dimensions={0} | all-to-all | bytes 262144 | tf_op jit(solution)/shard_map/all_to_all | solution.py:486
  78.3 10.6 %all_to_all.16 = bf16[8,64,128]{2,1,0:T(8,128)(2,1)S(1)} all-to-all(bf16[8,64,128]{2,1,0:T(8,128)(2,1)S(1)} %broadcast_in_dim.5), channel_id=1, replica_groups=mesh['spin'=2,'y'=4,'x'=2,'z'=8,'core'=2] {'z'}, dimensions={0} | all-to-all | bytes 262144 | tf_op jit(solution)/shard_map/all_to_all | solution.py:486
  88.9 3.0 %collective-permute-start.3 = (bf16[64,128]{1,0:T(8,128)(2,1)S(1)}, bf16[64,128]{1,0:T(8,128)(2,1)S(1)}, u32[]{:S(2)}, u32[]{:S(2)}) collective-permute-start(bf16[64,128]{1,0:T(8,128)(2,1)S(1)} %reduce_sum.25.mine_ref), channel_id=1, source_target_pairs={{0,1},{1,0},{2,3},{3,2},{4,5},{5,4},{6,7},{7,6},{8,9},{9,8},{10,11... | collective-permute-start | bytes 49160 | tf_op jit(solution)/shard_map/ppermute | solution.py:480
  91.9 0.8 collective-permute-done.3.other_ref
  92.7 1.0 %projected.1 = bf16[128,2048]{1,0:T(8,128)(2,1)} custom-call(bf16[2048,128]{1,0:T(8,128)(2,1)S(1)} %get-tuple-element.13.lines_ref, bf16[64,128]{1,0:T(8,128)(2,1)S(1)} %reduce_sum.25.mine_ref, bf16[64,128]{1,0:T(8,128)(2,1)S(1)} %collective-permute-done.3.other_ref, s32[1]{0:T(128)} %bitcast.3.core_ref), custom_call_target="tpu_custom_call" | custom-call | tf_op jit(solution)/shard_map/projected/pallas_call | solution.py:459
  (6 shorter events, 0.1 us)
Async XLA Ops:
  1.3 1.2 %copy-start = (bf16[1,262144]{1,0:T(2,128)(2,1)S(1)}, bf16[1,262144]{1,0:T(2,128)(2,1)}, u32[]{:S(2)}) copy-start(bf16[1,262144]{1,0:T(2,128)(2,1)} %flat_ref.2) | copy-start | bytes 1572868
  2.7 19.0 %collective-permute-start = (bf16[2064,128]{1,0:T(8,128)(2,1)S(1)}, bf16[2064,128]{1,0:T(8,128)(2,1)S(1)}, u32[]{:S(2)}, u32[]{:S(2)}) collective-permute-start(bf16[2064,128]{1,0:T(8,128)(2,1)S(1)} %pack_flagged.1.tiles_ref.own_ref), channel_id=1, source_target_pairs={{0,127},{1,2},{2,1},{3,4},{4,3},{5,6},{6,5},{7,8},{8,7},{9,10},{10... | collective-permute-start | bytes 1585160 | tf_op jit(solution)/shard_map/ppermute | solution.py:476
  5.8 10.3 %copy-start.1 = (bf16[1,262144]{1,0:T(2,128)(2,1)S(1)}, bf16[1,262144]{1,0:T(2,128)(2,1)}, u32[]{:S(2)}) copy-start(bf16[1,262144]{1,0:T(2,128)(2,1)} %flat_ref.3) | copy-start | bytes 1572868
  5.8 13.0 %collective-permute-start.1 = (bf16[2064,128]{1,0:T(8,128)(2,1)S(1)}, bf16[2064,128]{1,0:T(8,128)(2,1)S(1)}, u32[]{:S(2)}, u32[]{:S(2)}) collective-permute-start(bf16[2064,128]{1,0:T(8,128)(2,1)S(1)} %again.1.earlier_ref), channel_id=1, source_target_pairs={{0,1},{1,0},{2,3},{3,2},{4,5},{5,4},{6,7},{7,6},{8,9},{9,8},{10,11... | collective-permute-start | bytes 1585160 | tf_op jit(solution)/shard_map/ppermute | solution.py:480
  16.1 2.7 %copy-start.2 = (bf16[256,256]{1,0:T(8,128)(2,1)S(1)}, bf16[256,256]{1,0:T(8,128)(2,1)}, u32[]{:S(2)}) copy-start(bf16[256,256]{1,0:T(8,128)(2,1)} %constant.14.clone.table_ref) | copy-start | bytes 393220
  16.1 2.7 %copy-start.3 = (bf16[256,256]{1,0:T(8,128)(2,1)S(1)}, bf16[256,256]{1,0:T(8,128)(2,1)}, u32[]{:S(2)}) copy-start(bf16[256,256]{1,0:T(8,128)(2,1)} %constant.15.clone.mixed_ref) | copy-start | bytes 393220
  18.8 3.0 %copy-start.4 = (bf16[256,256]{1,0:T(8,128)(2,1)S(1)}, bf16[256,256]{1,0:T(8,128)(2,1)}, u32[]{:S(2)}) copy-start(bf16[256,256]{1,0:T(8,128)(2,1)} %constant.16.clone.halves_ref) | copy-start | bytes 393220
  24.9 41.5 %all-to-all-start = ((bf16[128,32,128]{2,1,0:T(8,128)(2,1)}), bf16[128,32,128]{2,1,0:T(8,128)(2,1)S(1)}, u32[]{:S(2)}, u32[]{:S(2)}) async-start(bf16[128,32,128]{2,1,0:T(8,128)(2,1)} %exchange.1), calls=%async_computation | async-start | bytes 2097152 | tf_op jit(solution)/shard_map/all_to_all | solution.py:500
  66.9 1.3 %collective-permute-start.2 = (f32[64,128]{1,0:T(8,128)S(1)}, f32[64,128]{1,0:T(8,128)S(1)}, u32[]{:S(2)}, u32[]{:S(2)}) collective-permute-start(f32[64,128]{1,0:T(8,128)S(1)} %get-tuple-element.15), channel_id=1, source_target_pairs={{0,1},{1,0},{2,3},{3,2},{4,5},{5,4},{6,7},{7,6},{8,9},{9,8},{10,11... | collective-permute-start | bytes 98312 | tf_op jit(solution)/shard_map/ppermute | solution.py:480
  88.9 3.8 %collective-permute-start.3 = (bf16[64,128]{1,0:T(8,128)(2,1)S(1)}, bf16[64,128]{1,0:T(8,128)(2,1)S(1)}, u32[]{:S(2)}, u32[]{:S(2)}) collective-permute-start(bf16[64,128]{1,0:T(8,128)(2,1)S(1)} %reduce_sum.25.mine_ref), channel_id=1, source_target_pairs={{0,1},{1,0},{2,3},{3,2},{4,5},{5,4},{6,7},{7,6},{8,9},{9,8},{10,11... | collective-permute-start | bytes 49160 | tf_op jit(solution)/shard_map/ppermute | solution.py:480

commit v9 on v8

--- a/solution.py
+++ b/solution.py
@@ -502,8 +502,8 @@
     core = lax.axis_index("core").astype(jnp.int32).reshape(1)
     lines, mine, other = intersection_of(tiles.reshape(2 * ROWS, 128), token, core)
     half = (mine + swapped(other)).astype(jnp.bfloat16)
+    half = summed_over(half, "z")
     half = summed_over(half, ("x", "y"))
-    half = summed_over(half, "z")
     return flat, projected_of(lines, half, swapped(half), core)
 
 

time: 94 us -> 94.4 us (level)
  no operation moved by 1% of the time
where the time goes in v9:
time: 94.4 us; the launch traced here: 94 us
  waiting for transfers between devices  30.7 us (33%)
  starting transfers between devices  24.9 us (26%)
  blocking collectives  20.6 us (22%)
  Pallas kernels  15.1 us (16%)
  between operations  1.42 us (2%)
  local copies, waits for them, and re-layouts  1.28 us (1%)
    all_to_all x1, waiting for transfers between devices, local(): tiles = lax.all_to_all(both, BAND, 0, 0, tiled=True)  28.6 us
    all_to_all x2, blocking collectives, summed_over(): tiles = lax.all_to_all(copies, axes, 0, 0, tiled=True)  20.6 us
    ppermute x3, starting transfers between devices, swapped(): return lax.ppermute(value, 'core', [(0, 1), (1, 0)])  12.1 us
    all_to_all x1, starting transfers between devices, local(): tiles = lax.all_to_all(both, BAND, 0, 0, tiled=True)  9.71 us
    pallas_call x1, Pallas kernels, unpacked(): pl.pallas_call(unpack_body, out_shape=(jax.ShapeDtypeStruct((1, G), jnp.b...  3.15 us
    pallas_call x1, Pallas kernels, exchange_of(): pl.pallas_call(exchange_body, out_shape=jax.ShapeDtypeStruct((128, 32, 12...  3.12 us
    ppermute x1, starting transfers between devices, from_far(): return lax.ppermute(value, BAND, pairs)  3.06 us
    pallas_call x1, Pallas kernels, near_term(): pl.pallas_call(near_body, out_shape=(jax.ShapeDtypeStruct((HALF * NG, 128...  2.92 us
  transfers between devices with their start and end apart: 5, of which 3 were waited for; matrix products, arithmetic and copies ran while one was open for 0% of the time, Pallas kernels for 11%

profile of v9, /device:TPU:1, one launch (start us, length us, event | category | flops | bytes accessed | tf_op | source)
XLA Modules:
  0.0 94.0 jit_solution(6231982943301872975)
XLA Ops:
  1.3 0.0 copy-start
  1.3 1.2 %copy-done = bf16[1,262144]{1,0:T(2,128)(2,1)S(1)} copy-done((bf16[1,262144]{1,0:T(2,128)(2,1)S(1)}, bf16[1,262144]{1,0:T(2,128)(2,1)}, u32[]{:S(2)}) %copy-start) | copy-done | bytes 524312
  2.5 0.2 pack_flagged.1.tiles_ref.own_ref
  2.7 3.1 %collective-permute-start = (bf16[2064,128]{1,0:T(8,128)(2,1)S(1)}, bf16[2064,128]{1,0:T(8,128)(2,1)S(1)}, u32[]{:S(2)}, u32[]{:S(2)}) collective-permute-start(bf16[2064,128]{1,0:T(8,128)(2,1)S(1)} %pack_flagged.1.tiles_ref.own_ref), channel_id=1, source_target_pairs={{0,127},{1,2},{2,1},{3,4},{4,3},{5,6},{6,5},{7,8},{8,7},{9,10},{10... | collective-permute-start | bytes 1585160 | tf_op jit(solution)/shard_map/ppermute | solution.py:476
  5.8 0.0 copy-start.1
  5.8 8.8 %collective-permute-start.1 = (bf16[2064,128]{1,0:T(8,128)(2,1)S(1)}, bf16[2064,128]{1,0:T(8,128)(2,1)S(1)}, u32[]{:S(2)}, u32[]{:S(2)}) collective-permute-start(bf16[2064,128]{1,0:T(8,128)(2,1)S(1)} %again.1.earlier_ref), channel_id=1, source_target_pairs={{0,1},{1,0},{2,3},{3,2},{4,5},{5,4},{6,7},{7,6},{8,9},{9,8},{10,11... | collective-permute-start | bytes 1585160 | tf_op jit(solution)/shard_map/ppermute | solution.py:480
  14.6 1.5 %screened_kernel.1.kernel_ref.earlier_ref = f32[64,64,128]{2,1,0:T(8,128)S(1)} custom-call(bf16[2064,128]{1,0:T(8,128)(2,1)S(1)} %again.1.earlier_ref), custom_call_target="tpu_custom_call" | custom-call | flops 10000000000 | bytes 2097152 | tf_op jit(solution)/shard_map/screened_kernel/pallas_call | solution.py:63
  16.1 0.0 copy-done.1
  16.1 0.0 copy-start.2
  16.1 0.0 copy-start.3
  16.1 2.6 %pack.1.both_ref = bf16[128,32,128]{2,1,0:T(8,128)(2,1)} custom-call(bf16[1,262144]{1,0:T(2,128)(2,1)S(1)} %copy-done.1, f32[64,64,128]{2,1,0:T(8,128)S(1)} %screened_kernel.1.kernel_ref.earlier_ref), custom_call_target="tpu_custom_call" | custom-call | tf_op jit(solution)/shard_map/pack/pallas_call | solution.py:115
  18.8 0.0 copy-start.4
  18.8 0.0 collective-permute-done.1.near_ref
  18.8 0.0 copy-done.2
  18.8 0.0 copy-done.3
  18.8 2.9 %near_term.1 = (bf16[2048,128]{1,0:T(8,128)(2,1)S(1)}, f32[2048,128]{1,0:T(8,128)S(1)}) custom-call(bf16[2064,128]{1,0:T(8,128)(2,1)S(1)} %pack_flagged.1.tiles_ref.own_ref, bf16[2064,128]{1,0:T(8,128)(2,1)S(1)} %collective-permute-done.1.near_ref, bf16[256,256]{1,0:T(8,128)(2,1)S(1)} %copy-done.2, bf16[256,256]{1,0:T(8,128)(2,1)S(1)} %copy-done.3, ...), custom_call_target="tpu_custom_call" | custom-call | flops 10000000000 | bytes 4194304 | tf_op jit(solution)/shard_map/near_term/pallas_call | solution.py:268
  21.7 0.0 collective-permute-done.far_ref
  21.7 0.0 copy-done.4
  21.7 3.1 %exchange.1 = bf16[128,32,128]{2,1,0:T(8,128)(2,1)} custom-call(bf16[2064,128]{1,0:T(8,128)(2,1)S(1)} %collective-permute-done.far_ref, bf16[2048,128]{1,0:T(8,128)(2,1)S(1)} %get-tuple-element.9.owner_ref, f32[2048,128]{1,0:T(8,128)S(1)} %get-tuple-element.10.term_ref, bf16[128,32,128]{2,1,0:T(8,128)(2,1)} %pack.1.both_ref, ...), custom_call_target="tpu_custom_call", output_to_operand_aliasing={{}: (3, {})} | custom-call | tf_op jit(solution)/shard_map/exchange/pallas_call | solution.py:363
  24.9 9.7 %all-to-all-start = ((bf16[128,32,128]{2,1,0:T(8,128)(2,1)}), bf16[128,32,128]{2,1,0:T(8,128)(2,1)S(1)}, u32[]{:S(2)}, u32[]{:S(2)}) async-start(bf16[128,32,128]{2,1,0:T(8,128)(2,1)} %exchange.1), calls=%async_computation | async-start | bytes 2097152 | tf_op jit(solution)/shard_map/all_to_all | solution.py:500
  34.6 3.1 %unpack.1 = (bf16[1,262144]{1,0:T(2,128)(2,1)}, bf16[16,128]{1,0:T(8,128)(2,1)S(1)}) custom-call(bf16[4096,128]{1,0:T(8,128)(2,1)} %bitcast.1.tiles_ref), custom_call_target="tpu_custom_call" | custom-call | tf_op jit(solution)/shard_map/unpack/pallas_call | solution.py:393
  37.7 28.6 %all-to-all-done = bf16[128,32,128]{2,1,0:T(8,128)(2,1)S(1)} async-done(((bf16[128,32,128]{2,1,0:T(8,128)(2,1)}), bf16[128,32,128]{2,1,0:T(8,128)(2,1)S(1)}, u32[]{:S(2)}, u32[]{:S(2)}) %all-to-all-start) | async-done | bytes 1048608 | tf_op jit(solution)/shard_map/all_to_all | solution.py:500
  66.4 0.6 intersection.1
  66.9 0.1 collective-permute-start.2
  67.0 1.2 %collective-permute-done.2 = f32[64,128]{1,0:T(8,128)S(1)} collective-permute-done((f32[64,128]{1,0:T(8,128)S(1)}, f32[64,128]{1,0:T(8,128)S(1)}, u32[]{:S(2)}, u32[]{:S(2)}) %collective-permute-start.2) | collective-permute-done | bytes 32800 | tf_op jit(solution)/shard_map/ppermute | solution.py:480
  68.3 11.2 %all_to_all.15 = bf16[8,64,128]{2,1,0:T(8,128)(2,1)S(1)} all-to-all(bf16[8,64,128]{2,1,0:T(8,128)(2,1)S(1)} %broadcast_in_dim.4), channel_id=1, replica_groups=mesh['spin'=2,'y'=4,'x'=2,'z'=8,'core'=2] {'z'}, dimensions={0} | all-to-all | bytes 262144 | tf_op jit(solution)/shard_map/all_to_all | solution.py:486
  79.5 9.4 %all_to_all.16 = bf16[8,64,128]{2,1,0:T(8,128)(2,1)S(1)} all-to-all(bf16[8,64,128]{2,1,0:T(8,128)(2,1)S(1)} %broadcast_in_dim.5), channel_id=1, replica_groups=mesh['spin'=2,'y'=4,'x'=2,'z'=8,'core'=2] {'x','y'}, dimensions={0} | all-to-all | bytes 262144 | tf_op jit(solution)/shard_map/all_to_all | solution.py:486
  89.0 3.2 %collective-permute-start.3 = (bf16[64,128]{1,0:T(8,128)(2,1)S(1)}, bf16[64,128]{1,0:T(8,128)(2,1)S(1)}, u32[]{:S(2)}, u32[]{:S(2)}) collective-permute-start(bf16[64,128]{1,0:T(8,128)(2,1)S(1)} %reduce_sum.25.mine_ref), channel_id=1, source_target_pairs={{0,1},{1,0},{2,3},{3,2},{4,5},{5,4},{6,7},{7,6},{8,9},{9,8},{10,11... | collective-permute-start | bytes 49160 | tf_op jit(solution)/shard_map/ppermute | solution.py:480
  92.2 0.8 collective-permute-done.3.other_ref
  93.0 1.0 %projected.1 = bf16[128,2048]{1,0:T(8,128)(2,1)} custom-call(bf16[2048,128]{1,0:T(8,128)(2,1)S(1)} %get-tuple-element.13.lines_ref, bf16[64,128]{1,0:T(8,128)(2,1)S(1)} %reduce_sum.25.mine_ref, bf16[64,128]{1,0:T(8,128)(2,1)S(1)} %collective-permute-done.3.other_ref, s32[1]{0:T(128)} %bitcast.3.core_ref), custom_call_target="tpu_custom_call" | custom-call | tf_op jit(solution)/shard_map/projected/pallas_call | solution.py:459
  (6 shorter events, 0.1 us)
Async XLA Ops:
  1.3 1.2 %copy-start = (bf16[1,262144]{1,0:T(2,128)(2,1)S(1)}, bf16[1,262144]{1,0:T(2,128)(2,1)}, u32[]{:S(2)}) copy-start(bf16[1,262144]{1,0:T(2,128)(2,1)} %flat_ref.2) | copy-start | bytes 1572868
  2.7 19.0 %collective-permute-start = (bf16[2064,128]{1,0:T(8,128)(2,1)S(1)}, bf16[2064,128]{1,0:T(8,128)(2,1)S(1)}, u32[]{:S(2)}, u32[]{:S(2)}) collective-permute-start(bf16[2064,128]{1,0:T(8,128)(2,1)S(1)} %pack_flagged.1.tiles_ref.own_ref), channel_id=1, source_target_pairs={{0,127},{1,2},{2,1},{3,4},{4,3},{5,6},{6,5},{7,8},{8,7},{9,10},{10... | collective-permute-start | bytes 1585160 | tf_op jit(solution)/shard_map/ppermute | solution.py:476
  5.8 10.3 %copy-start.1 = (bf16[1,262144]{1,0:T(2,128)(2,1)S(1)}, bf16[1,262144]{1,0:T(2,128)(2,1)}, u32[]{:S(2)}) copy-start(bf16[1,262144]{1,0:T(2,128)(2,1)} %flat_ref.3) | copy-start | bytes 1572868
  5.8 13.0 %collective-permute-start.1 = (bf16[2064,128]{1,0:T(8,128)(2,1)S(1)}, bf16[2064,128]{1,0:T(8,128)(2,1)S(1)}, u32[]{:S(2)}, u32[]{:S(2)}) collective-permute-start(bf16[2064,128]{1,0:T(8,128)(2,1)S(1)} %again.1.earlier_ref), channel_id=1, source_target_pairs={{0,1},{1,0},{2,3},{3,2},{4,5},{5,4},{6,7},{7,6},{8,9},{9,8},{10,11... | collective-permute-start | bytes 1585160 | tf_op jit(solution)/shard_map/ppermute | solution.py:480
  16.1 2.7 %copy-start.2 = (bf16[256,256]{1,0:T(8,128)(2,1)S(1)}, bf16[256,256]{1,0:T(8,128)(2,1)}, u32[]{:S(2)}) copy-start(bf16[256,256]{1,0:T(8,128)(2,1)} %constant.14.clone.table_ref) | copy-start | bytes 393220
  16.1 2.7 %copy-start.3 = (bf16[256,256]{1,0:T(8,128)(2,1)S(1)}, bf16[256,256]{1,0:T(8,128)(2,1)}, u32[]{:S(2)}) copy-start(bf16[256,256]{1,0:T(8,128)(2,1)} %constant.15.clone.mixed_ref) | copy-start | bytes 393220
  18.8 3.0 %copy-start.4 = (bf16[256,256]{1,0:T(8,128)(2,1)S(1)}, bf16[256,256]{1,0:T(8,128)(2,1)}, u32[]{:S(2)}) copy-start(bf16[256,256]{1,0:T(8,128)(2,1)} %constant.16.clone.halves_ref) | copy-start | bytes 393220
  24.9 41.5 %all-to-all-start = ((bf16[128,32,128]{2,1,0:T(8,128)(2,1)}), bf16[128,32,128]{2,1,0:T(8,128)(2,1)S(1)}, u32[]{:S(2)}, u32[]{:S(2)}) async-start(bf16[128,32,128]{2,1,0:T(8,128)(2,1)} %exchange.1), calls=%async_computation | async-start | bytes 2097152 | tf_op jit(solution)/shard_map/all_to_all | solution.py:500
  66.9 1.3 %collective-permute-start.2 = (f32[64,128]{1,0:T(8,128)S(1)}, f32[64,128]{1,0:T(8,128)S(1)}, u32[]{:S(2)}, u32[]{:S(2)}) collective-permute-start(f32[64,128]{1,0:T(8,128)S(1)} %get-tuple-element.15), channel_id=1, source_target_pairs={{0,1},{1,0},{2,3},{3,2},{4,5},{5,4},{6,7},{7,6},{8,9},{9,8},{10,11... | collective-permute-start | bytes 98312 | tf_op jit(solution)/shard_map/ppermute | solution.py:480
  89.0 4.1 %collective-permute-start.3 = (bf16[64,128]{1,0:T(8,128)(2,1)S(1)}, bf16[64,128]{1,0:T(8,128)(2,1)S(1)}, u32[]{:S(2)}, u32[]{:S(2)}) collective-permute-start(bf16[64,128]{1,0:T(8,128)(2,1)S(1)} %reduce_sum.25.mine_ref), channel_id=1, source_target_pairs={{0,1},{1,0},{2,3},{3,2},{4,5},{5,4},{6,7},{7,6},{8,9},{9,8},{10,11... | collective-permute-start | bytes 49160 | tf_op jit(solution)/shard_map/ppermute | solution.py:480

commit v10 on v8

--- a/solution.py
+++ b/solution.py
@@ -101,10 +101,41 @@
     lax.fori_loop(0, 16, part, 0)
 
 
-def pack_flagged_body(flat_ref, flag_ref, tiles_ref):
+def seed_body(seed_ref):
+    seed_ref[...] = jnp.zeros(seed_ref.shape, seed_ref.dtype)
+
+
+def seed():
+    return pl.pallas_call(
+        seed_body,
+        out_shape=jax.ShapeDtypeStruct((8, 128), jnp.int32),
+        out_specs=VMEM,
+        cost_estimate=pl.CostEstimate(
+            flops=NEAR_FLOPS, bytes_accessed=4096, transcendentals=0
+        ),
+        name="seed",
+    )()
+
+
+def flag_body(flag_ref, seed_ref, rows_ref):
+    flag = jnp.broadcast_to(flag_ref[...], (16, 128)) + seed_ref[pl.ds(0, 1), :]
+    rows_ref[...] = flag.astype(jnp.float32).astype(jnp.bfloat16)
+
+
+def flag_rows(flag):
+    return pl.pallas_call(
+        flag_body,
+        out_shape=jax.ShapeDtypeStruct((16, 128), jnp.bfloat16),
+        in_specs=[VMEM, VMEM],
+        out_specs=VMEM,
+        compiler_params=pltpu.CompilerParams(vmem_limit_bytes=16 * 1024 * 1024),
+        name="flag_rows",
+    )(flag.reshape(1, 1), seed())
+
+
+def pack_flagged_body(flat_ref, rows_ref, tiles_ref):
     pack_body(flat_ref, tiles_ref)
-    flag = jnp.broadcast_to(flag_ref[...], (16, 128))
-    tiles_ref[pl.ds(ROWS, 16), :] = flag.astype(jnp.float32).astype(jnp.bfloat16)
+    tiles_ref[pl.ds(ROWS, 16), :] = rows_ref[...]
 
 
 def pack_after_body(flat_ref, earlier_ref, both_ref):
@@ -141,7 +172,7 @@
     )(tiles)
 
 
-def packed_with_flag(flat, flag):
+def packed_with_flag(flat, rows):
     return pl.pallas_call(
         pack_flagged_body,
         out_shape=jax.ShapeDtypeStruct((ROWS + 16, 128), jnp.bfloat16),
@@ -149,7 +180,7 @@
         out_specs=VMEM,
         compiler_params=pltpu.CompilerParams(vmem_limit_bytes=16 * 1024 * 1024),
         name="pack_flagged",
-    )(flat, flag.reshape(1, 1))
+    )(flat, rows)
 
 
 def plane_rows(plane, height):
@@ -488,7 +519,7 @@
 
 
 def local(orbitals, trial, occupations):
-    own = packed_with_flag(orbitals, occupations)
+    own = packed_with_flag(orbitals, flag_rows(occupations))
     far = from_far(own)
     again = copied(own)
     near = swapped(again)

time: 94 us -> 94.2 us (level)
  no operation moved by 1% of the time
where the time goes in v10:
time: 94.2 us; the launch traced here: 93.9 us
  waiting for transfers between devices  30.7 us (33%)
  starting transfers between devices  24.7 us (26%)
  blocking collectives  20.5 us (22%)
  Pallas kernels  15.7 us (17%)
  between operations  1.44 us (2%)
    all_to_all x1, waiting for transfers between devices, local(): tiles = lax.all_to_all(both, BAND, 0, 0, tiled=True)  28.6 us
    all_to_all x2, blocking collectives, summed_over(): tiles = lax.all_to_all(copies, axes, 0, 0, tiled=True)  20.5 us
    ppermute x3, starting transfers between devices, swapped(): return lax.ppermute(value, 'core', [(0, 1), (1, 0)])  11.9 us
    all_to_all x1, starting transfers between devices, local(): tiles = lax.all_to_all(both, BAND, 0, 0, tiled=True)  9.71 us
    pallas_call x1, Pallas kernels, unpacked(): pl.pallas_call(unpack_body, out_shape=(jax.ShapeDtypeStruct((1, G), jnp.b...  3.15 us
    ppermute x1, starting transfers between devices, from_far(): return lax.ppermute(value, BAND, pairs)  3.11 us
    pallas_call x1, Pallas kernels, exchange_of(): pl.pallas_call(exchange_body, out_shape=jax.ShapeDtypeStruct((128, 32, 12...  3.11 us
    pallas_call x1, Pallas kernels, near_term(): pl.pallas_call(near_body, out_shape=(jax.ShapeDtypeStruct((HALF * NG, 128...  2.92 us
  transfers between devices with their start and end apart: 5, of which 3 were waited for; matrix products, arithmetic and copies ran while one was open for 0% of the time, Pallas kernels for 11%

profile of v10, /device:TPU:1, one launch (start us, length us, event | category | flops | bytes accessed | tf_op | source)
XLA Modules:
  0.0 93.9 jit_solution(13453445064036121139)
XLA Ops:
  0.6 0.0 copy-start
  0.6 0.6 seed.1.seed_ref
  1.9 0.0 copy-start.5
  1.9 0.7 copy-done.5
  2.6 0.1 flag_rows.1.rows_ref
  2.7 0.0 copy-done
  2.7 0.1 pack_flagged.1.tiles_ref.own_ref
  2.8 3.1 %collective-permute-start = (bf16[2064,128]{1,0:T(8,128)(2,1)S(1)}, bf16[2064,128]{1,0:T(8,128)(2,1)S(1)}, u32[]{:S(2)}, u32[]{:S(2)}) collective-permute-start(bf16[2064,128]{1,0:T(8,128)(2,1)S(1)} %pack_flagged.1.tiles_ref.own_ref), channel_id=1, source_target_pairs={{0,127},{1,2},{2,1},{3,4},{4,3},{5,6},{6,5},{7,8},{8,7},{9,10},{10... | collective-permute-start | bytes 1585160 | tf_op jit(solution)/shard_map/ppermute | solution.py:507
  5.9 0.0 copy-start.1
  6.0 8.8 %collective-permute-start.1 = (bf16[2064,128]{1,0:T(8,128)(2,1)S(1)}, bf16[2064,128]{1,0:T(8,128)(2,1)S(1)}, u32[]{:S(2)}, u32[]{:S(2)}) collective-permute-start(bf16[2064,128]{1,0:T(8,128)(2,1)S(1)} %again.1.earlier_ref), channel_id=1, source_target_pairs={{0,1},{1,0},{2,3},{3,2},{4,5},{5,4},{6,7},{7,6},{8,9},{9,8},{10,11... | collective-permute-start | bytes 1585160 | tf_op jit(solution)/shard_map/ppermute | solution.py:511
  14.7 1.5 %screened_kernel.1.kernel_ref.earlier_ref = f32[64,64,128]{2,1,0:T(8,128)S(1)} custom-call(bf16[2064,128]{1,0:T(8,128)(2,1)S(1)} %again.1.earlier_ref), custom_call_target="tpu_custom_call" | custom-call | flops 10000000000 | bytes 2097152 | tf_op jit(solution)/shard_map/screened_kernel/pallas_call | solution.py:63
  16.2 0.0 copy-done.1
  16.2 0.0 copy-start.2
  16.3 0.0 copy-start.3
  16.3 2.6 %pack.1.both_ref = bf16[128,32,128]{2,1,0:T(8,128)(2,1)} custom-call(bf16[1,262144]{1,0:T(2,128)(2,1)S(1)} %copy-done.1, f32[64,64,128]{2,1,0:T(8,128)S(1)} %screened_kernel.1.kernel_ref.earlier_ref), custom_call_target="tpu_custom_call" | custom-call | tf_op jit(solution)/shard_map/pack/pallas_call | solution.py:146
  18.9 0.0 copy-start.4
  18.9 0.0 collective-permute-done.1.near_ref
  18.9 0.0 copy-done.2
  18.9 0.0 copy-done.3
  18.9 2.9 %near_term.1 = (bf16[2048,128]{1,0:T(8,128)(2,1)S(1)}, f32[2048,128]{1,0:T(8,128)S(1)}) custom-call(bf16[2064,128]{1,0:T(8,128)(2,1)S(1)} %pack_flagged.1.tiles_ref.own_ref, bf16[2064,128]{1,0:T(8,128)(2,1)S(1)} %collective-permute-done.1.near_ref, bf16[256,256]{1,0:T(8,128)(2,1)S(1)} %copy-done.2, bf16[256,256]{1,0:T(8,128)(2,1)S(1)} %copy-done.3, ...), custom_call_target="tpu_custom_call" | custom-call | flops 10000000000 | bytes 4194304 | tf_op jit(solution)/shard_map/near_term/pallas_call | solution.py:299
  21.9 0.0 collective-permute-done.far_ref
  21.9 0.0 copy-done.4
  21.9 3.1 %exchange.1 = bf16[128,32,128]{2,1,0:T(8,128)(2,1)} custom-call(bf16[2064,128]{1,0:T(8,128)(2,1)S(1)} %collective-permute-done.far_ref, bf16[2048,128]{1,0:T(8,128)(2,1)S(1)} %get-tuple-element.9.owner_ref, f32[2048,128]{1,0:T(8,128)S(1)} %get-tuple-element.10.term_ref, bf16[128,32,128]{2,1,0:T(8,128)(2,1)} %pack.1.both_ref, ...), custom_call_target="tpu_custom_call", output_to_operand_aliasing={{}: (3, {})} | custom-call | tf_op jit(solution)/shard_map/exchange/pallas_call | solution.py:394
  25.0 9.7 %all-to-all-start = ((bf16[128,32,128]{2,1,0:T(8,128)(2,1)}), bf16[128,32,128]{2,1,0:T(8,128)(2,1)S(1)}, u32[]{:S(2)}, u32[]{:S(2)}) async-start(bf16[128,32,128]{2,1,0:T(8,128)(2,1)} %exchange.1), calls=%async_computation | async-start | bytes 2097152 | tf_op jit(solution)/shard_map/all_to_all | solution.py:531
  34.7 3.1 %unpack.1 = (bf16[1,262144]{1,0:T(2,128)(2,1)}, bf16[16,128]{1,0:T(8,128)(2,1)S(1)}) custom-call(bf16[4096,128]{1,0:T(8,128)(2,1)} %bitcast.1.tiles_ref), custom_call_target="tpu_custom_call" | custom-call | tf_op jit(solution)/shard_map/unpack/pallas_call | solution.py:424
  37.9 28.6 %all-to-all-done = bf16[128,32,128]{2,1,0:T(8,128)(2,1)S(1)} async-done(((bf16[128,32,128]{2,1,0:T(8,128)(2,1)}), bf16[128,32,128]{2,1,0:T(8,128)(2,1)S(1)}, u32[]{:S(2)}, u32[]{:S(2)}) %all-to-all-start) | async-done | bytes 1048608 | tf_op jit(solution)/shard_map/all_to_all | solution.py:531
  66.5 0.6 intersection.1
  67.1 0.1 collective-permute-start.2
  67.2 1.2 %collective-permute-done.2 = f32[64,128]{1,0:T(8,128)S(1)} collective-permute-done((f32[64,128]{1,0:T(8,128)S(1)}, f32[64,128]{1,0:T(8,128)S(1)}, u32[]{:S(2)}, u32[]{:S(2)}) %collective-permute-start.2) | collective-permute-done | bytes 32800 | tf_op jit(solution)/shard_map/ppermute | solution.py:511
  68.4 9.9 %all_to_all.15 = bf16[8,64,128]{2,1,0:T(8,128)(2,1)S(1)} all-to-all(bf16[8,64,128]{2,1,0:T(8,128)(2,1)S(1)} %broadcast_in_dim.4), channel_id=1, replica_groups=mesh['spin'=2,'y'=4,'x'=2,'z'=8,'core'=2] {'x','y'}, dimensions={0} | all-to-all | bytes 262144 | tf_op jit(solution)/shard_map/all_to_all | solution.py:517
  78.4 10.6 %all_to_all.16 = bf16[8,64,128]{2,1,0:T(8,128)(2,1)S(1)} all-to-all(bf16[8,64,128]{2,1,0:T(8,128)(2,1)S(1)} %broadcast_in_dim.5), channel_id=1, replica_groups=mesh['spin'=2,'y'=4,'x'=2,'z'=8,'core'=2] {'z'}, dimensions={0} | all-to-all | bytes 262144 | tf_op jit(solution)/shard_map/all_to_all | solution.py:517
  89.0 3.0 %collective-permute-start.3 = (bf16[64,128]{1,0:T(8,128)(2,1)S(1)}, bf16[64,128]{1,0:T(8,128)(2,1)S(1)}, u32[]{:S(2)}, u32[]{:S(2)}) collective-permute-start(bf16[64,128]{1,0:T(8,128)(2,1)S(1)} %reduce_sum.25.mine_ref), channel_id=1, source_target_pairs={{0,1},{1,0},{2,3},{3,2},{4,5},{5,4},{6,7},{7,6},{8,9},{9,8},{10,11... | collective-permute-start | bytes 49160 | tf_op jit(solution)/shard_map/ppermute | solution.py:511
  92.0 0.8 collective-permute-done.3.other_ref
  92.9 1.0 %projected.1 = bf16[128,2048]{1,0:T(8,128)(2,1)} custom-call(bf16[2048,128]{1,0:T(8,128)(2,1)S(1)} %get-tuple-element.13.lines_ref, bf16[64,128]{1,0:T(8,128)(2,1)S(1)} %reduce_sum.25.mine_ref, bf16[64,128]{1,0:T(8,128)(2,1)S(1)} %collective-permute-done.3.other_ref, s32[1]{0:T(128)} %bitcast.3.core_ref), custom_call_target="tpu_custom_call" | custom-call | tf_op jit(solution)/shard_map/projected/pallas_call | solution.py:490
  (6 shorter events, 0.1 us)
Async XLA Ops:
  0.6 2.0 %copy-start = (bf16[1,262144]{1,0:T(2,128)(2,1)S(1)}, bf16[1,262144]{1,0:T(2,128)(2,1)}, u32[]{:S(2)}) copy-start(bf16[1,262144]{1,0:T(2,128)(2,1)} %flat_ref.2) | copy-start | bytes 1572868
  1.9 0.7 copy-start.5
  2.8 19.1 %collective-permute-start = (bf16[2064,128]{1,0:T(8,128)(2,1)S(1)}, bf16[2064,128]{1,0:T(8,128)(2,1)S(1)}, u32[]{:S(2)}, u32[]{:S(2)}) collective-permute-start(bf16[2064,128]{1,0:T(8,128)(2,1)S(1)} %pack_flagged.1.tiles_ref.own_ref), channel_id=1, source_target_pairs={{0,127},{1,2},{2,1},{3,4},{4,3},{5,6},{6,5},{7,8},{8,7},{9,10},{10... | collective-permute-start | bytes 1585160 | tf_op jit(solution)/shard_map/ppermute | solution.py:507
  5.9 10.3 %copy-start.1 = (bf16[1,262144]{1,0:T(2,128)(2,1)S(1)}, bf16[1,262144]{1,0:T(2,128)(2,1)}, u32[]{:S(2)}) copy-start(bf16[1,262144]{1,0:T(2,128)(2,1)} %flat_ref.3) | copy-start | bytes 1572868
  6.0 13.0 %collective-permute-start.1 = (bf16[2064,128]{1,0:T(8,128)(2,1)S(1)}, bf16[2064,128]{1,0:T(8,128)(2,1)S(1)}, u32[]{:S(2)}, u32[]{:S(2)}) collective-permute-start(bf16[2064,128]{1,0:T(8,128)(2,1)S(1)} %again.1.earlier_ref), channel_id=1, source_target_pairs={{0,1},{1,0},{2,3},{3,2},{4,5},{5,4},{6,7},{7,6},{8,9},{9,8},{10,11... | collective-permute-start | bytes 1585160 | tf_op jit(solution)/shard_map/ppermute | solution.py:511
  16.2 2.7 %copy-start.2 = (bf16[256,256]{1,0:T(8,128)(2,1)S(1)}, bf16[256,256]{1,0:T(8,128)(2,1)}, u32[]{:S(2)}) copy-start(bf16[256,256]{1,0:T(8,128)(2,1)} %constant.14.clone.table_ref) | copy-start | bytes 393220
  16.3 2.7 %copy-start.3 = (bf16[256,256]{1,0:T(8,128)(2,1)S(1)}, bf16[256,256]{1,0:T(8,128)(2,1)}, u32[]{:S(2)}) copy-start(bf16[256,256]{1,0:T(8,128)(2,1)} %constant.15.clone.mixed_ref) | copy-start | bytes 393220
  18.9 3.0 %copy-start.4 = (bf16[256,256]{1,0:T(8,128)(2,1)S(1)}, bf16[256,256]{1,0:T(8,128)(2,1)}, u32[]{:S(2)}) copy-start(bf16[256,256]{1,0:T(8,128)(2,1)} %constant.16.clone.halves_ref) | copy-start | bytes 393220
  25.0 41.5 %all-to-all-start = ((bf16[128,32,128]{2,1,0:T(8,128)(2,1)}), bf16[128,32,128]{2,1,0:T(8,128)(2,1)S(1)}, u32[]{:S(2)}, u32[]{:S(2)}) async-start(bf16[128,32,128]{2,1,0:T(8,128)(2,1)} %exchange.1), calls=%async_computation | async-start | bytes 2097152 | tf_op jit(solution)/shard_map/all_to_all | solution.py:531
  67.1 1.3 %collective-permute-start.2 = (f32[64,128]{1,0:T(8,128)S(1)}, f32[64,128]{1,0:T(8,128)S(1)}, u32[]{:S(2)}, u32[]{:S(2)}) collective-permute-start(f32[64,128]{1,0:T(8,128)S(1)} %get-tuple-element.15), channel_id=1, source_target_pairs={{0,1},{1,0},{2,3},{3,2},{4,5},{5,4},{6,7},{7,6},{8,9},{9,8},{10,11... | collective-permute-start | bytes 98312 | tf_op jit(solution)/shard_map/ppermute | solution.py:511
  89.0 3.8 %collective-permute-start.3 = (bf16[64,128]{1,0:T(8,128)(2,1)S(1)}, bf16[64,128]{1,0:T(8,128)(2,1)S(1)}, u32[]{:S(2)}, u32[]{:S(2)}) collective-permute-start(bf16[64,128]{1,0:T(8,128)(2,1)S(1)} %reduce_sum.25.mine_ref), channel_id=1, source_target_pairs={{0,1},{1,0},{2,3},{3,2},{4,5},{5,4},{6,7},{7,6},{8,9},{9,8},{10,11... | collective-permute-start | bytes 49160 | tf_op jit(solution)/shard_map/ppermute | solution.py:511

commit v11 on v10

--- a/solution.py
+++ b/solution.py
@@ -110,6 +110,7 @@
         seed_body,
         out_shape=jax.ShapeDtypeStruct((8, 128), jnp.int32),
         out_specs=VMEM,
+        compiler_params=pltpu.CompilerParams(vmem_limit_bytes=16 * 1024 * 1024),
         cost_estimate=pl.CostEstimate(
             flops=NEAR_FLOPS, bytes_accessed=4096, transcendentals=0
         ),

time: 94.2 us -> 93.4 us (level)
  no operation moved by 1% of the time
where the time goes in v11:
time: 93.4 us; the launch traced here: 93.1 us
  waiting for transfers between devices  30.7 us (33%)
  starting transfers between devices  24.7 us (26%)
  blocking collectives  20.5 us (22%)
  Pallas kernels  15.1 us (16%)
  between operations  1.52 us (2%)
    all_to_all x1, waiting for transfers between devices, local(): tiles = lax.all_to_all(both, BAND, 0, 0, tiled=True)  28.6 us
    all_to_all x2, blocking collectives, summed_over(): tiles = lax.all_to_all(copies, axes, 0, 0, tiled=True)  20.5 us
    ppermute x3, starting transfers between devices, swapped(): return lax.ppermute(value, 'core', [(0, 1), (1, 0)])  11.9 us
    all_to_all x1, starting transfers between devices, local(): tiles = lax.all_to_all(both, BAND, 0, 0, tiled=True)  9.71 us
    pallas_call x1, Pallas kernels, unpacked(): pl.pallas_call(unpack_body, out_shape=(jax.ShapeDtypeStruct((1, G), jnp.b...  3.15 us
    pallas_call x1, Pallas kernels, exchange_of(): pl.pallas_call(exchange_body, out_shape=jax.ShapeDtypeStruct((128, 32, 12...  3.12 us
    ppermute x1, starting transfers between devices, from_far(): return lax.ppermute(value, BAND, pairs)  3.11 us
    pallas_call x1, Pallas kernels, near_term(): pl.pallas_call(near_body, out_shape=(jax.ShapeDtypeStruct((HALF * NG, 128...  2.92 us
  transfers between devices with their start and end apart: 5, of which 3 were waited for; matrix products, arithmetic and copies ran while one was open for 0% of the time, Pallas kernels for 11%

profile of v11, /device:TPU:1, one launch (start us, length us, event | category | flops | bytes accessed | tf_op | source)
XLA Modules:
  0.0 93.1 jit_solution(854540856466217244)
XLA Ops:
  0.6 0.0 copy-start
  1.4 0.1 flag_rows.1.rows_ref
  1.5 0.4 copy-done
  1.9 0.1 pack_flagged.1.tiles_ref.own_ref
  2.0 3.1 %collective-permute-start = (bf16[2064,128]{1,0:T(8,128)(2,1)S(1)}, bf16[2064,128]{1,0:T(8,128)(2,1)S(1)}, u32[]{:S(2)}, u32[]{:S(2)}) collective-permute-start(bf16[2064,128]{1,0:T(8,128)(2,1)S(1)} %pack_flagged.1.tiles_ref.own_ref), channel_id=1, source_target_pairs={{0,127},{1,2},{2,1},{3,4},{4,3},{5,6},{6,5},{7,8},{8,7},{9,10},{10... | collective-permute-start | bytes 1585160 | tf_op jit(solution)/shard_map/ppermute | solution.py:508
  5.2 0.0 copy-start.1
  5.2 8.8 %collective-permute-start.1 = (bf16[2064,128]{1,0:T(8,128)(2,1)S(1)}, bf16[2064,128]{1,0:T(8,128)(2,1)S(1)}, u32[]{:S(2)}, u32[]{:S(2)}) collective-permute-start(bf16[2064,128]{1,0:T(8,128)(2,1)S(1)} %again.1.earlier_ref), channel_id=1, source_target_pairs={{0,1},{1,0},{2,3},{3,2},{4,5},{5,4},{6,7},{7,6},{8,9},{9,8},{10,11... | collective-permute-start | bytes 1585160 | tf_op jit(solution)/shard_map/ppermute | solution.py:512
  13.9 1.5 %screened_kernel.1.kernel_ref.earlier_ref = f32[64,64,128]{2,1,0:T(8,128)S(1)} custom-call(bf16[2064,128]{1,0:T(8,128)(2,1)S(1)} %again.1.earlier_ref), custom_call_target="tpu_custom_call" | custom-call | flops 10000000000 | bytes 2097152 | tf_op jit(solution)/shard_map/screened_kernel/pallas_call | solution.py:63
  15.4 0.0 copy-done.1
  15.5 0.0 copy-start.2
  15.5 0.0 copy-start.3
  15.5 2.6 %pack.1.both_ref = bf16[128,32,128]{2,1,0:T(8,128)(2,1)} custom-call(bf16[1,262144]{1,0:T(2,128)(2,1)S(1)} %copy-done.1, f32[64,64,128]{2,1,0:T(8,128)S(1)} %screened_kernel.1.kernel_ref.earlier_ref), custom_call_target="tpu_custom_call" | custom-call | tf_op jit(solution)/shard_map/pack/pallas_call | solution.py:147
  18.1 0.0 copy-start.4
  18.1 0.0 collective-permute-done.1.near_ref
  18.1 0.0 copy-done.2
  18.1 0.0 copy-done.3
  18.1 2.9 %near_term.1 = (bf16[2048,128]{1,0:T(8,128)(2,1)S(1)}, f32[2048,128]{1,0:T(8,128)S(1)}) custom-call(bf16[2064,128]{1,0:T(8,128)(2,1)S(1)} %pack_flagged.1.tiles_ref.own_ref, bf16[2064,128]{1,0:T(8,128)(2,1)S(1)} %collective-permute-done.1.near_ref, bf16[256,256]{1,0:T(8,128)(2,1)S(1)} %copy-done.2, bf16[256,256]{1,0:T(8,128)(2,1)S(1)} %copy-done.3, ...), custom_call_target="tpu_custom_call" | custom-call | flops 10000000000 | bytes 4194304 | tf_op jit(solution)/shard_map/near_term/pallas_call | solution.py:300
  21.1 0.0 collective-permute-done.far_ref
  21.1 0.0 copy-done.4
  21.1 3.1 %exchange.1 = bf16[128,32,128]{2,1,0:T(8,128)(2,1)} custom-call(bf16[2064,128]{1,0:T(8,128)(2,1)S(1)} %collective-permute-done.far_ref, bf16[2048,128]{1,0:T(8,128)(2,1)S(1)} %get-tuple-element.9.owner_ref, f32[2048,128]{1,0:T(8,128)S(1)} %get-tuple-element.10.term_ref, bf16[128,32,128]{2,1,0:T(8,128)(2,1)} %pack.1.both_ref, ...), custom_call_target="tpu_custom_call", output_to_operand_aliasing={{}: (3, {})} | custom-call | tf_op jit(solution)/shard_map/exchange/pallas_call | solution.py:395
  24.2 9.7 %all-to-all-start = ((bf16[128,32,128]{2,1,0:T(8,128)(2,1)}), bf16[128,32,128]{2,1,0:T(8,128)(2,1)S(1)}, u32[]{:S(2)}, u32[]{:S(2)}) async-start(bf16[128,32,128]{2,1,0:T(8,128)(2,1)} %exchange.1), calls=%async_computation | async-start | bytes 2097152 | tf_op jit(solution)/shard_map/all_to_all | solution.py:532
  33.9 3.1 %unpack.1 = (bf16[1,262144]{1,0:T(2,128)(2,1)}, bf16[16,128]{1,0:T(8,128)(2,1)S(1)}) custom-call(bf16[4096,128]{1,0:T(8,128)(2,1)} %bitcast.1.tiles_ref), custom_call_target="tpu_custom_call" | custom-call | tf_op jit(solution)/shard_map/unpack/pallas_call | solution.py:425
  37.1 28.6 %all-to-all-done = bf16[128,32,128]{2,1,0:T(8,128)(2,1)S(1)} async-done(((bf16[128,32,128]{2,1,0:T(8,128)(2,1)}), bf16[128,32,128]{2,1,0:T(8,128)(2,1)S(1)}, u32[]{:S(2)}, u32[]{:S(2)}) %all-to-all-start) | async-done | bytes 1048608 | tf_op jit(solution)/shard_map/all_to_all | solution.py:532
  65.7 0.6 intersection.1
  66.3 0.1 collective-permute-start.2
  66.4 1.2 %collective-permute-done.2 = f32[64,128]{1,0:T(8,128)S(1)} collective-permute-done((f32[64,128]{1,0:T(8,128)S(1)}, f32[64,128]{1,0:T(8,128)S(1)}, u32[]{:S(2)}, u32[]{:S(2)}) %collective-permute-start.2) | collective-permute-done | bytes 32800 | tf_op jit(solution)/shard_map/ppermute | solution.py:512
  67.6 9.9 %all_to_all.15 = bf16[8,64,128]{2,1,0:T(8,128)(2,1)S(1)} all-to-all(bf16[8,64,128]{2,1,0:T(8,128)(2,1)S(1)} %broadcast_in_dim.4), channel_id=1, replica_groups=mesh['spin'=2,'y'=4,'x'=2,'z'=8,'core'=2] {'x','y'}, dimensions={0} | all-to-all | bytes 262144 | tf_op jit(solution)/shard_map/all_to_all | solution.py:518
  77.6 10.6 %all_to_all.16 = bf16[8,64,128]{2,1,0:T(8,128)(2,1)S(1)} all-to-all(bf16[8,64,128]{2,1,0:T(8,128)(2,1)S(1)} %broadcast_in_dim.5), channel_id=1, replica_groups=mesh['spin'=2,'y'=4,'x'=2,'z'=8,'core'=2] {'z'}, dimensions={0} | all-to-all | bytes 262144 | tf_op jit(solution)/shard_map/all_to_all | solution.py:518
  88.2 3.0 %collective-permute-start.3 = (bf16[64,128]{1,0:T(8,128)(2,1)S(1)}, bf16[64,128]{1,0:T(8,128)(2,1)S(1)}, u32[]{:S(2)}, u32[]{:S(2)}) collective-permute-start(bf16[64,128]{1,0:T(8,128)(2,1)S(1)} %reduce_sum.25.mine_ref), channel_id=1, source_target_pairs={{0,1},{1,0},{2,3},{3,2},{4,5},{5,4},{6,7},{7,6},{8,9},{9,8},{10,11... | collective-permute-start | bytes 49160 | tf_op jit(solution)/shard_map/ppermute | solution.py:512
  91.2 0.8 collective-permute-done.3.other_ref
  92.1 1.0 %projected.1 = bf16[128,2048]{1,0:T(8,128)(2,1)} custom-call(bf16[2048,128]{1,0:T(8,128)(2,1)S(1)} %get-tuple-element.13.lines_ref, bf16[64,128]{1,0:T(8,128)(2,1)S(1)} %reduce_sum.25.mine_ref, bf16[64,128]{1,0:T(8,128)(2,1)S(1)} %collective-permute-done.3.other_ref, s32[1]{0:T(128)} %bitcast.3.core_ref), custom_call_target="tpu_custom_call" | custom-call | tf_op jit(solution)/shard_map/projected/pallas_call | solution.py:491
  (7 shorter events, 0.1 us)
Async XLA Ops:
  0.6 1.2 %copy-start = (bf16[1,262144]{1,0:T(2,128)(2,1)S(1)}, bf16[1,262144]{1,0:T(2,128)(2,1)}, u32[]{:S(2)}) copy-start(bf16[1,262144]{1,0:T(2,128)(2,1)} %flat_ref.2) | copy-start | bytes 1572868
  2.0 19.1 %collective-permute-start = (bf16[2064,128]{1,0:T(8,128)(2,1)S(1)}, bf16[2064,128]{1,0:T(8,128)(2,1)S(1)}, u32[]{:S(2)}, u32[]{:S(2)}) collective-permute-start(bf16[2064,128]{1,0:T(8,128)(2,1)S(1)} %pack_flagged.1.tiles_ref.own_ref), channel_id=1, source_target_pairs={{0,127},{1,2},{2,1},{3,4},{4,3},{5,6},{6,5},{7,8},{8,7},{9,10},{10... | collective-permute-start | bytes 1585160 | tf_op jit(solution)/shard_map/ppermute | solution.py:508
  5.2 10.3 %copy-start.1 = (bf16[1,262144]{1,0:T(2,128)(2,1)S(1)}, bf16[1,262144]{1,0:T(2,128)(2,1)}, u32[]{:S(2)}) copy-start(bf16[1,262144]{1,0:T(2,128)(2,1)} %flat_ref.3) | copy-start | bytes 1572868
  5.2 13.0 %collective-permute-start.1 = (bf16[2064,128]{1,0:T(8,128)(2,1)S(1)}, bf16[2064,128]{1,0:T(8,128)(2,1)S(1)}, u32[]{:S(2)}, u32[]{:S(2)}) collective-permute-start(bf16[2064,128]{1,0:T(8,128)(2,1)S(1)} %again.1.earlier_ref), channel_id=1, source_target_pairs={{0,1},{1,0},{2,3},{3,2},{4,5},{5,4},{6,7},{7,6},{8,9},{9,8},{10,11... | collective-permute-start | bytes 1585160 | tf_op jit(solution)/shard_map/ppermute | solution.py:512
  15.5 2.7 %copy-start.2 = (bf16[256,256]{1,0:T(8,128)(2,1)S(1)}, bf16[256,256]{1,0:T(8,128)(2,1)}, u32[]{:S(2)}) copy-start(bf16[256,256]{1,0:T(8,128)(2,1)} %constant.14.clone.table_ref) | copy-start | bytes 393220
  15.5 2.7 %copy-start.3 = (bf16[256,256]{1,0:T(8,128)(2,1)S(1)}, bf16[256,256]{1,0:T(8,128)(2,1)}, u32[]{:S(2)}) copy-start(bf16[256,256]{1,0:T(8,128)(2,1)} %constant.15.clone.mixed_ref) | copy-start | bytes 393220
  18.1 3.0 %copy-start.4 = (bf16[256,256]{1,0:T(8,128)(2,1)S(1)}, bf16[256,256]{1,0:T(8,128)(2,1)}, u32[]{:S(2)}) copy-start(bf16[256,256]{1,0:T(8,128)(2,1)} %constant.16.clone.halves_ref) | copy-start | bytes 393220
  24.2 41.5 %all-to-all-start = ((bf16[128,32,128]{2,1,0:T(8,128)(2,1)}), bf16[128,32,128]{2,1,0:T(8,128)(2,1)S(1)}, u32[]{:S(2)}, u32[]{:S(2)}) async-start(bf16[128,32,128]{2,1,0:T(8,128)(2,1)} %exchange.1), calls=%async_computation | async-start | bytes 2097152 | tf_op jit(solution)/shard_map/all_to_all | solution.py:532
  66.3 1.3 %collective-permute-start.2 = (f32[64,128]{1,0:T(8,128)S(1)}, f32[64,128]{1,0:T(8,128)S(1)}, u32[]{:S(2)}, u32[]{:S(2)}) collective-permute-start(f32[64,128]{1,0:T(8,128)S(1)} %get-tuple-element.15), channel_id=1, source_target_pairs={{0,1},{1,0},{2,3},{3,2},{4,5},{5,4},{6,7},{7,6},{8,9},{9,8},{10,11... | collective-permute-start | bytes 98312 | tf_op jit(solution)/shard_map/ppermute | solution.py:512
  88.2 3.8 %collective-permute-start.3 = (bf16[64,128]{1,0:T(8,128)(2,1)S(1)}, bf16[64,128]{1,0:T(8,128)(2,1)S(1)}, u32[]{:S(2)}, u32[]{:S(2)}) collective-permute-start(bf16[64,128]{1,0:T(8,128)(2,1)S(1)} %reduce_sum.25.mine_ref), channel_id=1, source_target_pairs={{0,1},{1,0},{2,3},{3,2},{4,5},{5,4},{6,7},{7,6},{8,9},{9,8},{10,11... | collective-permute-start | bytes 49160 | tf_op jit(solution)/shard_map/ppermute | solution.py:512

commit v12 on v11

--- a/solution.py
+++ b/solution.py
@@ -440,12 +440,16 @@
     for peer in range(128):
         wide[pl.ds(peer * WIDE, 32), :] = tiles_ref[pl.ds(peer * 32, 32), :].astype(jnp.float32)
     total = jnp.zeros((128, 128), jnp.float32)
-    for line in range(16):
-        trial = wide[pl.ds(line, 128, stride=WIDE), :].astype(bf16)
-        value = wide[pl.ds(line + 16, 128, stride=WIDE), :].astype(bf16)
-        lines_ref[pl.ds(line * 128, 128), :] = value
+    for line in range(0, 16, 2):
+        trials, values = [], []
+        for index in (line, line + 1):
+            trials.append(wide[pl.ds(index, 128, stride=WIDE), :].astype(bf16))
+            value = wide[pl.ds(index + 16, 128, stride=WIDE), :].astype(bf16)
+            lines_ref[pl.ds(index * 128, 128), :] = value
+            values.append(value)
         total = total + lax.dot_general(
-            trial, value, (((1,), (1,)), ((), ())), preferred_element_type=jnp.float32
+            jnp.concatenate(trials, axis=1), jnp.concatenate(values, axis=1),
+            (((1,), (1,)), ((), ())), preferred_element_type=jnp.float32,
         )
     total = total * (1.0 / math.sqrt(G))
     first = core_ref[0] == 0
@@ -466,40 +470,64 @@
     )(tiles, token, core)
 
 
-def projected_body(lines_ref, mine_ref, other_ref, core_ref, out_ref, result, left):
-    first = core_ref[0] == 0
-    mine, other = mine_ref[...].astype(jnp.float32), other_ref[...].astype(jnp.float32)
-    table = jnp.concatenate(
-        [jnp.where(first, mine, other), jnp.where(first, other, mine)], axis=0
-    ).astype(jnp.bfloat16)
+def half_projected(lines_ref, half_ref, out_ref, row, result, left):
+    table = half_ref[...]
 
     def copy(part):
         columns = pl.ds(part * 512, 512)
-        return pltpu.make_async_copy(result.at[:, columns], out_ref.at[:, columns], left.at[part])
+        rows = pl.ds(pl.multiple_of(row * 64, 64), 64)
+        return pltpu.make_async_copy(result.at[:, columns], out_ref.at[rows, columns], left.at[part])
 
     for part in range(4):
-        for line in range(part * 4, part * 4 + 4):
-            rows = pl.ds(line * 128, 128)
-            value = dot(table, lines_ref[rows, :]) * (-1.0 / math.sqrt(128))
-            result[:, rows] = value.astype(jnp.bfloat16)
+        for line in (4 * part, 4 * part + 2):
+            both = [lines_ref[pl.ds(index * 128, 128), :] for index in (line, line + 1)]
+            value = dot(table, jnp.concatenate(both, axis=1)) * (-1.0 / math.sqrt(128))
+            result[:, pl.ds(line * 128, 256)] = value.astype(jnp.bfloat16)
         copy(part).start()
     for part in range(4):
         copy(part).wait()
 
 
-def projected_of(lines, mine, other, core):
-    return pl.pallas_call(
-        projected_body,
+def first_half_body(lines_ref, mine_ref, core_ref, out_ref, result, left):
+    row = jnp.where(core_ref[0] == 0, 0, 1)
+    half_projected(lines_ref, mine_ref, out_ref, row, result, left)
+
+
+def second_half_body(lines_ref, other_ref, core_ref, earlier_ref, out_ref, result, left):
+    row = jnp.where(core_ref[0] == 0, 1, 0)
+    half_projected(lines_ref, other_ref, out_ref, row, result, left)
+
+
+def projected_half(body, name, operands, flops, **aliases):
+    anywhere = pl.BlockSpec(memory_space=pltpu.HBM)
+    return pl.pallas_call(
+        body,
         out_shape=jax.ShapeDtypeStruct((128, ROWS), jnp.bfloat16),
-        in_specs=[VMEM, VMEM, VMEM, SMEM],
-        out_specs=pl.BlockSpec(memory_space=pltpu.HBM),
+        in_specs=[VMEM, VMEM, SMEM] + [anywhere] * (len(operands) - 3),
+        out_specs=anywhere,
         scratch_shapes=[
-            pltpu.VMEM((128, ROWS), jnp.bfloat16),
+            pltpu.VMEM((64, ROWS), jnp.bfloat16),
             pltpu.SemaphoreType.DMA((4,)),
         ],
         compiler_params=pltpu.CompilerParams(vmem_limit_bytes=16 * 1024 * 1024),
-        name="projected",
-    )(lines, mine, other, core)
+        cost_estimate=pl.CostEstimate(
+            flops=flops, bytes_accessed=1024 * 1024, transcendentals=0
+        ),
+        name=name,
+        **aliases,
+    )(*operands)
+
+
+def projected_of(lines, mine, core):
+    other = swapped(mine)
+    first = projected_half(first_half_body, "projected_first", (lines, mine, core), NEAR_FLOPS)
+    return projected_half(
+        second_half_body,
+        "projected_second",
+        (lines, other, core, first),
+        10**7,
+        input_output_aliases={3: 0},
+    )
 
 
 def from_far(value):
@@ -536,7 +564,7 @@
     half = (mine + swapped(other)).astype(jnp.bfloat16)
     half = summed_over(half, ("x", "y"))
     half = summed_over(half, "z")
-    return flat, projected_of(lines, half, swapped(half), core)
+    return flat, projected_of(lines, half, core)
 
 
 def solution(mesh):

time: 93.4 us -> 93.3 us (level)
  transfers between devices with their start and end apart: 5 -> 5, of which waited for: 3 -> 2; matrix products, arithmetic and copies ran while one was open for 0% -> 0% of each run, Pallas kernels for 11% -> 12%
where the time goes in v12:
time: 93.3 us; the launch traced here: 93 us
  waiting for transfers between devices  29.9 us (32%)
  starting transfers between devices  24.7 us (26%)
  blocking collectives  20.5 us (22%)
  Pallas kernels  15.9 us (17%)
  between operations  1.53 us (2%)
    all_to_all x1, waiting for transfers between devices, local(): tiles = lax.all_to_all(both, BAND, 0, 0, tiled=True)  28.6 us
    all_to_all x2, blocking collectives, summed_over(): tiles = lax.all_to_all(copies, axes, 0, 0, tiled=True)  20.5 us
    ppermute x3, starting transfers between devices, swapped(): return lax.ppermute(value, 'core', [(0, 1), (1, 0)])  11.9 us
    all_to_all x1, starting transfers between devices, local(): tiles = lax.all_to_all(both, BAND, 0, 0, tiled=True)  9.71 us
    pallas_call x1, Pallas kernels, unpacked(): pl.pallas_call(unpack_body, out_shape=(jax.ShapeDtypeStruct((1, G), jnp.b...  3.15 us
    pallas_call x1, Pallas kernels, exchange_of(): pl.pallas_call(exchange_body, out_shape=jax.ShapeDtypeStruct((128, 32, 12...  3.12 us
    ppermute x1, starting transfers between devices, from_far(): return lax.ppermute(value, BAND, pairs)  3.11 us
    pallas_call x1, Pallas kernels, near_term(): pl.pallas_call(near_body, out_shape=(jax.ShapeDtypeStruct((HALF * NG, 128...  2.92 us
  transfers between devices with their start and end apart: 5, of which 2 were waited for; matrix products, arithmetic and copies ran while one was open for 0% of the time, Pallas kernels for 12%

profile of v12, /device:TPU:1, one launch (start us, length us, event | category | flops | bytes accessed | tf_op | source)
XLA Modules:
  0.0 93.0 jit_solution(16829385991799009406)
XLA Ops:
  0.6 0.0 copy-start
  1.4 0.1 flag_rows.1.rows_ref
  1.5 0.4 copy-done
  1.9 0.1 pack_flagged.1.tiles_ref.own_ref
  2.0 3.1 %collective-permute-start = (bf16[2064,128]{1,0:T(8,128)(2,1)S(1)}, bf16[2064,128]{1,0:T(8,128)(2,1)S(1)}, u32[]{:S(2)}, u32[]{:S(2)}) collective-permute-start(bf16[2064,128]{1,0:T(8,128)(2,1)S(1)} %pack_flagged.1.tiles_ref.own_ref), channel_id=1, source_target_pairs={{0,127},{1,2},{2,1},{3,4},{4,3},{5,6},{6,5},{7,8},{8,7},{9,10},{10... | collective-permute-start | bytes 1585160 | tf_op jit(solution)/shard_map/ppermute | solution.py:536
  5.2 0.0 copy-start.1
  5.2 8.8 %collective-permute-start.1 = (bf16[2064,128]{1,0:T(8,128)(2,1)S(1)}, bf16[2064,128]{1,0:T(8,128)(2,1)S(1)}, u32[]{:S(2)}, u32[]{:S(2)}) collective-permute-start(bf16[2064,128]{1,0:T(8,128)(2,1)S(1)} %again.1.earlier_ref), channel_id=1, source_target_pairs={{0,1},{1,0},{2,3},{3,2},{4,5},{5,4},{6,7},{7,6},{8,9},{9,8},{10,11... | collective-permute-start | bytes 1585160 | tf_op jit(solution)/shard_map/ppermute | solution.py:540
  13.9 1.5 %screened_kernel.1.kernel_ref.earlier_ref = f32[64,64,128]{2,1,0:T(8,128)S(1)} custom-call(bf16[2064,128]{1,0:T(8,128)(2,1)S(1)} %again.1.earlier_ref), custom_call_target="tpu_custom_call" | custom-call | flops 10000000000 | bytes 2097152 | tf_op jit(solution)/shard_map/screened_kernel/pallas_call | solution.py:63
  15.4 0.0 copy-done.1
  15.5 0.0 copy-start.2
  15.5 0.0 copy-start.3
  15.5 2.6 %pack.1.both_ref = bf16[128,32,128]{2,1,0:T(8,128)(2,1)} custom-call(bf16[1,262144]{1,0:T(2,128)(2,1)S(1)} %copy-done.1, f32[64,64,128]{2,1,0:T(8,128)S(1)} %screened_kernel.1.kernel_ref.earlier_ref), custom_call_target="tpu_custom_call" | custom-call | tf_op jit(solution)/shard_map/pack/pallas_call | solution.py:147
  18.1 0.0 copy-start.4
  18.1 0.0 collective-permute-done.1.near_ref
  18.1 0.0 copy-done.2
  18.1 0.0 copy-done.3
  18.1 2.9 %near_term.1 = (bf16[2048,128]{1,0:T(8,128)(2,1)S(1)}, f32[2048,128]{1,0:T(8,128)S(1)}) custom-call(bf16[2064,128]{1,0:T(8,128)(2,1)S(1)} %pack_flagged.1.tiles_ref.own_ref, bf16[2064,128]{1,0:T(8,128)(2,1)S(1)} %collective-permute-done.1.near_ref, bf16[256,256]{1,0:T(8,128)(2,1)S(1)} %copy-done.2, bf16[256,256]{1,0:T(8,128)(2,1)S(1)} %copy-done.3, ...), custom_call_target="tpu_custom_call" | custom-call | flops 10000000000 | bytes 4194304 | tf_op jit(solution)/shard_map/near_term/pallas_call | solution.py:300
  21.1 0.0 collective-permute-done.far_ref
  21.1 0.0 copy-done.4
  21.1 3.1 %exchange.1 = bf16[128,32,128]{2,1,0:T(8,128)(2,1)} custom-call(bf16[2064,128]{1,0:T(8,128)(2,1)S(1)} %collective-permute-done.far_ref, bf16[2048,128]{1,0:T(8,128)(2,1)S(1)} %get-tuple-element.9.owner_ref, f32[2048,128]{1,0:T(8,128)S(1)} %get-tuple-element.10.term_ref, bf16[128,32,128]{2,1,0:T(8,128)(2,1)} %pack.1.both_ref, ...), custom_call_target="tpu_custom_call", output_to_operand_aliasing={{}: (3, {})} | custom-call | tf_op jit(solution)/shard_map/exchange/pallas_call | solution.py:395
  24.2 9.7 %all-to-all-start = ((bf16[128,32,128]{2,1,0:T(8,128)(2,1)}), bf16[128,32,128]{2,1,0:T(8,128)(2,1)S(1)}, u32[]{:S(2)}, u32[]{:S(2)}) async-start(bf16[128,32,128]{2,1,0:T(8,128)(2,1)} %exchange.1), calls=%async_computation | async-start | bytes 2097152 | tf_op jit(solution)/shard_map/all_to_all | solution.py:560
  33.9 3.1 %unpack.1 = (bf16[1,262144]{1,0:T(2,128)(2,1)}, bf16[16,128]{1,0:T(8,128)(2,1)S(1)}) custom-call(bf16[4096,128]{1,0:T(8,128)(2,1)} %bitcast.1.tiles_ref), custom_call_target="tpu_custom_call" | custom-call | tf_op jit(solution)/shard_map/unpack/pallas_call | solution.py:425
  37.1 28.6 %all-to-all-done = bf16[128,32,128]{2,1,0:T(8,128)(2,1)S(1)} async-done(((bf16[128,32,128]{2,1,0:T(8,128)(2,1)}), bf16[128,32,128]{2,1,0:T(8,128)(2,1)S(1)}, u32[]{:S(2)}, u32[]{:S(2)}) %all-to-all-start) | async-done | bytes 1048608 | tf_op jit(solution)/shard_map/all_to_all | solution.py:560
  65.7 0.5 intersection.1
  66.3 0.1 collective-permute-start.2
  66.4 1.2 %collective-permute-done.2 = f32[64,128]{1,0:T(8,128)S(1)} collective-permute-done((f32[64,128]{1,0:T(8,128)S(1)}, f32[64,128]{1,0:T(8,128)S(1)}, u32[]{:S(2)}, u32[]{:S(2)}) %collective-permute-start.2) | collective-permute-done | bytes 32800 | tf_op jit(solution)/shard_map/ppermute | solution.py:540
  67.6 9.9 %all_to_all.15 = bf16[8,64,128]{2,1,0:T(8,128)(2,1)S(1)} all-to-all(bf16[8,64,128]{2,1,0:T(8,128)(2,1)S(1)} %broadcast_in_dim.4), channel_id=1, replica_groups=mesh['spin'=2,'y'=4,'x'=2,'z'=8,'core'=2] {'x','y'}, dimensions={0} | all-to-all | bytes 262144 | tf_op jit(solution)/shard_map/all_to_all | solution.py:546
  77.6 10.6 %all_to_all.16 = bf16[8,64,128]{2,1,0:T(8,128)(2,1)S(1)} all-to-all(bf16[8,64,128]{2,1,0:T(8,128)(2,1)S(1)} %broadcast_in_dim.5), channel_id=1, replica_groups=mesh['spin'=2,'y'=4,'x'=2,'z'=8,'core'=2] {'z'}, dimensions={0} | all-to-all | bytes 262144 | tf_op jit(solution)/shard_map/all_to_all | solution.py:546
  88.2 3.0 %collective-permute-start.3 = (bf16[64,128]{1,0:T(8,128)(2,1)S(1)}, bf16[64,128]{1,0:T(8,128)(2,1)S(1)}, u32[]{:S(2)}, u32[]{:S(2)}) collective-permute-start(bf16[64,128]{1,0:T(8,128)(2,1)S(1)} %reduce_sum.25.mine_ref), channel_id=1, source_target_pairs={{0,1},{1,0},{2,3},{3,2},{4,5},{5,4},{6,7},{7,6},{8,9},{9,8},{10,11... | collective-permute-start | bytes 49160 | tf_op jit(solution)/shard_map/ppermute | solution.py:540
  91.2 0.9 projected_first.1.earlier_ref
  92.1 0.0 collective-permute-done.3.other_ref
  92.1 0.9 projected_second.1
  (7 shorter events, 0.1 us)
Async XLA Ops:
  0.6 1.2 %copy-start = (bf16[1,262144]{1,0:T(2,128)(2,1)S(1)}, bf16[1,262144]{1,0:T(2,128)(2,1)}, u32[]{:S(2)}) copy-start(bf16[1,262144]{1,0:T(2,128)(2,1)} %flat_ref.2) | copy-start | bytes 1572868
  2.0 19.1 %collective-permute-start = (bf16[2064,128]{1,0:T(8,128)(2,1)S(1)}, bf16[2064,128]{1,0:T(8,128)(2,1)S(1)}, u32[]{:S(2)}, u32[]{:S(2)}) collective-permute-start(bf16[2064,128]{1,0:T(8,128)(2,1)S(1)} %pack_flagged.1.tiles_ref.own_ref), channel_id=1, source_target_pairs={{0,127},{1,2},{2,1},{3,4},{4,3},{5,6},{6,5},{7,8},{8,7},{9,10},{10... | collective-permute-start | bytes 1585160 | tf_op jit(solution)/shard_map/ppermute | solution.py:536
  5.2 10.3 %copy-start.1 = (bf16[1,262144]{1,0:T(2,128)(2,1)S(1)}, bf16[1,262144]{1,0:T(2,128)(2,1)}, u32[]{:S(2)}) copy-start(bf16[1,262144]{1,0:T(2,128)(2,1)} %flat_ref.3) | copy-start | bytes 1572868
  5.2 13.0 %collective-permute-start.1 = (bf16[2064,128]{1,0:T(8,128)(2,1)S(1)}, bf16[2064,128]{1,0:T(8,128)(2,1)S(1)}, u32[]{:S(2)}, u32[]{:S(2)}) collective-permute-start(bf16[2064,128]{1,0:T(8,128)(2,1)S(1)} %again.1.earlier_ref), channel_id=1, source_target_pairs={{0,1},{1,0},{2,3},{3,2},{4,5},{5,4},{6,7},{7,6},{8,9},{9,8},{10,11... | collective-permute-start | bytes 1585160 | tf_op jit(solution)/shard_map/ppermute | solution.py:540
  15.5 2.7 %copy-start.2 = (bf16[256,256]{1,0:T(8,128)(2,1)S(1)}, bf16[256,256]{1,0:T(8,128)(2,1)}, u32[]{:S(2)}) copy-start(bf16[256,256]{1,0:T(8,128)(2,1)} %constant.14.clone.table_ref) | copy-start | bytes 393220
  15.5 2.7 %copy-start.3 = (bf16[256,256]{1,0:T(8,128)(2,1)S(1)}, bf16[256,256]{1,0:T(8,128)(2,1)}, u32[]{:S(2)}) copy-start(bf16[256,256]{1,0:T(8,128)(2,1)} %constant.15.clone.mixed_ref) | copy-start | bytes 393220
  18.1 3.0 %copy-start.4 = (bf16[256,256]{1,0:T(8,128)(2,1)S(1)}, bf16[256,256]{1,0:T(8,128)(2,1)}, u32[]{:S(2)}) copy-start(bf16[256,256]{1,0:T(8,128)(2,1)} %constant.16.clone.halves_ref) | copy-start | bytes 393220
  24.2 41.5 %all-to-all-start = ((bf16[128,32,128]{2,1,0:T(8,128)(2,1)}), bf16[128,32,128]{2,1,0:T(8,128)(2,1)S(1)}, u32[]{:S(2)}, u32[]{:S(2)}) async-start(bf16[128,32,128]{2,1,0:T(8,128)(2,1)} %exchange.1), calls=%async_computation | async-start | bytes 2097152 | tf_op jit(solution)/shard_map/all_to_all | solution.py:560
  66.3 1.3 %collective-permute-start.2 = (f32[64,128]{1,0:T(8,128)S(1)}, f32[64,128]{1,0:T(8,128)S(1)}, u32[]{:S(2)}, u32[]{:S(2)}) collective-permute-start(f32[64,128]{1,0:T(8,128)S(1)} %get-tuple-element.15), channel_id=1, source_target_pairs={{0,1},{1,0},{2,3},{3,2},{4,5},{5,4},{6,7},{7,6},{8,9},{9,8},{10,11... | collective-permute-start | bytes 98312 | tf_op jit(solution)/shard_map/ppermute | solution.py:540
  88.2 3.9 %collective-permute-start.3 = (bf16[64,128]{1,0:T(8,128)(2,1)S(1)}, bf16[64,128]{1,0:T(8,128)(2,1)S(1)}, u32[]{:S(2)}, u32[]{:S(2)}) collective-permute-start(bf16[64,128]{1,0:T(8,128)(2,1)S(1)} %reduce_sum.25.mine_ref), channel_id=1, source_target_pairs={{0,1},{1,0},{2,3},{3,2},{4,5},{5,4},{6,7},{7,6},{8,9},{9,8},{10,11... | collective-permute-start | bytes 49160 | tf_op jit(solution)/shard_map/ppermute | solution.py:540

commit v13 on v12

--- a/solution.py
+++ b/solution.py
@@ -338,7 +338,10 @@
             grid[pitched(plane), :] = part_of(values, part)
 
     def crossed(value):
-        return jnp.concatenate([value, pltpu.roll(value, 64, 1)], axis=0).astype(bf16)
+        value = value.astype(bf16)
+        return jnp.concatenate(
+            [value, jnp.concatenate([value[:, 64:], value[:, :64]], axis=1)], axis=0
+        )
 
     def joined(value):
         return jnp.where(low, value[:HALF], value[HALF:])
@@ -435,7 +438,7 @@
     )(tiles)
 
 
-def intersection_body(tiles_ref, token_ref, core_ref, lines_ref, mine_ref, other_ref, wide):
+def intersection_body(tiles_ref, token_ref, lines_ref, mine_ref, other_ref, wide):
     bf16 = jnp.bfloat16
     for peer in range(128):
         wide[pl.ds(peer * WIDE, 32), :] = tiles_ref[pl.ds(peer * 32, 32), :].astype(jnp.float32)
@@ -452,22 +455,22 @@
             (((1,), (1,)), ((), ())), preferred_element_type=jnp.float32,
         )
     total = total * (1.0 / math.sqrt(G))
-    first = core_ref[0] == 0
+    first = lax.axis_index("core") == 0
     mine_ref[...] = jnp.where(first, total[:64], total[64:])
     other_ref[...] = jnp.where(first, total[64:], total[:64])
 
 
-def intersection_of(tiles, token, core):
+def intersection_of(tiles, token):
     half = jax.ShapeDtypeStruct((64, 128), jnp.float32)
     return pl.pallas_call(
         intersection_body,
         out_shape=(jax.ShapeDtypeStruct((ROWS, 128), jnp.bfloat16), half, half),
-        in_specs=[VMEM, pl.BlockSpec(memory_space=pl.ANY), SMEM],
+        in_specs=[VMEM, pl.BlockSpec(memory_space=pl.ANY)],
         out_specs=(VMEM, VMEM, VMEM),
         scratch_shapes=[pltpu.VMEM((128 * WIDE, 128), jnp.float32)],
         compiler_params=pltpu.CompilerParams(vmem_limit_bytes=16 * 1024 * 1024),
         name="intersection",
-    )(tiles, token, core)
+    )(tiles, token)
 
 
 def half_projected(lines_ref, half_ref, out_ref, row, result, left):
@@ -488,13 +491,13 @@
         copy(part).wait()
 
 
-def first_half_body(lines_ref, mine_ref, core_ref, out_ref, result, left):
-    row = jnp.where(core_ref[0] == 0, 0, 1)
+def first_half_body(lines_ref, mine_ref, out_ref, result, left):
+    row = lax.axis_index("core")
     half_projected(lines_ref, mine_ref, out_ref, row, result, left)
 
 
-def second_half_body(lines_ref, other_ref, core_ref, earlier_ref, out_ref, result, left):
-    row = jnp.where(core_ref[0] == 0, 1, 0)
+def second_half_body(lines_ref, other_ref, earlier_ref, out_ref, result, left):
+    row = 1 - lax.axis_index("core")
     half_projected(lines_ref, other_ref, out_ref, row, result, left)
 
 
@@ -503,7 +506,7 @@
     return pl.pallas_call(
         body,
         out_shape=jax.ShapeDtypeStruct((128, ROWS), jnp.bfloat16),
-        in_specs=[VMEM, VMEM, SMEM] + [anywhere] * (len(operands) - 3),
+        in_specs=[VMEM, VMEM] + [anywhere] * (len(operands) - 2),
         out_specs=anywhere,
         scratch_shapes=[
             pltpu.VMEM((64, ROWS), jnp.bfloat16),
@@ -518,15 +521,15 @@
     )(*operands)
 
 
-def projected_of(lines, mine, core):
+def projected_of(lines, mine):
     other = swapped(mine)
-    first = projected_half(first_half_body, "projected_first", (lines, mine, core), NEAR_FLOPS)
+    first = projected_half(first_half_body, "projected_first", (lines, mine), NEAR_FLOPS)
     return projected_half(
         second_half_body,
         "projected_second",
-        (lines, other, core, first),
+        (lines, other, first),
         10**7,
-        input_output_aliases={3: 0},
+        input_output_aliases={2: 0},
     )
 
 
@@ -559,12 +562,11 @@
     both = exchange_of(far, owner, term, both, table, mixed, halves, kernel)
     tiles = lax.all_to_all(both, BAND, 0, 0, tiled=True)
     flat, token = unpacked(both.reshape(2 * ROWS, 128))
-    core = lax.axis_index("core").astype(jnp.int32).reshape(1)
-    lines, mine, other = intersection_of(tiles.reshape(2 * ROWS, 128), token, core)
+    lines, mine, other = intersection_of(tiles.reshape(2 * ROWS, 128), token)
     half = (mine + swapped(other)).astype(jnp.bfloat16)
     half = summed_over(half, ("x", "y"))
     half = summed_over(half, "z")
-    return flat, projected_of(lines, half, core)
+    return flat, projected_of(lines, half)
 
 
 def solution(mesh):

time: 93.3 us -> 93.3 us (level)
  no operation moved by 1% of the time
where the time goes in v13:
time: 93.3 us; the launch traced here: 93 us
  waiting for transfers between devices  29.9 us (32%)
  starting transfers between devices  24.8 us (27%)
  blocking collectives  20.5 us (22%)
  Pallas kernels  15.8 us (17%)
  between operations  1.53 us (2%)
    all_to_all x1, waiting for transfers between devices, local(): tiles = lax.all_to_all(both, BAND, 0, 0, tiled=True)  28.7 us
    all_to_all x2, blocking collectives, summed_over(): tiles = lax.all_to_all(copies, axes, 0, 0, tiled=True)  20.5 us
    ppermute x3, starting transfers between devices, swapped(): return lax.ppermute(value, 'core', [(0, 1), (1, 0)])  11.9 us
    all_to_all x1, starting transfers between devices, local(): tiles = lax.all_to_all(both, BAND, 0, 0, tiled=True)  9.77 us
    pallas_call x1, Pallas kernels, unpacked(): pl.pallas_call(unpack_body, out_shape=(jax.ShapeDtypeStruct((1, G), jnp.b...  3.14 us
    ppermute x1, starting transfers between devices, from_far(): return lax.ppermute(value, BAND, pairs)  3.11 us
    pallas_call x1, Pallas kernels, exchange_of(): pl.pallas_call(exchange_body, out_shape=jax.ShapeDtypeStruct((128, 32, 12...  3.07 us
    pallas_call x1, Pallas kernels, near_term(): pl.pallas_call(near_body, out_shape=(jax.ShapeDtypeStruct((HALF * NG, 128...  2.86 us
  transfers between devices with their start and end apart: 5, of which 2 were waited for; matrix products, arithmetic and copies ran while one was open for 0% of the time, Pallas kernels for 12%

profile of v13, /device:TPU:1, one launch (start us, length us, event | category | flops | bytes accessed | tf_op | source)
XLA Modules:
  0.0 93.0 jit_solution(7185740685032233138)
XLA Ops:
  0.6 0.0 copy-start
  1.4 0.1 flag_rows.1.rows_ref
  1.5 0.4 copy-done
  1.9 0.1 pack_flagged.1.tiles_ref.own_ref
  2.0 3.1 %collective-permute-start = (bf16[2064,128]{1,0:T(8,128)(2,1)S(1)}, bf16[2064,128]{1,0:T(8,128)(2,1)S(1)}, u32[]{:S(2)}, u32[]{:S(2)}) collective-permute-start(bf16[2064,128]{1,0:T(8,128)(2,1)S(1)} %pack_flagged.1.tiles_ref.own_ref), channel_id=1, source_target_pairs={{0,127},{1,2},{2,1},{3,4},{4,3},{5,6},{6,5},{7,8},{8,7},{9,10},{10... | collective-permute-start | bytes 1585160 | tf_op jit(solution)/shard_map/ppermute | solution.py:539
  5.2 0.0 copy-start.1
  5.2 8.8 %collective-permute-start.1 = (bf16[2064,128]{1,0:T(8,128)(2,1)S(1)}, bf16[2064,128]{1,0:T(8,128)(2,1)S(1)}, u32[]{:S(2)}, u32[]{:S(2)}) collective-permute-start(bf16[2064,128]{1,0:T(8,128)(2,1)S(1)} %again.1.earlier_ref), channel_id=1, source_target_pairs={{0,1},{1,0},{2,3},{3,2},{4,5},{5,4},{6,7},{7,6},{8,9},{9,8},{10,11... | collective-permute-start | bytes 1585160 | tf_op jit(solution)/shard_map/ppermute | solution.py:543
  13.9 1.5 %screened_kernel.1.kernel_ref.earlier_ref = f32[64,64,128]{2,1,0:T(8,128)S(1)} custom-call(bf16[2064,128]{1,0:T(8,128)(2,1)S(1)} %again.1.earlier_ref), custom_call_target="tpu_custom_call" | custom-call | flops 10000000000 | bytes 2097152 | tf_op jit(solution)/shard_map/screened_kernel/pallas_call | solution.py:63
  15.4 0.0 copy-done.1
  15.5 0.0 copy-start.2
  15.5 0.0 copy-start.3
  15.5 2.6 %pack.1.both_ref = bf16[128,32,128]{2,1,0:T(8,128)(2,1)} custom-call(bf16[1,262144]{1,0:T(2,128)(2,1)S(1)} %copy-done.1, f32[64,64,128]{2,1,0:T(8,128)S(1)} %screened_kernel.1.kernel_ref.earlier_ref), custom_call_target="tpu_custom_call" | custom-call | tf_op jit(solution)/shard_map/pack/pallas_call | solution.py:147
  18.1 0.0 copy-start.4
  18.1 0.0 collective-permute-done.1.near_ref
  18.1 0.0 copy-done.2
  18.1 0.0 copy-done.3
  18.1 2.9 %near_term.1 = (bf16[2048,128]{1,0:T(8,128)(2,1)S(1)}, f32[2048,128]{1,0:T(8,128)S(1)}) custom-call(bf16[2064,128]{1,0:T(8,128)(2,1)S(1)} %pack_flagged.1.tiles_ref.own_ref, bf16[2064,128]{1,0:T(8,128)(2,1)S(1)} %collective-permute-done.1.near_ref, bf16[256,256]{1,0:T(8,128)(2,1)S(1)} %copy-done.3, bf16[256,256]{1,0:T(8,128)(2,1)S(1)} %copy-done.2, ...), custom_call_target="tpu_custom_call" | custom-call | flops 10000000000 | bytes 4194304 | tf_op jit(solution)/shard_map/near_term/pallas_call | solution.py:300
  21.0 0.0 collective-permute-done.far_ref
  21.0 0.0 copy-done.4
  21.0 3.1 %exchange.1 = bf16[128,32,128]{2,1,0:T(8,128)(2,1)} custom-call(bf16[2064,128]{1,0:T(8,128)(2,1)S(1)} %collective-permute-done.far_ref, bf16[2048,128]{1,0:T(8,128)(2,1)S(1)} %get-tuple-element.9.owner_ref, f32[2048,128]{1,0:T(8,128)S(1)} %get-tuple-element.10.term_ref, bf16[128,32,128]{2,1,0:T(8,128)(2,1)} %pack.1.both_ref, ...), custom_call_target="tpu_custom_call", output_to_operand_aliasing={{}: (3, {})} | custom-call | tf_op jit(solution)/shard_map/exchange/pallas_call | solution.py:398
  24.1 9.8 %all-to-all-start = ((bf16[128,32,128]{2,1,0:T(8,128)(2,1)}), bf16[128,32,128]{2,1,0:T(8,128)(2,1)S(1)}, u32[]{:S(2)}, u32[]{:S(2)}) async-start(bf16[128,32,128]{2,1,0:T(8,128)(2,1)} %exchange.1), calls=%async_computation | async-start | bytes 2097152 | tf_op jit(solution)/shard_map/all_to_all | solution.py:563
  33.9 3.1 %unpack.1 = (bf16[1,262144]{1,0:T(2,128)(2,1)}, bf16[16,128]{1,0:T(8,128)(2,1)S(1)}) custom-call(bf16[4096,128]{1,0:T(8,128)(2,1)} %bitcast.1.tiles_ref), custom_call_target="tpu_custom_call" | custom-call | tf_op jit(solution)/shard_map/unpack/pallas_call | solution.py:428
  37.0 28.7 %all-to-all-done = bf16[128,32,128]{2,1,0:T(8,128)(2,1)S(1)} async-done(((bf16[128,32,128]{2,1,0:T(8,128)(2,1)}), bf16[128,32,128]{2,1,0:T(8,128)(2,1)S(1)}, u32[]{:S(2)}, u32[]{:S(2)}) %all-to-all-start) | async-done | bytes 1048608 | tf_op jit(solution)/shard_map/all_to_all | solution.py:563
  65.7 0.5 intersection.1
  66.2 0.1 collective-permute-start.2
  66.3 1.2 %collective-permute-done.2 = f32[64,128]{1,0:T(8,128)S(1)} collective-permute-done((f32[64,128]{1,0:T(8,128)S(1)}, f32[64,128]{1,0:T(8,128)S(1)}, u32[]{:S(2)}, u32[]{:S(2)}) %collective-permute-start.2) | collective-permute-done | bytes 32800 | tf_op jit(solution)/shard_map/ppermute | solution.py:543
  67.6 9.9 %all_to_all.15 = bf16[8,64,128]{2,1,0:T(8,128)(2,1)S(1)} all-to-all(bf16[8,64,128]{2,1,0:T(8,128)(2,1)S(1)} %broadcast_in_dim.4), channel_id=1, replica_groups=mesh['spin'=2,'y'=4,'x'=2,'z'=8,'core'=2] {'x','y'}, dimensions={0} | all-to-all | bytes 262144 | tf_op jit(solution)/shard_map/all_to_all | solution.py:549
  77.6 10.6 %all_to_all.16 = bf16[8,64,128]{2,1,0:T(8,128)(2,1)S(1)} all-to-all(bf16[8,64,128]{2,1,0:T(8,128)(2,1)S(1)} %broadcast_in_dim.5), channel_id=1, replica_groups=mesh['spin'=2,'y'=4,'x'=2,'z'=8,'core'=2] {'z'}, dimensions={0} | all-to-all | bytes 262144 | tf_op jit(solution)/shard_map/all_to_all | solution.py:549
  88.2 3.0 %collective-permute-start.3 = (bf16[64,128]{1,0:T(8,128)(2,1)S(1)}, bf16[64,128]{1,0:T(8,128)(2,1)S(1)}, u32[]{:S(2)}, u32[]{:S(2)}) collective-permute-start(bf16[64,128]{1,0:T(8,128)(2,1)S(1)} %reduce_sum.25.mine_ref), channel_id=1, source_target_pairs={{0,1},{1,0},{2,3},{3,2},{4,5},{5,4},{6,7},{7,6},{8,9},{9,8},{10,11... | collective-permute-start | bytes 49160 | tf_op jit(solution)/shard_map/ppermute | solution.py:543
  91.2 0.9 projected_first.1.earlier_ref
  92.1 0.0 collective-permute-done.3.other_ref
  92.1 0.9 projected_second.1
  (7 shorter events, 0.1 us)
Async XLA Ops:
  0.6 1.2 %copy-start = (bf16[1,262144]{1,0:T(2,128)(2,1)S(1)}, bf16[1,262144]{1,0:T(2,128)(2,1)}, u32[]{:S(2)}) copy-start(bf16[1,262144]{1,0:T(2,128)(2,1)} %flat_ref.2) | copy-start | bytes 1572868
  2.0 19.0 %collective-permute-start = (bf16[2064,128]{1,0:T(8,128)(2,1)S(1)}, bf16[2064,128]{1,0:T(8,128)(2,1)S(1)}, u32[]{:S(2)}, u32[]{:S(2)}) collective-permute-start(bf16[2064,128]{1,0:T(8,128)(2,1)S(1)} %pack_flagged.1.tiles_ref.own_ref), channel_id=1, source_target_pairs={{0,127},{1,2},{2,1},{3,4},{4,3},{5,6},{6,5},{7,8},{8,7},{9,10},{10... | collective-permute-start | bytes 1585160 | tf_op jit(solution)/shard_map/ppermute | solution.py:539
  5.2 10.3 %copy-start.1 = (bf16[1,262144]{1,0:T(2,128)(2,1)S(1)}, bf16[1,262144]{1,0:T(2,128)(2,1)}, u32[]{:S(2)}) copy-start(bf16[1,262144]{1,0:T(2,128)(2,1)} %flat_ref.3) | copy-start | bytes 1572868
  5.2 13.0 %collective-permute-start.1 = (bf16[2064,128]{1,0:T(8,128)(2,1)S(1)}, bf16[2064,128]{1,0:T(8,128)(2,1)S(1)}, u32[]{:S(2)}, u32[]{:S(2)}) collective-permute-start(bf16[2064,128]{1,0:T(8,128)(2,1)S(1)} %again.1.earlier_ref), channel_id=1, source_target_pairs={{0,1},{1,0},{2,3},{3,2},{4,5},{5,4},{6,7},{7,6},{8,9},{9,8},{10,11... | collective-permute-start | bytes 1585160 | tf_op jit(solution)/shard_map/ppermute | solution.py:543
  15.5 2.7 %copy-start.2 = (bf16[256,256]{1,0:T(8,128)(2,1)S(1)}, bf16[256,256]{1,0:T(8,128)(2,1)}, u32[]{:S(2)}) copy-start(bf16[256,256]{1,0:T(8,128)(2,1)} %constant.11.clone.mixed_ref) | copy-start | bytes 393220
  15.5 2.7 %copy-start.3 = (bf16[256,256]{1,0:T(8,128)(2,1)S(1)}, bf16[256,256]{1,0:T(8,128)(2,1)}, u32[]{:S(2)}) copy-start(bf16[256,256]{1,0:T(8,128)(2,1)} %constant.10.clone.table_ref) | copy-start | bytes 393220
  18.1 2.9 %copy-start.4 = (bf16[256,256]{1,0:T(8,128)(2,1)S(1)}, bf16[256,256]{1,0:T(8,128)(2,1)}, u32[]{:S(2)}) copy-start(bf16[256,256]{1,0:T(8,128)(2,1)} %constant.12.clone.halves_ref) | copy-start | bytes 393220
  24.1 41.6 %all-to-all-start = ((bf16[128,32,128]{2,1,0:T(8,128)(2,1)}), bf16[128,32,128]{2,1,0:T(8,128)(2,1)S(1)}, u32[]{:S(2)}, u32[]{:S(2)}) async-start(bf16[128,32,128]{2,1,0:T(8,128)(2,1)} %exchange.1), calls=%async_computation | async-start | bytes 2097152 | tf_op jit(solution)/shard_map/all_to_all | solution.py:563
  66.2 1.3 %collective-permute-start.2 = (f32[64,128]{1,0:T(8,128)S(1)}, f32[64,128]{1,0:T(8,128)S(1)}, u32[]{:S(2)}, u32[]{:S(2)}) collective-permute-start(f32[64,128]{1,0:T(8,128)S(1)} %get-tuple-element.15), channel_id=1, source_target_pairs={{0,1},{1,0},{2,3},{3,2},{4,5},{5,4},{6,7},{7,6},{8,9},{9,8},{10,11... | collective-permute-start | bytes 98312 | tf_op jit(solution)/shard_map/ppermute | solution.py:543
  88.2 3.9 %collective-permute-start.3 = (bf16[64,128]{1,0:T(8,128)(2,1)S(1)}, bf16[64,128]{1,0:T(8,128)(2,1)S(1)}, u32[]{:S(2)}, u32[]{:S(2)}) collective-permute-start(bf16[64,128]{1,0:T(8,128)(2,1)S(1)} %reduce_sum.25.mine_ref), channel_id=1, source_target_pairs={{0,1},{1,0},{2,3},{3,2},{4,5},{5,4},{6,7},{7,6},{8,9},{9,8},{10,11... | collective-permute-start | bytes 49160 | tf_op jit(solution)/shard_map/ppermute | solution.py:543

commit v14 on v13

--- a/solution.py
+++ b/solution.py
@@ -477,17 +477,17 @@
     table = half_ref[...]
 
     def copy(part):
-        columns = pl.ds(part * 512, 512)
+        columns = pl.ds(part * 256, 256)
         rows = pl.ds(pl.multiple_of(row * 64, 64), 64)
         return pltpu.make_async_copy(result.at[:, columns], out_ref.at[rows, columns], left.at[part])
 
-    for part in range(4):
-        for line in (4 * part, 4 * part + 2):
+    for part in range(8):
+        for line in (2 * part,):
             both = [lines_ref[pl.ds(index * 128, 128), :] for index in (line, line + 1)]
             value = dot(table, jnp.concatenate(both, axis=1)) * (-1.0 / math.sqrt(128))
             result[:, pl.ds(line * 128, 256)] = value.astype(jnp.bfloat16)
         copy(part).start()
-    for part in range(4):
+    for part in range(8):
         copy(part).wait()
 
 
@@ -510,7 +510,7 @@
         out_specs=anywhere,
         scratch_shapes=[
             pltpu.VMEM((64, ROWS), jnp.bfloat16),
-            pltpu.SemaphoreType.DMA((4,)),
+            pltpu.SemaphoreType.DMA((8,)),
         ],
         compiler_params=pltpu.CompilerParams(vmem_limit_bytes=16 * 1024 * 1024),
         cost_estimate=pl.CostEstimate(

time: 93.3 us -> 93.3 us (level)
  no operation moved by 1% of the time
where the time goes in v14:
time: 93.3 us; the launch traced here: 93 us
  waiting for transfers between devices  29.9 us (32%)
  starting transfers between devices  24.8 us (27%)
  blocking collectives  20.5 us (22%)
  Pallas kernels  15.9 us (17%)
  between operations  1.53 us (2%)
    all_to_all x1, waiting for transfers between devices, local(): tiles = lax.all_to_all(both, BAND, 0, 0, tiled=True)  28.7 us
    all_to_all x2, blocking collectives, summed_over(): tiles = lax.all_to_all(copies, axes, 0, 0, tiled=True)  20.5 us
    ppermute x3, starting transfers between devices, swapped(): return lax.ppermute(value, 'core', [(0, 1), (1, 0)])  11.9 us
    all_to_all x1, starting transfers between devices, local(): tiles = lax.all_to_all(both, BAND, 0, 0, tiled=True)  9.77 us
    pallas_call x1, Pallas kernels, unpacked(): pl.pallas_call(unpack_body, out_shape=(jax.ShapeDtypeStruct((1, G), jnp.b...  3.14 us
    ppermute x1, starting transfers between devices, from_far(): return lax.ppermute(value, BAND, pairs)  3.11 us
    pallas_call x1, Pallas kernels, exchange_of(): pl.pallas_call(exchange_body, out_shape=jax.ShapeDtypeStruct((128, 32, 12...  3.07 us
    pallas_call x1, Pallas kernels, near_term(): pl.pallas_call(near_body, out_shape=(jax.ShapeDtypeStruct((HALF * NG, 128...  2.86 us
  transfers between devices with their start and end apart: 5, of which 2 were waited for; matrix products, arithmetic and copies ran while one was open for 0% of the time, Pallas kernels for 12%

profile of v14, /device:TPU:1, one launch (start us, length us, event | category | flops | bytes accessed | tf_op | source)
XLA Modules:
  0.0 93.0 jit_solution(7230683588164319888)
XLA Ops:
  0.6 0.0 copy-start
  1.4 0.1 flag_rows.1.rows_ref
  1.5 0.4 copy-done
  1.9 0.1 pack_flagged.1.tiles_ref.own_ref
  2.0 3.1 %collective-permute-start = (bf16[2064,128]{1,0:T(8,128)(2,1)S(1)}, bf16[2064,128]{1,0:T(8,128)(2,1)S(1)}, u32[]{:S(2)}, u32[]{:S(2)}) collective-permute-start(bf16[2064,128]{1,0:T(8,128)(2,1)S(1)} %pack_flagged.1.tiles_ref.own_ref), channel_id=1, source_target_pairs={{0,127},{1,2},{2,1},{3,4},{4,3},{5,6},{6,5},{7,8},{8,7},{9,10},{10... | collective-permute-start | bytes 1585160 | tf_op jit(solution)/shard_map/ppermute | solution.py:539
  5.2 0.0 copy-start.1
  5.2 8.8 %collective-permute-start.1 = (bf16[2064,128]{1,0:T(8,128)(2,1)S(1)}, bf16[2064,128]{1,0:T(8,128)(2,1)S(1)}, u32[]{:S(2)}, u32[]{:S(2)}) collective-permute-start(bf16[2064,128]{1,0:T(8,128)(2,1)S(1)} %again.1.earlier_ref), channel_id=1, source_target_pairs={{0,1},{1,0},{2,3},{3,2},{4,5},{5,4},{6,7},{7,6},{8,9},{9,8},{10,11... | collective-permute-start | bytes 1585160 | tf_op jit(solution)/shard_map/ppermute | solution.py:543
  13.9 1.5 %screened_kernel.1.kernel_ref.earlier_ref = f32[64,64,128]{2,1,0:T(8,128)S(1)} custom-call(bf16[2064,128]{1,0:T(8,128)(2,1)S(1)} %again.1.earlier_ref), custom_call_target="tpu_custom_call" | custom-call | flops 10000000000 | bytes 2097152 | tf_op jit(solution)/shard_map/screened_kernel/pallas_call | solution.py:63
  15.4 0.0 copy-done.1
  15.5 0.0 copy-start.2
  15.5 0.0 copy-start.3
  15.5 2.6 %pack.1.both_ref = bf16[128,32,128]{2,1,0:T(8,128)(2,1)} custom-call(bf16[1,262144]{1,0:T(2,128)(2,1)S(1)} %copy-done.1, f32[64,64,128]{2,1,0:T(8,128)S(1)} %screened_kernel.1.kernel_ref.earlier_ref), custom_call_target="tpu_custom_call" | custom-call | tf_op jit(solution)/shard_map/pack/pallas_call | solution.py:147
  18.1 0.0 copy-start.4
  18.1 0.0 collective-permute-done.1.near_ref
  18.1 0.0 copy-done.2
  18.1 0.0 copy-done.3
  18.1 2.9 %near_term.1 = (bf16[2048,128]{1,0:T(8,128)(2,1)S(1)}, f32[2048,128]{1,0:T(8,128)S(1)}) custom-call(bf16[2064,128]{1,0:T(8,128)(2,1)S(1)} %pack_flagged.1.tiles_ref.own_ref, bf16[2064,128]{1,0:T(8,128)(2,1)S(1)} %collective-permute-done.1.near_ref, bf16[256,256]{1,0:T(8,128)(2,1)S(1)} %copy-done.3, bf16[256,256]{1,0:T(8,128)(2,1)S(1)} %copy-done.2, ...), custom_call_target="tpu_custom_call" | custom-call | flops 10000000000 | bytes 4194304 | tf_op jit(solution)/shard_map/near_term/pallas_call | solution.py:300
  21.0 0.0 collective-permute-done.far_ref
  21.0 0.0 copy-done.4
  21.0 3.1 %exchange.1 = bf16[128,32,128]{2,1,0:T(8,128)(2,1)} custom-call(bf16[2064,128]{1,0:T(8,128)(2,1)S(1)} %collective-permute-done.far_ref, bf16[2048,128]{1,0:T(8,128)(2,1)S(1)} %get-tuple-element.9.owner_ref, f32[2048,128]{1,0:T(8,128)S(1)} %get-tuple-element.10.term_ref, bf16[128,32,128]{2,1,0:T(8,128)(2,1)} %pack.1.both_ref, ...), custom_call_target="tpu_custom_call", output_to_operand_aliasing={{}: (3, {})} | custom-call | tf_op jit(solution)/shard_map/exchange/pallas_call | solution.py:398
  24.1 9.8 %all-to-all-start = ((bf16[128,32,128]{2,1,0:T(8,128)(2,1)}), bf16[128,32,128]{2,1,0:T(8,128)(2,1)S(1)}, u32[]{:S(2)}, u32[]{:S(2)}) async-start(bf16[128,32,128]{2,1,0:T(8,128)(2,1)} %exchange.1), calls=%async_computation | async-start | bytes 2097152 | tf_op jit(solution)/shard_map/all_to_all | solution.py:563
  33.9 3.1 %unpack.1 = (bf16[1,262144]{1,0:T(2,128)(2,1)}, bf16[16,128]{1,0:T(8,128)(2,1)S(1)}) custom-call(bf16[4096,128]{1,0:T(8,128)(2,1)} %bitcast.1.tiles_ref), custom_call_target="tpu_custom_call" | custom-call | tf_op jit(solution)/shard_map/unpack/pallas_call | solution.py:428
  37.0 28.7 %all-to-all-done = bf16[128,32,128]{2,1,0:T(8,128)(2,1)S(1)} async-done(((bf16[128,32,128]{2,1,0:T(8,128)(2,1)}), bf16[128,32,128]{2,1,0:T(8,128)(2,1)S(1)}, u32[]{:S(2)}, u32[]{:S(2)}) %all-to-all-start) | async-done | bytes 1048608 | tf_op jit(solution)/shard_map/all_to_all | solution.py:563
  65.7 0.5 intersection.1
  66.2 0.1 collective-permute-start.2
  66.3 1.2 %collective-permute-done.2 = f32[64,128]{1,0:T(8,128)S(1)} collective-permute-done((f32[64,128]{1,0:T(8,128)S(1)}, f32[64,128]{1,0:T(8,128)S(1)}, u32[]{:S(2)}, u32[]{:S(2)}) %collective-permute-start.2) | collective-permute-done | bytes 32800 | tf_op jit(solution)/shard_map/ppermute | solution.py:543
  67.6 9.9 %all_to_all.15 = bf16[8,64,128]{2,1,0:T(8,128)(2,1)S(1)} all-to-all(bf16[8,64,128]{2,1,0:T(8,128)(2,1)S(1)} %broadcast_in_dim.4), channel_id=1, replica_groups=mesh['spin'=2,'y'=4,'x'=2,'z'=8,'core'=2] {'x','y'}, dimensions={0} | all-to-all | bytes 262144 | tf_op jit(solution)/shard_map/all_to_all | solution.py:549
  77.6 10.6 %all_to_all.16 = bf16[8,64,128]{2,1,0:T(8,128)(2,1)S(1)} all-to-all(bf16[8,64,128]{2,1,0:T(8,128)(2,1)S(1)} %broadcast_in_dim.5), channel_id=1, replica_groups=mesh['spin'=2,'y'=4,'x'=2,'z'=8,'core'=2] {'z'}, dimensions={0} | all-to-all | bytes 262144 | tf_op jit(solution)/shard_map/all_to_all | solution.py:549
  88.2 3.0 %collective-permute-start.3 = (bf16[64,128]{1,0:T(8,128)(2,1)S(1)}, bf16[64,128]{1,0:T(8,128)(2,1)S(1)}, u32[]{:S(2)}, u32[]{:S(2)}) collective-permute-start(bf16[64,128]{1,0:T(8,128)(2,1)S(1)} %reduce_sum.25.mine_ref), channel_id=1, source_target_pairs={{0,1},{1,0},{2,3},{3,2},{4,5},{5,4},{6,7},{7,6},{8,9},{9,8},{10,11... | collective-permute-start | bytes 49160 | tf_op jit(solution)/shard_map/ppermute | solution.py:543
  91.2 0.9 projected_first.1.earlier_ref
  92.1 0.0 collective-permute-done.3.other_ref
  92.1 0.9 projected_second.1
  (7 shorter events, 0.1 us)
Async XLA Ops:
  0.6 1.2 %copy-start = (bf16[1,262144]{1,0:T(2,128)(2,1)S(1)}, bf16[1,262144]{1,0:T(2,128)(2,1)}, u32[]{:S(2)}) copy-start(bf16[1,262144]{1,0:T(2,128)(2,1)} %flat_ref.2) | copy-start | bytes 1572868
  2.0 19.0 %collective-permute-start = (bf16[2064,128]{1,0:T(8,128)(2,1)S(1)}, bf16[2064,128]{1,0:T(8,128)(2,1)S(1)}, u32[]{:S(2)}, u32[]{:S(2)}) collective-permute-start(bf16[2064,128]{1,0:T(8,128)(2,1)S(1)} %pack_flagged.1.tiles_ref.own_ref), channel_id=1, source_target_pairs={{0,127},{1,2},{2,1},{3,4},{4,3},{5,6},{6,5},{7,8},{8,7},{9,10},{10... | collective-permute-start | bytes 1585160 | tf_op jit(solution)/shard_map/ppermute | solution.py:539
  5.2 10.3 %copy-start.1 = (bf16[1,262144]{1,0:T(2,128)(2,1)S(1)}, bf16[1,262144]{1,0:T(2,128)(2,1)}, u32[]{:S(2)}) copy-start(bf16[1,262144]{1,0:T(2,128)(2,1)} %flat_ref.3) | copy-start | bytes 1572868
  5.2 13.0 %collective-permute-start.1 = (bf16[2064,128]{1,0:T(8,128)(2,1)S(1)}, bf16[2064,128]{1,0:T(8,128)(2,1)S(1)}, u32[]{:S(2)}, u32[]{:S(2)}) collective-permute-start(bf16[2064,128]{1,0:T(8,128)(2,1)S(1)} %again.1.earlier_ref), channel_id=1, source_target_pairs={{0,1},{1,0},{2,3},{3,2},{4,5},{5,4},{6,7},{7,6},{8,9},{9,8},{10,11... | collective-permute-start | bytes 1585160 | tf_op jit(solution)/shard_map/ppermute | solution.py:543
  15.5 2.7 %copy-start.2 = (bf16[256,256]{1,0:T(8,128)(2,1)S(1)}, bf16[256,256]{1,0:T(8,128)(2,1)}, u32[]{:S(2)}) copy-start(bf16[256,256]{1,0:T(8,128)(2,1)} %constant.11.clone.mixed_ref) | copy-start | bytes 393220
  15.5 2.7 %copy-start.3 = (bf16[256,256]{1,0:T(8,128)(2,1)S(1)}, bf16[256,256]{1,0:T(8,128)(2,1)}, u32[]{:S(2)}) copy-start(bf16[256,256]{1,0:T(8,128)(2,1)} %constant.10.clone.table_ref) | copy-start | bytes 393220
  18.1 2.9 %copy-start.4 = (bf16[256,256]{1,0:T(8,128)(2,1)S(1)}, bf16[256,256]{1,0:T(8,128)(2,1)}, u32[]{:S(2)}) copy-start(bf16[256,256]{1,0:T(8,128)(2,1)} %constant.12.clone.halves_ref) | copy-start | bytes 393220
  24.1 41.6 %all-to-all-start = ((bf16[128,32,128]{2,1,0:T(8,128)(2,1)}), bf16[128,32,128]{2,1,0:T(8,128)(2,1)S(1)}, u32[]{:S(2)}, u32[]{:S(2)}) async-start(bf16[128,32,128]{2,1,0:T(8,128)(2,1)} %exchange.1), calls=%async_computation | async-start | bytes 2097152 | tf_op jit(solution)/shard_map/all_to_all | solution.py:563
  66.2 1.3 %collective-permute-start.2 = (f32[64,128]{1,0:T(8,128)S(1)}, f32[64,128]{1,0:T(8,128)S(1)}, u32[]{:S(2)}, u32[]{:S(2)}) collective-permute-start(f32[64,128]{1,0:T(8,128)S(1)} %get-tuple-element.15), channel_id=1, source_target_pairs={{0,1},{1,0},{2,3},{3,2},{4,5},{5,4},{6,7},{7,6},{8,9},{9,8},{10,11... | collective-permute-start | bytes 98312 | tf_op jit(solution)/shard_map/ppermute | solution.py:543
  88.2 3.9 %collective-permute-start.3 = (bf16[64,128]{1,0:T(8,128)(2,1)S(1)}, bf16[64,128]{1,0:T(8,128)(2,1)S(1)}, u32[]{:S(2)}, u32[]{:S(2)}) collective-permute-start(bf16[64,128]{1,0:T(8,128)(2,1)S(1)} %reduce_sum.25.mine_ref), channel_id=1, source_target_pairs={{0,1},{1,0},{2,3},{3,2},{4,5},{5,4},{6,7},{7,6},{8,9},{9,8},{10,11... | collective-permute-start | bytes 49160 | tf_op jit(solution)/shard_map/ppermute | solution.py:543
